TPU v7x, 32 devices: a whole 2x2x4 slice. The times are simulated.
32 devices in a mesh: shift: 2 (over y), node: 4 (over z), rhs: 4 (over x, core).
Axes of the slice: x: 2, y: 2, z: 4, core: 2. Of those that a mesh axis runs over, the one named last changes fastest.
Arguments:
- loads: bfloat16 [8192, 4096], P('node', ('shift', 'rhs')), parts along dimension 1, may hold values from -6 to 6
- root_loads: bfloat16 [1024, 4096], P(None, ('shift', 'rhs')), parts along dimension 1, may hold values from -6 to 6
- send_rows: int32 [8192], P('node'), may hold values from 0 to 2047, as said below
- leaf_inv: bfloat16 [16, 512, 512], P('node'), as said below
- couple: bfloat16 [16, 512, 512], P('node'), may hold values from -0.09375 to 0.09375
- couple_rows: int32 [16, 512], P('node'), may hold values from 0 to 1023, as said below
- root_inv: bfloat16 [1024, 1024], P('node'), as said below
Outputs:
- leaf_solution: bfloat16 [8192, 4096], P('node', ('shift', 'rhs')), parts along dimension 1
- root_solution: bfloat16 [1024, 4096], P(None, ('shift', 'rhs')), parts along dimension 1
There are 2 independent parts, one for each index of `shift`. A program takes and returns all parts, laid end to end along the dimension named above; an argument that names none is the same for every part. Nothing has to cross between parts.
Inputs may be any that keep to these rules, and one draw needn't show every extreme that they name: `send_rows`: each device's 4 * 512 entries form a permutation. `couple_rows`: the 512 entries of one leaf are distinct. `leaf_inv`: each block is lower triangular with a positive diagonal. `root_inv`: lower triangular with a positive diagonal.
All inputs are finite; a program needn't handle non-finite values.
Results may differ from a plain program's by a relative error of at most 0.0061.
Values may be sent and summed in bfloat16 or wider, within the bound.
No kernel may reach another device: no remote copies, remote signals or barrier semaphores. Data moves between devices by JAX's collectives and lax.ppermute only.
A program may use at most 64 MiB of HBM per device.

v0:
```python
import jax
import jax.numpy as jnp
from jax import lax
from jax.sharding import PartitionSpec as P


def per_device(loads, root_loads, send_rows, leaf_inv, couple, couple_rows, root_inv):
    leaves = leaf_inv.shape[0]
    order = leaf_inv.shape[1]
    columns = loads.shape[1]
    root_order = root_loads.shape[0]
    picked = loads[send_rows]
    arrived = lax.all_to_all(picked, "node", split_axis=0, concat_axis=0, tiled=True)
    blocks = arrived.reshape(leaves, order, columns)
    fwd = jnp.einsum("nij,njc->nic", leaf_inv, blocks, preferred_element_type=jnp.float32).astype(
        jnp.bfloat16
    )
    terms = jnp.einsum("nrj,njc->nrc", couple, fwd, preferred_element_type=jnp.float32)
    local_update = (
        jnp.zeros((root_order, columns), jnp.float32)
        .at[couple_rows.reshape(-1)]
        .add(terms.reshape(-1, columns))
    )
    update = lax.psum(local_update, "node")
    reduced = (root_loads.astype(jnp.float32) - update).astype(jnp.bfloat16)
    transposed = (((0,), (0,)), ((), ()))
    root_fwd = jnp.dot(root_inv, reduced, preferred_element_type=jnp.float32).astype(jnp.bfloat16)
    partial_back = lax.dot_general(
        root_inv, root_fwd, transposed, preferred_element_type=jnp.float32
    )
    root_solution = lax.psum(partial_back, "node").astype(jnp.bfloat16)
    root_picked = root_solution[couple_rows.reshape(-1)].reshape(leaves, couple.shape[1], columns)
    backsub = jnp.einsum("nrj,nrc->njc", couple, root_picked, preferred_element_type=jnp.float32)
    corrected = (fwd.astype(jnp.float32) - backsub).astype(jnp.bfloat16)
    leaf_solution = jnp.einsum(
        "nji,njc->nic", leaf_inv, corrected, preferred_element_type=jnp.float32
    ).astype(jnp.bfloat16)
    return (leaf_solution.reshape(leaves * order, columns), root_solution)


def solution(mesh):
    return jax.shard_map(
        per_device,
        mesh=mesh,
        in_specs=(
            P("node", ("shift", "rhs")),
            P(None, ("shift", "rhs")),
            P("node"),
            P("node", None, None),
            P("node", None, None),
            P("node", None),
            P("node", None),
        ),
        out_specs=(P("node", ("shift", "rhs")), P(None, ("shift", "rhs"))),
        check_vma=False,
    )
```

profile of v0, /device:TPU:0, one launch (start us, length us, event | category | flops | bytes accessed | tf_op | source)
XLA Modules:
  0.0 289.8 jit_solution(9873849155275104142)
XLA Ops:
  7.2 0.0 copy-start
  7.2 0.9 fusion.2
  8.0 11.1 %gather_fusion = bf16[2048,512]{1,0:T(8,128)(2,1)} fusion(bf16[2048,512]{1,0:T(8,128)(2,1)} %param.7, s32[2048]{0:T(1024)S(1)} %fusion.2), kind=kCustom, calls=%fused_computation | custom fusion | bytes 4202496 | tf_op jit(solution)/shard_map/gather | solution.py:12
  19.1 4.1 %copy.12 = bf16[4,512,512]{1,2,0:T(8,128)(2,1)} copy(bf16[4,512,512]{2,1,0:T(8,128)(2,1)} %bitcast.24) | data formatting | bytes 4194304 | tf_op jit(solution)/shard_map/all_to_all | solution.py:13
  23.3 0.0 copy-start.5
  23.3 6.4 %all-to-all-start = ((bf16[4,512,512]{1,2,0:T(8,128)(2,1)}), bf16[4,512,512]{1,2,0:T(8,128)(2,1)}, u32[]{:S(2)}, u32[]{:S(2)}) async-start(bf16[4,512,512]{1,2,0:T(8,128)(2,1)} %copy.12), calls=%async_computation | async-start | bytes 4194304 | tf_op jit(solution)/shard_map/all_to_all | solution.py:13
  29.7 0.0 all-reduce.3.cloned.1.call-start
  29.7 0.0 copy-done.5
  29.8 48.3 %all-to-all-done = bf16[4,512,512]{1,2,0:T(8,128)(2,1)} async-done(((bf16[4,512,512]{1,2,0:T(8,128)(2,1)}), bf16[4,512,512]{1,2,0:T(8,128)(2,1)}, u32[]{:S(2)}, u32[]{:S(2)}) %all-to-all-start) | async-done | bytes 2097184 | tf_op jit(solution)/shard_map/all_to_all | solution.py:13
  78.0 0.0 copy-done
  78.0 0.0 copy-start.2
  78.0 3.0 %convolution_convert_fusion.1 = bf16[4,512,512]{2,1,0:T(8,128)(2,1)S(1)} fusion(bf16[4,512,512]{1,2,0:T(8,128)(2,1)} %all-to-all-done, bf16[4,512,512]{2,1,0:T(8,128)(2,1)S(1)} %copy-done), kind=kOutput, calls=%fused_computation.6 | convolution fusion | flops 1074790400 | bytes 6291456 | tf_op jit(solution)/shard_map/nij,njc->nic/dot_general | solution.py:15
  81.1 0.0 copy-done.2
  81.1 0.0 copy-start.3
  81.1 3.2 %fusion.3 = f32[4,512,512]{1,2,0:T(8,128)} fusion(bf16[4,512,512]{2,1,0:T(8,128)(2,1)S(1)} %convolution_convert_fusion.1, bf16[4,512,512]{2,1,0:T(8,128)(2,1)S(1)} %copy-done.2), kind=kOutput, calls=%fused_computation.15 | convolution fusion | flops 1073741824 | bytes 8388608 | tf_op jit(solution)/shard_map/nrj,njc->nrc/dot_general | solution.py:18
  84.3 0.0 copy-done.3
  84.3 0.0 copy-start.4
  84.3 14.7 %scatter_custom_fusion = f32[1024,512]{1,0:T(8,128)} fusion(s32[2048]{0:T(1024)S(1)} %bitcast.27, f32[2048,512]{1,0:T(8,128)} %bitcast.25, f32[]{:T(128)} %constant.2.clone.1), kind=kCustom, calls=%fused_computation.9 | custom fusion | flops 1048576 | bytes 2097664 | tf_op jit(solution)/shard_map/scatter-add | solution.py:22
  99.0 0.0 all-reduce.3.cloned.1.call-update
  99.0 85.8 %all-reduce.3.cloned.1.call-done = f32[1024,512]{1,0:T(8,128)} async-done(((f32[1024,512]{1,0:T(8,128)}), f32[1024,512]{1,0:T(8,128)}) %all-reduce.3.cloned.1.call-update) | async-done | bytes 2097168 | tf_op jit(solution)/shard_map/psum | solution.py:24
  184.8 0.0 copy-done.4
  184.8 4.4 %convolution_bitcast_fusion = f32[1024,512]{0,1:T(8,128)} fusion(bf16[256,1024]{1,0:T(8,128)(2,1)S(1)} %copy-done.4, f32[1024,512]{1,0:T(8,128)} %all-reduce.3.cloned.1.call-done, bf16[1024,512]{1,0:T(8,128)(2,1)} %param.8), kind=kOutput, calls=%fused_computation.7 | convolution fusion | flops 538574848 | bytes 5767168 | tf_op jit(solution)/shard_map/dot_general | solution.py:28
  189.2 76.3 %all-reduce.4 = bf16[1024,512]{0,1:T(8,128)(2,1)} all-reduce(f32[1024,512]{0,1:T(8,128)} %convolution_bitcast_fusion), channel_id=1, replica_groups=mesh['shift'=2,'node'=4,'rhs'=4] {'node'}, use_global_device_ids=true, to_apply=%region_2.0 | all-reduce | flops 524288 | bytes 3145728 | tf_op jit(solution)/shard_map/psum | solution.py:31
  265.5 1.5 copy.13
  267.0 0.0 copy-start.1
  267.0 9.2 %gather_fusion.1 = bf16[2048,512]{1,0:T(8,128)(2,1)} fusion(bf16[1024,512]{1,0:T(8,128)(2,1)S(1)} %copy.13, s32[2048]{0:T(1024)S(1)} %broadcast_clamp_fusion), kind=kCustom, calls=%fused_computation.1 | custom fusion | bytes 4202496 | tf_op jit(solution)/shard_map/gather | solution.py:32
  276.2 0.0 copy-done.1
  276.2 6.7 %convolution_convert_fusion = bf16[4,512,512]{1,2,0:T(8,128)(2,1)} fusion(bf16[4,512,512]{2,1,0:T(8,128)(2,1)S(1)} %copy-done, bf16[4,512,512]{2,1,0:T(8,128)(2,1)} %copy-done.3, bf16[4,512,512]{2,1,0:T(8,128)(2,1)} %bitcast.26, bf16[4,512,512]{2,1,0:T(8,128)(2,1)} %param.11), kind=kOutput, calls=%fused_computation.5 | convolution fusion | flops 2151677952 | bytes 10485760 | tf_op jit(solution)/shard_map/nji,njc->nic/dot_general | solution.py:35
  (3 shorter events, 0.0 us)
Async XLA Ops:
  7.2 70.9 %copy-start = (bf16[4,512,512]{2,1,0:T(8,128)(2,1)S(1)}, bf16[4,512,512]{2,1,0:T(8,128)(2,1)}, u32[]{:S(2)}) copy-start(bf16[4,512,512]{2,1,0:T(8,128)(2,1)} %param.10) | copy-start | bytes 6291460
  23.3 6.5 %copy-start.5 = (s32[4,512]{1,0:T(4,128)S(1)}, s32[4,512]{1,0:T(4,128)}, u32[]{:S(2)}) copy-start(s32[4,512]{1,0:T(4,128)} %param.12) | copy-start | bytes 24580
  23.3 54.8 %all-to-all-start = ((bf16[4,512,512]{1,2,0:T(8,128)(2,1)}), bf16[4,512,512]{1,2,0:T(8,128)(2,1)}, u32[]{:S(2)}, u32[]{:S(2)}) async-start(bf16[4,512,512]{1,2,0:T(8,128)(2,1)} %copy.12), calls=%async_computation | async-start | bytes 4194304 | tf_op jit(solution)/shard_map/all_to_all | solution.py:13
  29.7 155.1 %all-reduce.3.cloned.1.call-start = ((), (), s32[]{:S(2)}) async-start(), calls=%async_computation.1 | async-start | bytes 4194304 | tf_op jit(solution)/shard_map/psum | solution.py:24
  78.0 3.0 %copy-start.2 = (bf16[4,512,512]{2,1,0:T(8,128)(2,1)S(1)}, bf16[4,512,512]{2,1,0:T(8,128)(2,1)}, u32[]{:S(2)}) copy-start(bf16[4,512,512]{2,1,0:T(8,128)(2,1)} %param.11) | copy-start | bytes 6291460
  81.1 3.2 %copy-start.3 = (bf16[4,512,512]{2,1,0:T(8,128)(2,1)}, bf16[4,512,512]{2,1,0:T(8,128)(2,1)S(1)}, u32[]{:S(2)}) copy-start(bf16[4,512,512]{2,1,0:T(8,128)(2,1)S(1)} %convolution_convert_fusion.1) | copy-start | bytes 6291460
  84.3 100.5 %copy-start.4 = (bf16[256,1024]{1,0:T(8,128)(2,1)S(1)}, bf16[256,1024]{1,0:T(8,128)(2,1)}, u32[]{:S(2)}) copy-start(bf16[256,1024]{1,0:T(8,128)(2,1)} %param.13) | copy-start | bytes 1572868
  267.0 9.2 %copy-start.1 = (bf16[1024,512]{1,0:T(8,128)(2,1)}, bf16[1024,512]{1,0:T(8,128)(2,1)S(1)}, u32[]{:S(2)}) copy-start(bf16[1024,512]{1,0:T(8,128)(2,1)S(1)} %copy.13) | copy-start | bytes 3145732
Sparse Core Ops, SparseCore 0:
  99.1 85.6 all-reduce.2
where the time goes:
time: 290 us
  waiting for transfers between devices  134 us (46%)
  blocking collectives  76.3 us (26%)
  local copies, waits for them, and re-layouts  26 us (9%)
  matrix products  17.4 us (6%)
  other arithmetic  15.5 us (5%)
  between operations  14.1 us (5%)
  starting transfers between devices  6.45 us (2%)
    psum x1, waiting for transfers between devices, per_device(): update = lax.psum(local_update, 'node')  85.8 us
    psum x1, blocking collectives, per_device(): root_solution = lax.psum(partial_back, 'node').astype(jnp.bfloat16)  76.3 us
    all_to_all x1, waiting for transfers between devices, per_device(): lax.all_to_all(picked, 'node', split_axis=0, concat_axis=0, tiled=True)  48.3 us
    scatter-add x1, other arithmetic, per_device(): local_update = jnp.zeros((root_order, columns), jnp.float32).at[couple_ro...  14.7 us
    gather x1, local copies, waits for them, and re-layouts, per_device(): picked = loads[send_rows]  11.1 us
    gather x1, local copies, waits for them, and re-layouts, per_device(): root_solution[couple_rows.reshape(-1)]  9.17 us
    dot_general x1, matrix products, per_device(): jnp.einsum('nji,njc->nic', leaf_inv, corrected, preferred_element_type=jn...  6.72 us
    all_to_all x1, starting transfers between devices, per_device(): lax.all_to_all(picked, 'node', split_axis=0, concat_axis=0, tiled=True)  6.45 us
  transfers between devices with their start and end apart: 2, of which 2 were waited for; matrix products, arithmetic and copies ran while one was open for 0% of the time, Pallas kernels for 0%

commit v1 on v0

v1 whole, which is shorter than its diff:
```python
import functools

import jax
import jax.numpy as jnp
from jax import lax
from jax.experimental import pallas as pl
from jax.experimental.pallas import tpu as pltpu
from jax.sharding import PartitionSpec as P

BF = jnp.bfloat16
F32 = jnp.float32
LANES = 128
VMEM_LIMIT = 24 * 1024 * 1024
NT = (((1,), (1,)), ((), ()))


def dot(a, b):
    return jnp.dot(a, b, preferred_element_type=F32)


def dot_nt(a, b):
    return lax.dot_general(a, b, NT, preferred_element_type=F32)


def any_spec():
    return pl.BlockSpec(memory_space=pl.ANY)


def vmem_spec():
    return pl.BlockSpec(memory_space=pltpu.VMEM)


def smem_spec():
    return pl.BlockSpec(memory_space=pltpu.SMEM)


def params():
    return pltpu.CompilerParams(vmem_limit_bytes=VMEM_LIMIT)


def cost(flops, moved):
    return pl.CostEstimate(flops=int(flops), bytes_accessed=int(moved), transcendentals=0)


def leader(level, group):
    if level == 0:
        return group
    return leader(level - 1, 2 * group + (1 if group % 2 == 0 else 0))


def tree(nodes):
    depth = nodes.bit_length() - 1
    ups = []
    for level in range(1, depth):
        pairs = []
        for group in range(nodes >> level):
            left, right = leader(level - 1, 2 * group), leader(level - 1, 2 * group + 1)
            pairs.append((left, right) if group % 2 == 0 else (right, left))
        ups.append(pairs)
    left, right = leader(depth - 1, 0), leader(depth - 1, 1)
    return ups, [(left, right), (right, left)]


def pick_kernel(nodes, first, count, me_ref, rows_ref, loads_ref, *rest):
    outs, held = rest[:-1], rest[-1]
    total = loads_ref.shape[0]
    block = total // nodes
    me = me_ref[0]
    tile = 128
    x = loads_ref[:, first * LANES : (first + count) * LANES]
    for k in range(total // tile):
        row = rows_ref[k : k + 1, :]
        column = jnp.broadcast_to(row, (tile, tile)).T
        parts = []
        for j in range(total // tile):
            wanted = lax.broadcasted_iota(jnp.int32, (tile, tile), 1) + j * tile
            parts.append(jnp.where(column == wanted, 1.0, 0.0).astype(BF))
        onehot = jnp.concatenate(parts, axis=1)
        held[k * tile : (k + 1) * tile, :] = dot(onehot, x).astype(BF)
    for c in range(count):
        for s in range(nodes):
            start = pl.multiple_of((me ^ s) * block, block)
            outs[c * nodes + s][...] = held[pl.ds(start, block), c * LANES : (c + 1) * LANES]


def pick(nodes, first, count, me, rows, loads):
    total = loads.shape[0]
    block = total // nodes
    width = count * LANES
    return pl.pallas_call(
        functools.partial(pick_kernel, nodes, first, count),
        in_specs=[smem_spec(), vmem_spec(), vmem_spec()],
        out_specs=[vmem_spec()] * (count * nodes),
        out_shape=[jax.ShapeDtypeStruct((block, LANES), BF)] * (count * nodes),
        scratch_shapes=[pltpu.VMEM((total, width), BF)],
        compiler_params=params(),
        cost_estimate=cost(2 * total * total * width, 4 * total * width),
        name="pick",
    )(me, rows, loads)


def identity(size):
    same = lax.broadcasted_iota(jnp.int32, (size, size), 0) == lax.broadcasted_iota(jnp.int32, (size, size), 1)
    return jnp.where(same, 1.0, 0.0).astype(BF)


def prep_kernel(rows_ref, couple_ref, inv_ref, spread_ref, spread_t_ref, inv_t_ref):
    leaves, picked, order = couple_ref.shape
    root = spread_ref.shape[0]
    eye = identity(picked)
    for n in range(leaves):
        c = couple_ref[n]
        at = slice(n * order, (n + 1) * order)
        rows = rows_ref[n : n + 1, :]
        onehot = lax.broadcasted_iota(jnp.int32, (root, picked), 0) == jnp.broadcast_to(rows, (root, picked))
        onehot = jnp.where(onehot, 1.0, 0.0).astype(BF)
        spread_ref[:, at] = dot(onehot, c).astype(BF)
        c_t = dot_nt(eye, c).astype(BF)
        spread_t_ref[at, :] = dot_nt(c_t, onehot).astype(BF)
        inv_t_ref[n] = dot_nt(identity(order), inv_ref[n]).astype(BF)


def prep(rows, couple, inv, root):
    leaves, picked, order = couple.shape
    return pl.pallas_call(
        prep_kernel,
        in_specs=[vmem_spec()] * 3,
        out_specs=[vmem_spec()] * 3,
        out_shape=[
            jax.ShapeDtypeStruct((root, leaves * order), BF),
            jax.ShapeDtypeStruct((leaves * order, root), BF),
            jax.ShapeDtypeStruct((leaves, order, order), BF),
        ],
        compiler_params=params(),
        cost_estimate=cost(2 * leaves * picked * order * (2 * root + 2 * order), leaves * order * (4 * root + 6 * order)),
        name="prep",
    )(rows, couple, inv)


def forward_kernel(nodes, me_ref, inv_ref, spread_ref, *rest):
    blocks, (fwd_ref, part_ref, wide_ref, held) = rest[:nodes], rest[nodes:]
    block = blocks[0].shape[0]
    leaves, order, _ = inv_ref.shape
    half = order // 2
    me = me_ref[0]
    for s in range(nodes):
        held[pl.ds(pl.multiple_of((me ^ s) * block, block), block), :] = blocks[s][...]
    for n in range(leaves):
        at = n * order
        x = held[at : at + order, :]
        fwd_ref[at : at + half, :] = dot(inv_ref[n, :half, :half], x[:half]).astype(BF)
        fwd_ref[at + half : at + order, :] = dot(inv_ref[n, half:, :], x).astype(BF)
    part = dot(spread_ref[...], fwd_ref[...])
    wide_ref[...] = part
    part_ref[...] = part.astype(BF)


def forward(nodes, me, inv, spread, blocks):
    leaves, order, _ = inv.shape
    root = spread.shape[0]
    return pl.pallas_call(
        functools.partial(forward_kernel, nodes),
        in_specs=[smem_spec()] + [vmem_spec()] * (2 + nodes),
        out_specs=[vmem_spec()] * 3,
        out_shape=[
            jax.ShapeDtypeStruct((leaves * order, LANES), BF),
            jax.ShapeDtypeStruct((root, LANES), BF),
            jax.ShapeDtypeStruct((root, LANES), F32),
        ],
        scratch_shapes=[pltpu.VMEM((leaves * order, LANES), BF)],
        compiler_params=params(),
        cost_estimate=cost(
            2 * leaves * order * LANES * (order + root),
            2 * leaves * order * (order + root + 3 * LANES) + 2 * root * LANES,
        ),
        name="forward",
    )(me, inv, spread, *blocks)


def root_prep_kernel(count, *rest):
    pieces, (whole_ref, whole_t_ref) = rest[:count], rest[count:]
    width = pieces[0].shape[1]
    for q in range(count):
        piece = pieces[q][...]
        whole_ref[:, q * width : (q + 1) * width] = piece
        whole_t_ref[q * width : (q + 1) * width, :] = dot_nt(identity(width), piece).astype(BF)


def root_prep(pieces):
    count = len(pieces)
    root, width = pieces[0].shape
    return pl.pallas_call(
        functools.partial(root_prep_kernel, count),
        in_specs=[vmem_spec()] * count,
        out_specs=[vmem_spec()] * 2,
        out_shape=[
            jax.ShapeDtypeStruct((root, count * width), BF),
            jax.ShapeDtypeStruct((count * width, root), BF),
        ],
        compiler_params=params(),
        cost_estimate=cost(2 * root * root * width, 6 * root * root),
        name="root_prep",
    )(*pieces)


def root_kernel(chunk, count, order_ref, whole_ref, whole_t_ref, loads_ref, one_ref, two_ref, out_ref, held, solved):
    root = whole_ref.shape[1]
    width = root // count
    update = one_ref[...].astype(F32) + two_ref[...].astype(F32)
    held[...] = (loads_ref[:, chunk * LANES : (chunk + 1) * LANES].astype(F32) - update).astype(BF)
    blocks = [held[pl.ds(pl.multiple_of(order_ref[q] * width, width), width), :] for q in range(count)]
    reduced = jnp.concatenate(blocks, axis=0)
    root_fwd = dot(whole_ref[...], reduced).astype(BF)
    solved[...] = dot(whole_t_ref[...], root_fwd).astype(BF)
    for q in range(count):
        start = pl.multiple_of(order_ref[q] * width, width)
        out_ref[pl.ds(start, width), :] = solved[q * width : (q + 1) * width, :]


def root_solve(chunk, order, whole, whole_t, root_loads, one, two):
    count = order.shape[0]
    root = whole.shape[1]
    return pl.pallas_call(
        functools.partial(root_kernel, chunk, count),
        in_specs=[smem_spec()] + [vmem_spec()] * 5,
        out_specs=vmem_spec(),
        out_shape=jax.ShapeDtypeStruct((root, LANES), BF),
        scratch_shapes=[pltpu.VMEM((root, LANES), BF), pltpu.VMEM((root, LANES), BF)],
        compiler_params=params(),
        cost_estimate=cost(4 * root * root * LANES, 4 * root * root + 8 * root * LANES),
        name="root_solve",
    )(order, whole, whole_t, root_loads, one, two)


def backward_kernel(chunk, take_ref, own_ref, got_ref, fwd_ref, spread_t_ref, inv_t_ref, *rest):
    out_ref, root_ref, held, solved, sems = rest[-5:]
    leaves, order, _ = inv_t_ref.shape
    half = order // 2
    columns = pl.ds(chunk * LANES, LANES)
    held[...] = jnp.where(take_ref[0] > 0, got_ref[...], own_ref[...])
    copies = [pltpu.make_async_copy(held, root_ref.at[:, columns], sems.at[leaves])]
    copies[0].start()
    back = dot(spread_t_ref[...], held[...])
    corrected = (fwd_ref[...].astype(F32) - back).astype(BF)
    for n in range(leaves):
        at = n * order
        x = corrected[at : at + order]
        solved[at : at + half, :] = dot(inv_t_ref[n, :half, :], x).astype(BF)
        solved[at + half : at + order, :] = dot(inv_t_ref[n, half:, half:], x[half:]).astype(BF)
        rows = pl.ds(at, order)
        copy = pltpu.make_async_copy(solved.at[rows], out_ref.at[rows, columns], sems.at[n])
        copy.start()
        copies.append(copy)
    for copy in copies:
        copy.wait()


def backward(chunk, width, take, own, got, fwd, spread_t, inv_t, before):
    leaves, order, _ = inv_t.shape
    root = spread_t.shape[1]
    inputs = [take, own, got, fwd, spread_t, inv_t]
    aliases, extra = {}, []
    if before is not None:
        aliases = {len(inputs): 0, len(inputs) + 1: 1}
        extra = list(before)
    return pl.pallas_call(
        functools.partial(backward_kernel, chunk),
        in_specs=[smem_spec()] + [vmem_spec()] * 5 + [any_spec()] * len(extra),
        out_specs=[any_spec()] * 2,
        out_shape=[
            jax.ShapeDtypeStruct((leaves * order, width), BF),
            jax.ShapeDtypeStruct((root, width), BF),
        ],
        scratch_shapes=[
            pltpu.VMEM((root, LANES), BF),
            pltpu.VMEM((leaves * order, LANES), BF),
            pltpu.SemaphoreType.DMA((leaves + 1,)),
        ],
        input_output_aliases=aliases,
        compiler_params=params(),
        cost_estimate=cost(
            2 * leaves * order * LANES * (order + root),
            2 * leaves * order * (order + root + 2 * LANES) + 6 * root * LANES,
        ),
        name="backward",
    )(*inputs, *extra)


def per_device(sizes, loads, root_loads, send_rows, leaf_inv, couple, couple_rows, root_inv):
    nodes = sizes["node"]
    root, width = root_loads.shape
    total = loads.shape[0]
    chunks = width // LANES
    ups, top = tree(nodes)
    node = lax.axis_index("node")
    me = node.astype(jnp.int32).reshape(1)
    rows = send_rows.reshape(total // 128, 128)

    stages, count = [], 1
    for axis in ("rhs", "shift"):
        if count * sizes[axis] * LANES <= root:
            bits = sizes[axis].bit_length() - 1
            stages = [(axis, bit) for bit in range(bits)] + stages if axis == "rhs" else stages + [(axis, bit) for bit in range(bits)]
            count *= sizes[axis]
    mine = jnp.int32(0)
    for place, (axis, bit) in enumerate(stages):
        mine = mine + (((lax.axis_index(axis).astype(jnp.int32) >> bit) & 1) << place)
    piece = lax.dynamic_slice_in_dim(root_inv, mine * (root // count), root // count, axis=1)
    for pairs in ups:
        piece = jnp.concatenate([piece, lax.ppermute(piece, "node", pairs)], axis=0)
    other = lax.ppermute(piece, "node", top)
    is_left = node == top[0][0]
    piece = jnp.concatenate([jnp.where(is_left, piece, other), jnp.where(is_left, other, piece)], axis=0)
    held = [(0, piece)]
    for place in reversed(range(len(stages))):
        axis, bit = stages[place]
        pairs = [(i, i ^ (1 << bit)) for i in range(sizes[axis])]
        held = held + [(q | (1 << place), lax.ppermute(x, axis, pairs)) for q, x in held]
    held.sort(key=lambda pair: pair[0])
    order = jnp.arange(count, dtype=jnp.int32) ^ mine

    sends = pick(nodes, 0, 1, me, rows, loads)
    if chunks > 1:
        sends = list(sends) + list(pick(nodes, 1, chunks - 1, me, rows, loads))
    spread, spread_t, inv_t = prep(couple_rows, couple, leaf_inv, root)
    whole, whole_t = root_prep([x for _, x in held])

    result = None
    for c in range(chunks):
        mine_blocks = sends[c * nodes : (c + 1) * nodes]
        blocks = [mine_blocks[0]]
        for s in range(1, nodes):
            blocks.append(lax.ppermute(mine_blocks[s], "node", [(i, i ^ s) for i in range(nodes)]))
        fwd, part, wide = forward(nodes, me, leaf_inv, spread, blocks)
        for pairs in ups:
            wide = wide + lax.ppermute(part, "node", pairs).astype(F32)
            part = wide.astype(BF)
        other = lax.ppermute(part, "node", top)
        own = root_solve(c, order, whole, whole_t, root_loads, part, other)
        got = own
        take = jnp.zeros((1,), jnp.int32)
        for level, pairs in enumerate(reversed(ups)):
            if level > 0:
                own = jnp.where(take[0] > 0, got, own)
            got = lax.ppermute(own, "node", [(b, a) for a, b in pairs])
            take = jnp.zeros((), jnp.int32)
            for sender, _ in pairs:
                take = take + (node == sender).astype(jnp.int32)
            take = take.reshape(1)
        result = backward(c, width, take, own, got, fwd, spread_t, inv_t, result)
    return tuple(result)


def solution(mesh):
    return jax.shard_map(
        functools.partial(per_device, dict(mesh.shape)),
        mesh=mesh,
        in_specs=(
            P("node", ("shift", "rhs")),
            P(None, ("shift", "rhs")),
            P("node"),
            P("node", None, None),
            P("node", None, None),
            P("node", None),
            P("node", None),
        ),
        out_specs=(P("node", ("shift", "rhs")), P(None, ("shift", "rhs"))),
        check_vma=False,
    )
```

time: 290 us -> 150 us (0.52)
  the two profiles are of different devices: /device:TPU:0 before, /device:TPU:12 now
where the time goes in v1:
time: 150 us; the launch traced here: 149 us
  Pallas kernels  52.1 us (35%)
  starting transfers between devices  51.1 us (34%)
  local copies, waits for them, and re-layouts  21.6 us (14%)
  waiting for transfers between devices  20.6 us (14%)
  other arithmetic  2.05 us (1%)
    unnamed x68, local copies, waits for them, and re-layouts  21 us
    ppermute x12, starting transfers between devices, per_device(): lax.ppermute(mine_blocks[s], 'node', [(i, i ^ s) for i in range(nodes)])  17 us
    pallas_call x4, Pallas kernels, backward(): pl.pallas_call(functools.partial(backward_kernel, chunk), in_specs=[smem_...  15.6 us
    pallas_call x4, Pallas kernels, root_solve(): pl.pallas_call(functools.partial(root_kernel, chunk, count), in_specs=[sm...  12.8 us
    ppermute x4, starting transfers between devices, per_device(): other = lax.ppermute(part, 'node', top)  11.8 us
    ppermute x4, waiting for transfers between devices, per_device(): wide = wide + lax.ppermute(part, 'node', pairs).astype(F32)  8.44 us
    pallas_call x2, Pallas kernels, pick(): pl.pallas_call(functools.partial(pick_kernel, nodes, first, count), in_sp...  8.19 us
    ppermute x4, starting transfers between devices, per_device(): got = lax.ppermute(own, 'node', [(b, a) for a, b in pairs])  8.18 us
  transfers between devices with their start and end apart: 33, of which 7 were waited for; matrix products, arithmetic and copies ran while one was open for 1% of the time, Pallas kernels for 32%

profile of v1, /device:TPU:12, one launch (start us, length us, event | category | flops | bytes accessed | tf_op | source)
XLA Modules:
  0.0 148.8 jit_solution(11827845061400380242)
XLA Ops:
  2.3 1.3 collective-permute-start
  3.6 1.6 %copy-done.18 = bf16[2048,512]{1,0:T(8,128)(2,1)S(1)} copy-done((bf16[2048,512]{1,0:T(8,128)(2,1)S(1)}, bf16[2048,512]{1,0:T(8,128)(2,1)}, u32[]{:S(2)}) %copy-start.18) | copy-done | bytes 2097176
  5.9 5.5 %pick.2 = (bf16[512,128]{1,0:T(8,128)(2,1)S(1)}, bf16[512,128]{1,0:T(8,128)(2,1)S(1)}, bf16[512,128]{1,0:T(8,128)(2,1)S(1)}, bf16[512,128]{1,0:T(8,128)(2,1)S(1)...) custom-call(s32[1]{0:T(128)} %bitcast.1.me_ref, ...), custom_call_target="tpu_custom_call" | custom-call | flops 3221225472 | bytes 3145728 | tf_op jit(solution)/shard_map/pick/pallas_call | solution.py:90
  14.7 3.3 %collective-permute-start.9 = (bf16[512,128]{1,0:T(8,128)(2,1)}, bf16[512,128]{1,0:T(8,128)(2,1)S(1)}, u32[]{:S(2)}, u32[]{:S(2)}) collective-permute-start(bf16[512,128]{1,0:T(8,128)(2,1)} %get-tuple-element.45), channel_id=1, source_target_pairs={{0,4},{4,0},{8,12},{12,8},{1,5},{5,1},{9,13},{13,9},{2,6},{6,2},{1... | collective-permute-start | bytes 393224 | tf_op jit(solution)/shard_map/ppermute | solution.py:333
  19.5 2.8 %collective-permute-start.15 = (bf16[512,128]{1,0:T(8,128)(2,1)}, bf16[512,128]{1,0:T(8,128)(2,1)S(1)}, u32[]{:S(2)}, u32[]{:S(2)}) collective-permute-start(bf16[512,128]{1,0:T(8,128)(2,1)} %get-tuple-element.54), channel_id=1, source_target_pairs={{0,4},{4,0},{8,12},{12,8},{1,5},{5,1},{9,13},{13,9},{2,6},{6,2},{1... | collective-permute-start | bytes 393224 | tf_op jit(solution)/shard_map/ppermute | solution.py:333
  22.4 6.7 %prep.1 = (bf16[1024,2048]{1,0:T(8,128)(2,1)S(1)}, bf16[2048,1024]{1,0:T(8,128)(2,1)S(1)}, bf16[4,512,512]{2,1,0:T(8,128)(2,1)S(1)}) custom-call(s32[4,512]{1,0:T(4,128)S(1)} %copy-done.31, bf16[4,512,512]{2,1,0:T(8,128)(2,1)S(1)} %copy-done.17, bf16[4,512,512]{2,1,0:T(8,128)(2,1)S(1)} %copy-done.5), custom_call_target="tpu_custom_call" | custom-call | flops 6442450944 | bytes 14680064 | tf_op jit(solution)/shard_map/prep/pallas_call | solution.py:125
  29.1 2.0 %copy-done.1 = bf16[2048,1024]{1,0:T(8,128)(2,1)} copy-done((bf16[2048,1024]{1,0:T(8,128)(2,1)}, bf16[2048,1024]{1,0:T(8,128)(2,1)S(1)}, u32[]{:S(2)}) %copy-start.1) | copy-done | bytes 4194328
  31.1 2.0 %copy-done.3 = bf16[1024,2048]{1,0:T(8,128)(2,1)} copy-done((bf16[1024,2048]{1,0:T(8,128)(2,1)}, bf16[1024,2048]{1,0:T(8,128)(2,1)S(1)}, u32[]{:S(2)}) %copy-start.3) | copy-done | bytes 4194328
  33.1 1.3 copy-done.6
  34.4 2.7 %pick.3 = (bf16[512,128]{1,0:T(8,128)(2,1)S(1)}, bf16[512,128]{1,0:T(8,128)(2,1)S(1)}, bf16[512,128]{1,0:T(8,128)(2,1)S(1)}, bf16[512,128]{1,0:T(8,128)(2,1)S(1)}) custom-call(s32[1]{0:T(128)} %bitcast.1.me_ref, s32[16,128]{1,0:T(8,128)S(1)} %bitcast.4, bf16[2048,512]{1,0:T(8,128)(2,1)S(1)} %copy-done.19), custom_call_target="tpu_custom_call" | custom-call | flops 1073741824 | bytes 1048576 | tf_op jit(solution)/shard_map/pick/pallas_call | solution.py:90
  41.6 2.8 %collective-permute-start.21 = (bf16[512,128]{1,0:T(8,128)(2,1)}, bf16[512,128]{1,0:T(8,128)(2,1)S(1)}, u32[]{:S(2)}, u32[]{:S(2)}) collective-permute-start(bf16[512,128]{1,0:T(8,128)(2,1)} %copy-done.28), channel_id=1, source_target_pairs={{0,4},{4,0},{8,12},{12,8},{1,5},{5,1},{9,13},{13,9},{2,6},{6,2},{1... | collective-permute-start | bytes 393224 | tf_op jit(solution)/shard_map/ppermute | solution.py:333
  46.1 2.2 %copy-done.4 = bf16[1024,2048]{1,0:T(8,128)(2,1)S(1)} copy-done((bf16[1024,2048]{1,0:T(8,128)(2,1)S(1)}, bf16[1024,2048]{1,0:T(8,128)(2,1)}, u32[]{:S(2)}) %copy-start.4) | copy-done | bytes 4194328
  48.3 2.7 %forward.4 = (bf16[2048,128]{1,0:T(8,128)(2,1)S(1)}, bf16[1024,128]{1,0:T(8,128)(2,1)S(1)}, f32[1024,128]{1,0:T(8,128)S(1)}) custom-call(s32[1]{0:T(128)} %bitcast.1.me_ref, bf16[4,512,512]{2,1,0:T(8,128)(2,1)S(1)} %copy-done.5, bf16[1024,2048]{1,0:T(8,128)(2,1)S(1)} %copy-done.4, bf16[512,128]{1,0:T(8,128)(2,1)S(1)} %get-tuple-element.44.rest_0_, ...), custom_call_target="tpu_custom_call" | custom-call | flops 805306368 | bytes 8126464 | tf_op jit(solution)/shard_map/forward/pallas_call | solution.py:161
  51.8 2.7 %collective-permute-start.27 = (bf16[512,128]{1,0:T(8,128)(2,1)S(1)}, bf16[512,128]{1,0:T(8,128)(2,1)S(1)}, u32[]{:S(2)}, u32[]{:S(2)}) collective-permute-start(bf16[512,128]{1,0:T(8,128)(2,1)S(1)} %copy-done.25), channel_id=1, source_target_pairs={{0,4},{4,0},{8,12},{12,8},{1,5},{5,1},{9,13},{13,9},{2,6},{6,2},{1... | collective-permute-start | bytes 393224 | tf_op jit(solution)/shard_map/ppermute | solution.py:333
  54.5 3.7 %collective-permute-done.17.rest_3_ = bf16[512,128]{1,0:T(8,128)(2,1)S(1)} collective-permute-done((bf16[512,128]{1,0:T(8,128)(2,1)}, bf16[512,128]{1,0:T(8,128)(2,1)S(1)}, u32[]{:S(2)}, u32[]{:S(2)}) %collective-permute-start.17) | collective-permute-done | bytes 131104 | tf_op jit(solution)/shard_map/ppermute | solution.py:333
  58.2 3.5 %collective-permute-start.1 = (bf16[512,128]{1,0:T(8,128)(2,1)S(1)}, bf16[512,128]{1,0:T(8,128)(2,1)S(1)}, u32[]{:S(2)}, u32[]{:S(2)}) collective-permute-start(bf16[512,128]{1,0:T(8,128)(2,1)S(1)} %pad_maximum_fusion.1), channel_id=1, source_target_pairs={{4,8},{8,4},{5,9},{9,5},{6,10},{10,6},{7,11},{11,7},{20,24},{24,20... | collective-permute-start | bytes 393224 | tf_op jit(solution)/shard_map/ppermute | solution.py:311
  61.7 1.7 %forward.5 = (bf16[2048,128]{1,0:T(8,128)(2,1)S(1)}, bf16[1024,128]{1,0:T(8,128)(2,1)S(1)}, f32[1024,128]{1,0:T(8,128)S(1)}) custom-call(s32[1]{0:T(128)} %bitcast.1.me_ref, bf16[4,512,512]{2,1,0:T(8,128)(2,1)S(1)} %copy-done.5, bf16[1024,2048]{1,0:T(8,128)(2,1)S(1)} %copy-done.4, bf16[512,128]{1,0:T(8,128)(2,1)S(1)} %get-tuple-element.53.rest_0_, ...), custom_call_target="tpu_custom_call" | custom-call | flops 805306368 | bytes 8126464 | tf_op jit(solution)/shard_map/forward/pallas_call | solution.py:161
  64.8 1.8 %collective-permute-done.23.rest_3_ = bf16[512,128]{1,0:T(8,128)(2,1)S(1)} collective-permute-done((bf16[512,128]{1,0:T(8,128)(2,1)}, bf16[512,128]{1,0:T(8,128)(2,1)S(1)}, u32[]{:S(2)}, u32[]{:S(2)}) %collective-permute-start.23) | collective-permute-done | bytes 131104 | tf_op jit(solution)/shard_map/ppermute | solution.py:333
  66.7 1.3 collective-permute-start.12
  67.9 1.7 %forward.6 = (bf16[2048,128]{1,0:T(8,128)(2,1)S(1)}, bf16[1024,128]{1,0:T(8,128)(2,1)S(1)}, f32[1024,128]{1,0:T(8,128)S(1)}) custom-call(s32[1]{0:T(128)} %bitcast.1.me_ref, bf16[4,512,512]{2,1,0:T(8,128)(2,1)S(1)} %copy-done.5, bf16[1024,2048]{1,0:T(8,128)(2,1)S(1)} %copy-done.4, bf16[512,128]{1,0:T(8,128)(2,1)S(1)} %get-tuple-element.60.rest_0_, ...), custom_call_target="tpu_custom_call" | custom-call | flops 805306368 | bytes 8126464 | tf_op jit(solution)/shard_map/forward/pallas_call | solution.py:161
  69.7 1.6 %collective-permute-done.1 = bf16[512,128]{1,0:T(8,128)(2,1)S(1)} collective-permute-done((bf16[512,128]{1,0:T(8,128)(2,1)S(1)}, bf16[512,128]{1,0:T(8,128)(2,1)S(1)}, u32[]{:S(2)}, u32[]{:S(2)}) %collective-permute-start.1) | collective-permute-done | bytes 131104 | tf_op jit(solution)/shard_map/ppermute | solution.py:311
  71.2 1.3 collective-permute-start.18
  73.5 1.3 collective-permute-start.24
  75.4 1.3 collective-permute-done.29.rest_3_
  76.7 1.7 %forward.7 = (bf16[2048,128]{1,0:T(8,128)(2,1)S(1)}, bf16[1024,128]{1,0:T(8,128)(2,1)S(1)}, f32[1024,128]{1,0:T(8,128)S(1)}) custom-call(s32[1]{0:T(128)} %bitcast.1.me_ref, bf16[4,512,512]{2,1,0:T(8,128)(2,1)S(1)} %copy-done.5, bf16[1024,2048]{1,0:T(8,128)(2,1)S(1)} %copy-done.4, bf16[512,128]{1,0:T(8,128)(2,1)S(1)} %get-tuple-element.67.rest_0_, ...), custom_call_target="tpu_custom_call" | custom-call | flops 805306368 | bytes 8126464 | tf_op jit(solution)/shard_map/forward/pallas_call | solution.py:161
  78.4 1.3 collective-permute-start.30
  79.7 1.6 %collective-permute-start.3 = (bf16[1024,128]{1,0:T(8,128)(2,1)S(1)}, bf16[1024,128]{1,0:T(8,128)(2,1)S(1)}, u32[]{:S(2)}, u32[]{:S(2)}) collective-permute-start(bf16[1024,128]{1,0:T(8,128)(2,1)S(1)} %pad_maximum_fusion.rest_0_), channel_id=1, source_target_pairs={{0,2},{1,3},{2,0},{3,1},{4,6},{5,7},{6,4},{7,5},{8,10},{9,11},{10,... | collective-permute-start | bytes 786440 | tf_op jit(solution)/shard_map/ppermute | solution.py:318
  81.3 7.2 %collective-permute-done.24 = bf16[1024,128]{1,0:T(8,128)(2,1)S(1)} collective-permute-done((bf16[1024,128]{1,0:T(8,128)(2,1)S(1)}, bf16[1024,128]{1,0:T(8,128)(2,1)S(1)}, u32[]{:S(2)}, u32[]{:S(2)}) %collective-permute-start.24) | collective-permute-done | bytes 262176 | tf_op jit(solution)/shard_map/ppermute | solution.py:336
  88.5 1.5 collective-permute-start.7
  90.0 1.3 collective-permute-done.30
  91.9 3.4 %collective-permute-start.25 = (bf16[1024,128]{1,0:T(8,128)(2,1)S(1)}, bf16[1024,128]{1,0:T(8,128)(2,1)S(1)}, u32[]{:S(2)}, u32[]{:S(2)}) collective-permute-start(bf16[1024,128]{1,0:T(8,128)(2,1)S(1)} %add_convert_fusion.1.one_ref), channel_id=1, source_target_pairs={{4,8},{8,4},{5,9},{9,5},{6,10},{10,6},{7,11},{11,7},{20,24},{24,20... | collective-permute-start | bytes 786440 | tf_op jit(solution)/shard_map/ppermute | solution.py:338
  95.3 2.5 %collective-permute-start.31 = (bf16[1024,128]{1,0:T(8,128)(2,1)S(1)}, bf16[1024,128]{1,0:T(8,128)(2,1)S(1)}, u32[]{:S(2)}, u32[]{:S(2)}) collective-permute-start(bf16[1024,128]{1,0:T(8,128)(2,1)S(1)} %add_convert_fusion.one_ref), channel_id=1, source_target_pairs={{4,8},{8,4},{5,9},{9,5},{6,10},{10,6},{7,11},{11,7},{20,24},{24,20... | collective-permute-start | bytes 786440 | tf_op jit(solution)/shard_map/ppermute | solution.py:338
  98.1 3.3 %collective-permute-start.13 = (bf16[1024,128]{1,0:T(8,128)(2,1)S(1)}, bf16[1024,128]{1,0:T(8,128)(2,1)S(1)}, u32[]{:S(2)}, u32[]{:S(2)}) collective-permute-start(bf16[1024,128]{1,0:T(8,128)(2,1)S(1)} %add_convert_fusion.3.one_ref), channel_id=1, source_target_pairs={{4,8},{8,4},{5,9},{9,5},{6,10},{10,6},{7,11},{11,7},{20,24},{24,20... | collective-permute-start | bytes 786440 | tf_op jit(solution)/shard_map/ppermute | solution.py:338
  101.4 2.5 %collective-permute-start.19 = (bf16[1024,128]{1,0:T(8,128)(2,1)S(1)}, bf16[1024,128]{1,0:T(8,128)(2,1)S(1)}, u32[]{:S(2)}, u32[]{:S(2)}) collective-permute-start(bf16[1024,128]{1,0:T(8,128)(2,1)S(1)} %add_convert_fusion.2.one_ref), channel_id=1, source_target_pairs={{4,8},{8,4},{5,9},{9,5},{6,10},{10,6},{7,11},{11,7},{20,24},{24,20... | collective-permute-start | bytes 786440 | tf_op jit(solution)/shard_map/ppermute | solution.py:338
  105.0 3.7 %collective-permute-done.31.two_ref = bf16[1024,128]{1,0:T(8,128)(2,1)S(1)} collective-permute-done((bf16[1024,128]{1,0:T(8,128)(2,1)S(1)}, bf16[1024,128]{1,0:T(8,128)(2,1)S(1)}, u32[]{:S(2)}, u32[]{:S(2)}) %collective-permute-start.31) | collective-permute-done | bytes 262176 | tf_op jit(solution)/shard_map/ppermute | solution.py:338
  108.7 3.7 %root_solve.7.own_ref = bf16[1024,128]{1,0:T(8,128)(2,1)} custom-call(s32[8]{0:T(128)S(1)} %iota_xor_fusion.order_ref, bf16[1024,1024]{1,0:T(8,128)(2,1)S(1)} %get-tuple-element.41.whole_ref, bf16[1024,1024]{1,0:T(8,128)(2,1)S(1)} %get-tuple-element.42.whole_t_ref, bf16[1024,512]{1,0:T(8,128)(2,1)S(1)} %copy-done.8, ...), custom_call_target="tpu_custom_call" | custom-call | flops 536870912 | bytes 5242880 | tf_op jit(solution)/shard_map/root_solve/pallas_call | solution.py:223
  112.4 2.0 %collective-permute-start.32 = (bf16[1024,128]{1,0:T(8,128)(2,1)}, bf16[1024,128]{1,0:T(8,128)(2,1)}, u32[]{:S(2)}, u32[]{:S(2)}) collective-permute-start(bf16[1024,128]{1,0:T(8,128)(2,1)} %root_solve.7.own_ref), channel_id=1, source_target_pairs={{4,0},{8,12},{5,1},{9,13},{6,2},{10,14},{7,3},{11,15},{20,16},{24,... | collective-permute-start | bytes 786440 | tf_op jit(solution)/shard_map/ppermute | solution.py:345
  114.5 3.0 %root_solve.6.own_ref = bf16[1024,128]{1,0:T(8,128)(2,1)S(1)} custom-call(s32[8]{0:T(128)S(1)} %iota_xor_fusion.order_ref, bf16[1024,1024]{1,0:T(8,128)(2,1)S(1)} %get-tuple-element.41.whole_ref, bf16[1024,1024]{1,0:T(8,128)(2,1)S(1)} %get-tuple-element.42.whole_t_ref, bf16[1024,512]{1,0:T(8,128)(2,1)S(1)} %copy-done.8, ...), custom_call_target="tpu_custom_call" | custom-call | flops 536870912 | bytes 5242880 | tf_op jit(solution)/shard_map/root_solve/pallas_call | solution.py:223
  117.5 2.0 %collective-permute-start.26 = (bf16[1024,128]{1,0:T(8,128)(2,1)S(1)}, bf16[1024,128]{1,0:T(8,128)(2,1)}, u32[]{:S(2)}, u32[]{:S(2)}) collective-permute-start(bf16[1024,128]{1,0:T(8,128)(2,1)S(1)} %root_solve.6.own_ref), channel_id=1, source_target_pairs={{4,0},{8,12},{5,1},{9,13},{6,2},{10,14},{7,3},{11,15},{20,16},{24,... | collective-permute-start | bytes 786440 | tf_op jit(solution)/shard_map/ppermute | solution.py:345
  119.5 3.0 %root_solve.5.own_ref = bf16[1024,128]{1,0:T(8,128)(2,1)S(1)} custom-call(s32[8]{0:T(128)S(1)} %iota_xor_fusion.order_ref, bf16[1024,1024]{1,0:T(8,128)(2,1)S(1)} %get-tuple-element.41.whole_ref, bf16[1024,1024]{1,0:T(8,128)(2,1)S(1)} %get-tuple-element.42.whole_t_ref, bf16[1024,512]{1,0:T(8,128)(2,1)S(1)} %copy-done.8, ...), custom_call_target="tpu_custom_call" | custom-call | flops 536870912 | bytes 5242880 | tf_op jit(solution)/shard_map/root_solve/pallas_call | solution.py:223
  122.5 2.2 %collective-permute-start.20 = (bf16[1024,128]{1,0:T(8,128)(2,1)S(1)}, bf16[1024,128]{1,0:T(8,128)(2,1)}, u32[]{:S(2)}, u32[]{:S(2)}) collective-permute-start(bf16[1024,128]{1,0:T(8,128)(2,1)S(1)} %root_solve.5.own_ref), channel_id=1, source_target_pairs={{4,0},{8,12},{5,1},{9,13},{6,2},{10,14},{7,3},{11,15},{20,16},{24,... | collective-permute-start | bytes 786440 | tf_op jit(solution)/shard_map/ppermute | solution.py:345
  124.7 3.0 %root_solve.4.own_ref = bf16[1024,128]{1,0:T(8,128)(2,1)S(1)} custom-call(s32[8]{0:T(128)S(1)} %iota_xor_fusion.order_ref, bf16[1024,1024]{1,0:T(8,128)(2,1)S(1)} %get-tuple-element.41.whole_ref, bf16[1024,1024]{1,0:T(8,128)(2,1)S(1)} %get-tuple-element.42.whole_t_ref, bf16[1024,512]{1,0:T(8,128)(2,1)S(1)} %copy-done.8, ...), custom_call_target="tpu_custom_call" | custom-call | flops 536870912 | bytes 5242880 | tf_op jit(solution)/shard_map/root_solve/pallas_call | solution.py:223
  127.7 2.0 %collective-permute-start.14 = (bf16[1024,128]{1,0:T(8,128)(2,1)S(1)}, bf16[1024,128]{1,0:T(8,128)(2,1)}, u32[]{:S(2)}, u32[]{:S(2)}) collective-permute-start(bf16[1024,128]{1,0:T(8,128)(2,1)S(1)} %root_solve.4.own_ref), channel_id=1, source_target_pairs={{4,0},{8,12},{5,1},{9,13},{6,2},{10,14},{7,3},{11,15},{20,16},{24,... | collective-permute-start | bytes 786440 | tf_op jit(solution)/shard_map/ppermute | solution.py:345
  129.7 2.2 %copy-done.2 = bf16[2048,1024]{1,0:T(8,128)(2,1)S(1)} copy-done((bf16[2048,1024]{1,0:T(8,128)(2,1)S(1)}, bf16[2048,1024]{1,0:T(8,128)(2,1)}, u32[]{:S(2)}) %copy-start.2) | copy-done | bytes 4194328
  133.0 4.0 %backward.4 = (bf16[2048,512]{1,0:T(8,128)(2,1)}, bf16[1024,512]{1,0:T(8,128)(2,1)}) custom-call(s32[1]{0:T(128)} %bitcast.take_ref, bf16[1024,128]{1,0:T(8,128)(2,1)} %root_solve.7.own_ref, bf16[1024,128]{1,0:T(8,128)(2,1)} %collective-permute-done.32.got_ref, bf16[2048,128]{1,0:T(8,128)(2,1)S(1)} %copy-done.10, bf16[2048,1024]{1,0:T(8,128)(2,1)S(1)} %copy-done.2, ...), custom_call_target="tpu_custom_call" | custom-call | flops 805306368 | bytes 8126464 | tf_op jit(solution)/shard_map/backward/pallas_call | solution.py:266
  137.0 3.9 %backward.5 = (bf16[2048,512]{1,0:T(8,128)(2,1)}, bf16[1024,512]{1,0:T(8,128)(2,1)}) custom-call(s32[1]{0:T(128)} %bitcast.take_ref, bf16[1024,128]{1,0:T(8,128)(2,1)S(1)} %root_solve.6.own_ref, bf16[1024,128]{1,0:T(8,128)(2,1)} %collective-permute-done.26.got_ref, bf16[2048,128]{1,0:T(8,128)(2,1)S(1)} %copy-done.16, ...), custom_call_target="tpu_custom_call", output_to_operand_aliasing={{0}: (6, {}), {1}: (7, {})} | custom-call | flops 805306368 | bytes 8126464 | tf_op jit(solution)/shard_map/backward/pallas_call | solution.py:266
  140.9 3.9 %backward.6 = (bf16[2048,512]{1,0:T(8,128)(2,1)}, bf16[1024,512]{1,0:T(8,128)(2,1)}) custom-call(s32[1]{0:T(128)} %bitcast.take_ref, bf16[1024,128]{1,0:T(8,128)(2,1)S(1)} %root_solve.5.own_ref, bf16[1024,128]{1,0:T(8,128)(2,1)} %collective-permute-done.20.got_ref, bf16[2048,128]{1,0:T(8,128)(2,1)S(1)} %copy-done.14, ...), custom_call_target="tpu_custom_call", output_to_operand_aliasing={{0}: (6, {}), {1}: (7, {})} | custom-call | flops 805306368 | bytes 8126464 | tf_op jit(solution)/shard_map/backward/pallas_call | solution.py:266
  144.8 3.8 %backward.7 = (bf16[2048,512]{1,0:T(8,128)(2,1)}, bf16[1024,512]{1,0:T(8,128)(2,1)}) custom-call(s32[1]{0:T(128)} %bitcast.take_ref, bf16[1024,128]{1,0:T(8,128)(2,1)S(1)} %root_solve.4.own_ref, bf16[1024,128]{1,0:T(8,128)(2,1)} %collective-permute-done.14.got_ref, bf16[2048,128]{1,0:T(8,128)(2,1)S(1)} %copy-done.12, ...), custom_call_target="tpu_custom_call", output_to_operand_aliasing={{0}: (6, {}), {1}: (7, {})} | custom-call | flops 805306368 | bytes 8126464 | tf_op jit(solution)/shard_map/backward/pallas_call | solution.py:266
  (111 shorter events, 20.0 us)
Async XLA Ops:
  2.3 36.7 %collective-permute-start = (bf16[256,128]{1,0:T(8,128)(2,1)}, bf16[256,128]{1,0:T(8,128)(2,1)}, u32[]{:S(2)}, u32[]{:S(2)}) collective-permute-start(bf16[256,128]{1,0:T(8,128)(2,1)} %constant_dynamic-slice_fusion), channel_id=1, source_target_pairs={{0,4},{12,8},{1,5},{13,9},{2,6},{14,10},{3,7},{15,11},{16,20},{28,... | collective-permute-start | bytes 196616 | tf_op jit(solution)/shard_map/ppermute | solution.py:310
  5.9 16.4 %copy-start.5 = (bf16[4,512,512]{2,1,0:T(8,128)(2,1)S(1)}, bf16[4,512,512]{2,1,0:T(8,128)(2,1)}, u32[]{:S(2)}) copy-start(bf16[4,512,512]{2,1,0:T(8,128)(2,1)} %inv_ref.9) | copy-start | bytes 6291460
  5.9 16.4 %copy-start.17 = (bf16[4,512,512]{2,1,0:T(8,128)(2,1)S(1)}, bf16[4,512,512]{2,1,0:T(8,128)(2,1)}, u32[]{:S(2)}) copy-start(bf16[4,512,512]{2,1,0:T(8,128)(2,1)} %couple_ref.1) | copy-start | bytes 6291460
  5.9 16.4 %copy-start.31 = (s32[4,512]{1,0:T(4,128)S(1)}, s32[4,512]{1,0:T(4,128)}, u32[]{:S(2)}) copy-start(s32[4,512]{1,0:T(4,128)} %rows_ref.1) | copy-start | bytes 24580
  14.7 25.4 %collective-permute-start.9 = (bf16[512,128]{1,0:T(8,128)(2,1)}, bf16[512,128]{1,0:T(8,128)(2,1)S(1)}, u32[]{:S(2)}, u32[]{:S(2)}) collective-permute-start(bf16[512,128]{1,0:T(8,128)(2,1)} %get-tuple-element.45), channel_id=1, source_target_pairs={{0,4},{4,0},{8,12},{12,8},{1,5},{5,1},{9,13},{13,9},{2,6},{6,2},{1... | collective-permute-start | bytes 393224 | tf_op jit(solution)/shard_map/ppermute | solution.py:333
  18.0 23.7 %collective-permute-start.10 = (bf16[512,128]{1,0:T(8,128)(2,1)}, bf16[512,128]{1,0:T(8,128)(2,1)S(1)}, u32[]{:S(2)}, u32[]{:S(2)}) collective-permute-start(bf16[512,128]{1,0:T(8,128)(2,1)} %get-tuple-element.46), channel_id=1, source_target_pairs={{0,8},{4,12},{8,0},{12,4},{1,9},{5,13},{9,1},{13,5},{2,10},{6,14},... | collective-permute-start | bytes 393224 | tf_op jit(solution)/shard_map/ppermute | solution.py:333
  19.0 25.4 %collective-permute-start.11 = (bf16[512,128]{1,0:T(8,128)(2,1)}, bf16[512,128]{1,0:T(8,128)(2,1)}, u32[]{:S(2)}, u32[]{:S(2)}) collective-permute-start(bf16[512,128]{1,0:T(8,128)(2,1)} %get-tuple-element.47), channel_id=1, source_target_pairs={{0,12},{4,8},{8,4},{12,0},{1,13},{5,9},{9,5},{13,1},{2,14},{6,10},... | collective-permute-start | bytes 393224 | tf_op jit(solution)/shard_map/ppermute | solution.py:333
  19.5 14.9 %copy-start.19 = (bf16[2048,512]{1,0:T(8,128)(2,1)S(1)}, bf16[2048,512]{1,0:T(8,128)(2,1)}, u32[]{:S(2)}) copy-start(bf16[2048,512]{1,0:T(8,128)(2,1)} %loads_ref.10) | copy-start | bytes 6291460
  19.5 14.9 %copy-start.33 = (s32[2048]{0:T(1024)S(1)}, s32[2048]{0:T(1024)}, u32[]{:S(2)}) copy-start(s32[2048]{0:T(1024)} %param.9) | copy-start | bytes 24580
  19.5 26.0 %collective-permute-start.15 = (bf16[512,128]{1,0:T(8,128)(2,1)}, bf16[512,128]{1,0:T(8,128)(2,1)S(1)}, u32[]{:S(2)}, u32[]{:S(2)}) collective-permute-start(bf16[512,128]{1,0:T(8,128)(2,1)} %get-tuple-element.54), channel_id=1, source_target_pairs={{0,4},{4,0},{8,12},{12,8},{1,5},{5,1},{9,13},{13,9},{2,6},{6,2},{1... | collective-permute-start | bytes 393224 | tf_op jit(solution)/shard_map/ppermute | solution.py:333
  39.1 12.7 %collective-permute-start.16 = (bf16[512,128]{1,0:T(8,128)(2,1)}, bf16[512,128]{1,0:T(8,128)(2,1)S(1)}, u32[]{:S(2)}, u32[]{:S(2)}) collective-permute-start(bf16[512,128]{1,0:T(8,128)(2,1)} %copy-done.30), channel_id=1, source_target_pairs={{0,8},{4,12},{8,0},{12,4},{1,9},{5,13},{9,1},{13,5},{2,10},{6,14},... | collective-permute-start | bytes 393224 | tf_op jit(solution)/shard_map/ppermute | solution.py:333
  40.1 18.1 %collective-permute-start.17 = (bf16[512,128]{1,0:T(8,128)(2,1)}, bf16[512,128]{1,0:T(8,128)(2,1)S(1)}, u32[]{:S(2)}, u32[]{:S(2)}) collective-permute-start(bf16[512,128]{1,0:T(8,128)(2,1)} %copy-done.29), channel_id=1, source_target_pairs={{0,12},{4,8},{8,4},{12,0},{1,13},{5,9},{9,5},{13,1},{2,14},{6,10},... | collective-permute-start | bytes 393224 | tf_op jit(solution)/shard_map/ppermute | solution.py:333
  41.6 22.6 %collective-permute-start.21 = (bf16[512,128]{1,0:T(8,128)(2,1)}, bf16[512,128]{1,0:T(8,128)(2,1)S(1)}, u32[]{:S(2)}, u32[]{:S(2)}) collective-permute-start(bf16[512,128]{1,0:T(8,128)(2,1)} %copy-done.28), channel_id=1, source_target_pairs={{0,4},{4,0},{8,12},{12,8},{1,5},{5,1},{9,13},{13,9},{2,6},{6,2},{1... | collective-permute-start | bytes 393224 | tf_op jit(solution)/shard_map/ppermute | solution.py:333
  44.4 19.9 %collective-permute-start.22 = (bf16[512,128]{1,0:T(8,128)(2,1)}, bf16[512,128]{1,0:T(8,128)(2,1)S(1)}, u32[]{:S(2)}, u32[]{:S(2)}) collective-permute-start(bf16[512,128]{1,0:T(8,128)(2,1)} %copy-done.27), channel_id=1, source_target_pairs={{0,8},{4,12},{8,0},{12,4},{1,9},{5,13},{9,1},{13,5},{2,10},{6,14},... | collective-permute-start | bytes 393224 | tf_op jit(solution)/shard_map/ppermute | solution.py:333
  45.5 21.1 %collective-permute-start.23 = (bf16[512,128]{1,0:T(8,128)(2,1)}, bf16[512,128]{1,0:T(8,128)(2,1)S(1)}, u32[]{:S(2)}, u32[]{:S(2)}) collective-permute-start(bf16[512,128]{1,0:T(8,128)(2,1)} %copy-done.26), channel_id=1, source_target_pairs={{0,12},{4,8},{8,4},{12,0},{1,13},{5,9},{9,5},{13,1},{2,14},{6,10},... | collective-permute-start | bytes 393224 | tf_op jit(solution)/shard_map/ppermute | solution.py:333
  48.3 3.5 %copy-start.25 = (bf16[512,128]{1,0:T(8,128)(2,1)S(1)}, bf16[512,128]{1,0:T(8,128)(2,1)}, u32[]{:S(2)}) copy-start(bf16[512,128]{1,0:T(8,128)(2,1)} %copy-done.24) | copy-start | bytes 393220
  51.8 21.7 %collective-permute-start.27 = (bf16[512,128]{1,0:T(8,128)(2,1)S(1)}, bf16[512,128]{1,0:T(8,128)(2,1)S(1)}, u32[]{:S(2)}, u32[]{:S(2)}) collective-permute-start(bf16[512,128]{1,0:T(8,128)(2,1)S(1)} %copy-done.25), channel_id=1, source_target_pairs={{0,4},{4,0},{8,12},{12,8},{1,5},{5,1},{9,13},{13,9},{2,6},{6,2},{1... | collective-permute-start | bytes 393224 | tf_op jit(solution)/shard_map/ppermute | solution.py:333
  58.2 13.0 %collective-permute-start.1 = (bf16[512,128]{1,0:T(8,128)(2,1)S(1)}, bf16[512,128]{1,0:T(8,128)(2,1)S(1)}, u32[]{:S(2)}, u32[]{:S(2)}) collective-permute-start(bf16[512,128]{1,0:T(8,128)(2,1)S(1)} %pad_maximum_fusion.1), channel_id=1, source_target_pairs={{4,8},{8,4},{5,9},{9,5},{6,10},{10,6},{7,11},{11,7},{20,24},{24,20... | collective-permute-start | bytes 393224 | tf_op jit(solution)/shard_map/ppermute | solution.py:311
  61.7 2.6 %copy-start.23 = (bf16[512,128]{1,0:T(8,128)(2,1)S(1)}, bf16[512,128]{1,0:T(8,128)(2,1)}, u32[]{:S(2)}) copy-start(bf16[512,128]{1,0:T(8,128)(2,1)} %copy-done.22) | copy-start | bytes 393220
  61.7 2.6 %copy-start.21 = (bf16[512,128]{1,0:T(8,128)(2,1)S(1)}, bf16[512,128]{1,0:T(8,128)(2,1)}, u32[]{:S(2)}) copy-start(bf16[512,128]{1,0:T(8,128)(2,1)} %copy-done.20) | copy-start | bytes 393220
  64.3 10.5 %collective-permute-start.28 = (bf16[512,128]{1,0:T(8,128)(2,1)S(1)}, bf16[512,128]{1,0:T(8,128)(2,1)S(1)}, u32[]{:S(2)}, u32[]{:S(2)}) collective-permute-start(bf16[512,128]{1,0:T(8,128)(2,1)S(1)} %copy-done.23), channel_id=1, source_target_pairs={{0,8},{4,12},{8,0},{12,4},{1,9},{5,13},{9,1},{13,5},{2,10},{6,14},... | collective-permute-start | bytes 393224 | tf_op jit(solution)/shard_map/ppermute | solution.py:333
  64.3 12.4 %collective-permute-start.29 = (bf16[512,128]{1,0:T(8,128)(2,1)S(1)}, bf16[512,128]{1,0:T(8,128)(2,1)S(1)}, u32[]{:S(2)}, u32[]{:S(2)}) collective-permute-start(bf16[512,128]{1,0:T(8,128)(2,1)S(1)} %copy-done.21), channel_id=1, source_target_pairs={{0,12},{4,8},{8,4},{12,0},{1,13},{5,9},{9,5},{13,1},{2,14},{6,10},... | collective-permute-start | bytes 393224 | tf_op jit(solution)/shard_map/ppermute | solution.py:333
  66.7 13.1 %collective-permute-start.12 = (bf16[1024,128]{1,0:T(8,128)(2,1)S(1)}, bf16[1024,128]{1,0:T(8,128)(2,1)S(1)}, u32[]{:S(2)}, u32[]{:S(2)}) collective-permute-start(bf16[1024,128]{1,0:T(8,128)(2,1)S(1)} %get-tuple-element.49), channel_id=1, source_target_pairs={{0,4},{12,8},{1,5},{13,9},{2,6},{14,10},{3,7},{15,11},{16,20},{28,... | collective-permute-start | bytes 786440 | tf_op jit(solution)/shard_map/ppermute | solution.py:336
  69.7 7.0 %copy-start.15 = (bf16[2048,128]{1,0:T(8,128)(2,1)}, bf16[2048,128]{1,0:T(8,128)(2,1)S(1)}, u32[]{:S(2)}) copy-start(bf16[2048,128]{1,0:T(8,128)(2,1)S(1)} %get-tuple-element.66.fwd_ref) | copy-start | bytes 1572868
  71.2 20.7 %collective-permute-start.18 = (bf16[1024,128]{1,0:T(8,128)(2,1)S(1)}, bf16[1024,128]{1,0:T(8,128)(2,1)S(1)}, u32[]{:S(2)}, u32[]{:S(2)}) collective-permute-start(bf16[1024,128]{1,0:T(8,128)(2,1)S(1)} %get-tuple-element.58), channel_id=1, source_target_pairs={{0,4},{12,8},{1,5},{13,9},{2,6},{14,10},{3,7},{15,11},{16,20},{28,... | collective-permute-start | bytes 786440 | tf_op jit(solution)/shard_map/ppermute | solution.py:336
  73.5 15.0 %collective-permute-start.24 = (bf16[1024,128]{1,0:T(8,128)(2,1)S(1)}, bf16[1024,128]{1,0:T(8,128)(2,1)S(1)}, u32[]{:S(2)}, u32[]{:S(2)}) collective-permute-start(bf16[1024,128]{1,0:T(8,128)(2,1)S(1)} %get-tuple-element.65), channel_id=1, source_target_pairs={{0,4},{12,8},{1,5},{13,9},{2,6},{14,10},{3,7},{15,11},{16,20},{28,... | collective-permute-start | bytes 786440 | tf_op jit(solution)/shard_map/ppermute | solution.py:336
  74.8 13.7 %collective-permute-start.5 = (bf16[1024,128]{1,0:T(8,128)(2,1)S(1)}, bf16[1024,128]{1,0:T(8,128)(2,1)S(1)}, u32[]{:S(2)}, u32[]{:S(2)}) collective-permute-start(bf16[1024,128]{1,0:T(8,128)(2,1)S(1)} %pad_maximum_fusion.rest_0_), channel_id=1, source_target_pairs={{0,16},{16,0},{1,17},{17,1},{2,18},{18,2},{3,19},{19,3},{4,20},{20... | collective-permute-start | bytes 786440 | tf_op jit(solution)/shard_map/ppermute | solution.py:318
  78.4 19.7 %copy-start.9 = (bf16[2048,128]{1,0:T(8,128)(2,1)}, bf16[2048,128]{1,0:T(8,128)(2,1)S(1)}, u32[]{:S(2)}) copy-start(bf16[2048,128]{1,0:T(8,128)(2,1)S(1)} %get-tuple-element.73.fwd_ref) | copy-start | bytes 1572868
  78.4 12.9 %collective-permute-start.30 = (bf16[1024,128]{1,0:T(8,128)(2,1)S(1)}, bf16[1024,128]{1,0:T(8,128)(2,1)S(1)}, u32[]{:S(2)}, u32[]{:S(2)}) collective-permute-start(bf16[1024,128]{1,0:T(8,128)(2,1)S(1)} %get-tuple-element.72), channel_id=1, source_target_pairs={{0,4},{12,8},{1,5},{13,9},{2,6},{14,10},{3,7},{15,11},{16,20},{28,... | collective-permute-start | bytes 786440 | tf_op jit(solution)/shard_map/ppermute | solution.py:336
  79.7 11.6 %collective-permute-start.3 = (bf16[1024,128]{1,0:T(8,128)(2,1)S(1)}, bf16[1024,128]{1,0:T(8,128)(2,1)S(1)}, u32[]{:S(2)}, u32[]{:S(2)}) collective-permute-start(bf16[1024,128]{1,0:T(8,128)(2,1)S(1)} %pad_maximum_fusion.rest_0_), channel_id=1, source_target_pairs={{0,2},{1,3},{2,0},{3,1},{4,6},{5,7},{6,4},{7,5},{8,10},{9,11},{10,... | collective-permute-start | bytes 786440 | tf_op jit(solution)/shard_map/ppermute | solution.py:318
  88.5 6.8 %collective-permute-start.2 = (bf16[1024,128]{1,0:T(8,128)(2,1)S(1)}, bf16[1024,128]{1,0:T(8,128)(2,1)S(1)}, u32[]{:S(2)}, u32[]{:S(2)}) collective-permute-start(bf16[1024,128]{1,0:T(8,128)(2,1)S(1)} %pad_maximum_fusion.rest_0_), channel_id=1, source_target_pairs={{0,1},{1,0},{2,3},{3,2},{4,5},{5,4},{6,7},{7,6},{8,9},{9,8},{10,11... | collective-permute-start | bytes 786440 | tf_op jit(solution)/shard_map/ppermute | solution.py:318
  88.5 9.4 %collective-permute-start.7 = (bf16[1024,128]{1,0:T(8,128)(2,1)S(1)}, bf16[1024,128]{1,0:T(8,128)(2,1)S(1)}, u32[]{:S(2)}, u32[]{:S(2)}) collective-permute-start(bf16[1024,128]{1,0:T(8,128)(2,1)S(1)} %collective-permute-done.5.rest_4_), channel_id=1, source_target_pairs={{0,2},{1,3},{2,0},{3,1},{4,6},{5,7},{6,4},{7,5},{8,10},{9,11},{10,... | collective-permute-start | bytes 786440 | tf_op jit(solution)/shard_map/ppermute | solution.py:318
  91.3 10.1 %collective-permute-start.6 = (bf16[1024,128]{1,0:T(8,128)(2,1)S(1)}, bf16[1024,128]{1,0:T(8,128)(2,1)S(1)}, u32[]{:S(2)}, u32[]{:S(2)}) collective-permute-start(bf16[1024,128]{1,0:T(8,128)(2,1)S(1)} %collective-permute-done.5.rest_4_), channel_id=1, source_target_pairs={{0,1},{1,0},{2,3},{3,2},{4,5},{5,4},{6,7},{7,6},{8,9},{9,8},{10,11... | collective-permute-start | bytes 786440 | tf_op jit(solution)/shard_map/ppermute | solution.py:318
  91.3 6.7 %collective-permute-start.4 = (bf16[1024,128]{1,0:T(8,128)(2,1)S(1)}, bf16[1024,128]{1,0:T(8,128)(2,1)S(1)}, u32[]{:S(2)}, u32[]{:S(2)}) collective-permute-start(bf16[1024,128]{1,0:T(8,128)(2,1)S(1)} %collective-permute-done.3.rest_2_), channel_id=1, source_target_pairs={{0,1},{1,0},{2,3},{3,2},{4,5},{5,4},{6,7},{7,6},{8,9},{9,8},{10,11... | collective-permute-start | bytes 786440 | tf_op jit(solution)/shard_map/ppermute | solution.py:318
  91.8 16.9 %copy-start.8 = (bf16[1024,512]{1,0:T(8,128)(2,1)S(1)}, bf16[1024,512]{1,0:T(8,128)(2,1)}, u32[]{:S(2)}) copy-start(bf16[1024,512]{1,0:T(8,128)(2,1)} %loads_ref.11) | copy-start | bytes 3145732
  91.9 22.6 %collective-permute-start.25 = (bf16[1024,128]{1,0:T(8,128)(2,1)S(1)}, bf16[1024,128]{1,0:T(8,128)(2,1)S(1)}, u32[]{:S(2)}, u32[]{:S(2)}) collective-permute-start(bf16[1024,128]{1,0:T(8,128)(2,1)S(1)} %add_convert_fusion.1.one_ref), channel_id=1, source_target_pairs={{4,8},{8,4},{5,9},{9,5},{6,10},{10,6},{7,11},{11,7},{20,24},{24,20... | collective-permute-start | bytes 786440 | tf_op jit(solution)/shard_map/ppermute | solution.py:338
  95.3 13.4 %collective-permute-start.31 = (bf16[1024,128]{1,0:T(8,128)(2,1)S(1)}, bf16[1024,128]{1,0:T(8,128)(2,1)S(1)}, u32[]{:S(2)}, u32[]{:S(2)}) collective-permute-start(bf16[1024,128]{1,0:T(8,128)(2,1)S(1)} %add_convert_fusion.one_ref), channel_id=1, source_target_pairs={{4,8},{8,4},{5,9},{9,5},{6,10},{10,6},{7,11},{11,7},{20,24},{24,20... | collective-permute-start | bytes 786440 | tf_op jit(solution)/shard_map/ppermute | solution.py:338
  97.9 6.0 %collective-permute-start.8 = (bf16[1024,128]{1,0:T(8,128)(2,1)S(1)}, bf16[1024,128]{1,0:T(8,128)(2,1)S(1)}, u32[]{:S(2)}, u32[]{:S(2)}) collective-permute-start(bf16[1024,128]{1,0:T(8,128)(2,1)S(1)} %collective-permute-done.7.rest_6_), channel_id=1, source_target_pairs={{0,1},{1,0},{2,3},{3,2},{4,5},{5,4},{6,7},{7,6},{8,9},{9,8},{10,11... | collective-permute-start | bytes 786440 | tf_op jit(solution)/shard_map/ppermute | solution.py:318
  98.1 26.6 %collective-permute-start.13 = (bf16[1024,128]{1,0:T(8,128)(2,1)S(1)}, bf16[1024,128]{1,0:T(8,128)(2,1)S(1)}, u32[]{:S(2)}, u32[]{:S(2)}) collective-permute-start(bf16[1024,128]{1,0:T(8,128)(2,1)S(1)} %add_convert_fusion.3.one_ref), channel_id=1, source_target_pairs={{4,8},{8,4},{5,9},{9,5},{6,10},{10,6},{7,11},{11,7},{20,24},{24,20... | collective-permute-start | bytes 786440 | tf_op jit(solution)/shard_map/ppermute | solution.py:338
  101.4 18.1 %collective-permute-start.19 = (bf16[1024,128]{1,0:T(8,128)(2,1)S(1)}, bf16[1024,128]{1,0:T(8,128)(2,1)S(1)}, u32[]{:S(2)}, u32[]{:S(2)}) collective-permute-start(bf16[1024,128]{1,0:T(8,128)(2,1)S(1)} %add_convert_fusion.2.one_ref), channel_id=1, source_target_pairs={{4,8},{8,4},{5,9},{9,5},{6,10},{10,6},{7,11},{11,7},{20,24},{24,20... | collective-permute-start | bytes 786440 | tf_op jit(solution)/shard_map/ppermute | solution.py:338
  112.4 17.3 %collective-permute-start.32 = (bf16[1024,128]{1,0:T(8,128)(2,1)}, bf16[1024,128]{1,0:T(8,128)(2,1)}, u32[]{:S(2)}, u32[]{:S(2)}) collective-permute-start(bf16[1024,128]{1,0:T(8,128)(2,1)} %root_solve.7.own_ref), channel_id=1, source_target_pairs={{4,0},{8,12},{5,1},{9,13},{6,2},{10,14},{7,3},{11,15},{20,16},{24,... | collective-permute-start | bytes 786440 | tf_op jit(solution)/shard_map/ppermute | solution.py:345
  117.5 19.4 %collective-permute-start.26 = (bf16[1024,128]{1,0:T(8,128)(2,1)S(1)}, bf16[1024,128]{1,0:T(8,128)(2,1)}, u32[]{:S(2)}, u32[]{:S(2)}) collective-permute-start(bf16[1024,128]{1,0:T(8,128)(2,1)S(1)} %root_solve.6.own_ref), channel_id=1, source_target_pairs={{4,0},{8,12},{5,1},{9,13},{6,2},{10,14},{7,3},{11,15},{20,16},{24,... | collective-permute-start | bytes 786440 | tf_op jit(solution)/shard_map/ppermute | solution.py:345
  122.5 7.2 %copy-start.7 = (bf16[4,512,512]{2,1,0:T(8,128)(2,1)S(1)}, bf16[4,512,512]{2,1,0:T(8,128)(2,1)}, u32[]{:S(2)}) copy-start(bf16[4,512,512]{2,1,0:T(8,128)(2,1)} %copy-done.6) | copy-start | bytes 6291460
  122.5 18.3 %collective-permute-start.20 = (bf16[1024,128]{1,0:T(8,128)(2,1)S(1)}, bf16[1024,128]{1,0:T(8,128)(2,1)}, u32[]{:S(2)}, u32[]{:S(2)}) collective-permute-start(bf16[1024,128]{1,0:T(8,128)(2,1)S(1)} %root_solve.5.own_ref), channel_id=1, source_target_pairs={{4,0},{8,12},{5,1},{9,13},{6,2},{10,14},{7,3},{11,15},{20,16},{24,... | collective-permute-start | bytes 786440 | tf_op jit(solution)/shard_map/ppermute | solution.py:345
  127.7 17.1 %collective-permute-start.14 = (bf16[1024,128]{1,0:T(8,128)(2,1)S(1)}, bf16[1024,128]{1,0:T(8,128)(2,1)}, u32[]{:S(2)}, u32[]{:S(2)}) collective-permute-start(bf16[1024,128]{1,0:T(8,128)(2,1)S(1)} %root_solve.4.own_ref), channel_id=1, source_target_pairs={{4,0},{8,12},{5,1},{9,13},{6,2},{10,14},{7,3},{11,15},{20,16},{24,... | collective-permute-start | bytes 786440 | tf_op jit(solution)/shard_map/ppermute | solution.py:345
  133.0 4.0 %copy-start.16 = (bf16[2048,128]{1,0:T(8,128)(2,1)S(1)}, bf16[2048,128]{1,0:T(8,128)(2,1)}, u32[]{:S(2)}) copy-start(bf16[2048,128]{1,0:T(8,128)(2,1)} %copy-done.15) | copy-start | bytes 1572868
  136.9 3.9 %copy-start.14 = (bf16[2048,128]{1,0:T(8,128)(2,1)S(1)}, bf16[2048,128]{1,0:T(8,128)(2,1)}, u32[]{:S(2)}) copy-start(bf16[2048,128]{1,0:T(8,128)(2,1)} %copy-done.13) | copy-start | bytes 1572868
  140.9 3.9 %copy-start.12 = (bf16[2048,128]{1,0:T(8,128)(2,1)S(1)}, bf16[2048,128]{1,0:T(8,128)(2,1)}, u32[]{:S(2)}) copy-start(bf16[2048,128]{1,0:T(8,128)(2,1)} %copy-done.11) | copy-start | bytes 1572868
  (19 other events, 21.0 us)

commit v2 on v1

v2 whole, which is shorter than its diff:
```python
import functools

import jax
import jax.numpy as jnp
from jax import lax
from jax.experimental import pallas as pl
from jax.experimental.pallas import tpu as pltpu
from jax.sharding import PartitionSpec as P

BF = jnp.bfloat16
F32 = jnp.float32
LANES = 128
GROUP = 2
SHARE = 1.0
VMEM_LIMIT = 24 * 1024 * 1024
NT = (((1,), (1,)), ((), ()))


def dot(a, b):
    return jnp.dot(a, b, preferred_element_type=F32)


def dot_nt(a, b):
    return lax.dot_general(a, b, NT, preferred_element_type=F32)


def any_spec():
    return pl.BlockSpec(memory_space=pl.ANY)


def vmem_spec():
    return pl.BlockSpec(memory_space=pltpu.VMEM)


def smem_spec():
    return pl.BlockSpec(memory_space=pltpu.SMEM)


def params():
    return pltpu.CompilerParams(vmem_limit_bytes=VMEM_LIMIT)


def cost(flops, moved):
    return pl.CostEstimate(flops=int(flops * SHARE), bytes_accessed=int(moved * SHARE), transcendentals=0)


def leader(level, group):
    if level == 0:
        return group
    return leader(level - 1, 2 * group + (1 if group % 2 == 0 else 0))


def tree(nodes):
    depth = nodes.bit_length() - 1
    ups = []
    for level in range(1, depth):
        pairs = []
        for group in range(nodes >> level):
            left, right = leader(level - 1, 2 * group), leader(level - 1, 2 * group + 1)
            pairs.append((left, right) if group % 2 == 0 else (right, left))
        ups.append(pairs)
    left, right = leader(depth - 1, 0), leader(depth - 1, 1)
    return ups, [(left, right), (right, left)]


def pick_kernel(nodes, firsts, widths, me_ref, rows_ref, loads_ref, *rest):
    count = len(widths)
    outs, (picked, held, sem, sems) = rest[-count * nodes - 4 : -4], rest[-4:]
    load = pltpu.make_async_copy(loads_ref.at[:, pl.ds(firsts[0], sum(widths))], picked, sem)
    load.start()
    total = loads_ref.shape[0]
    block = total // nodes
    me = me_ref[0]
    tile = 128
    load.wait()
    x = picked[...]
    for k in range(total // tile):
        row = rows_ref[k : k + 1, :]
        column = jnp.broadcast_to(row, (tile, tile)).T
        parts = []
        for j in range(total // tile):
            wanted = lax.broadcasted_iota(jnp.int32, (tile, tile), 1) + j * tile
            parts.append(jnp.where(column == wanted, 1.0, 0.0).astype(BF))
        onehot = jnp.concatenate(parts, axis=1)
        held[k * tile : (k + 1) * tile, :] = dot(onehot, x).astype(BF)
    copies = []
    for c in range(count):
        for s in range(nodes):
            start = pl.multiple_of((me ^ s) * block, block)
            source = held.at[pl.ds(start, block), pl.ds(firsts[c] - firsts[0], widths[c])]
            copies.append(pltpu.make_async_copy(source, outs[c * nodes + s], sems.at[c * nodes + s]))
            copies[-1].start()
    for copy in copies:
        copy.wait()


def pick(nodes, firsts, widths, me, rows, loads, after):
    total = loads.shape[0]
    block = total // nodes
    width, count = sum(widths), len(widths) * nodes
    return pl.pallas_call(
        functools.partial(pick_kernel, nodes, firsts, widths),
        in_specs=[smem_spec(), vmem_spec(), any_spec()] + [any_spec()] * len(after),
        out_specs=[any_spec()] * count,
        out_shape=[jax.ShapeDtypeStruct((block, size), BF) for size in widths for _ in range(nodes)],
        scratch_shapes=[pltpu.VMEM((total, width), BF)] * 2
        + [pltpu.SemaphoreType.DMA, pltpu.SemaphoreType.DMA((count,))],
        compiler_params=params(),
        cost_estimate=cost(2 * total * total * width, 4 * total * width),
        name="pick",
    )(me, rows, loads, *after)


def identity(size):
    same = lax.broadcasted_iota(jnp.int32, (size, size), 0) == lax.broadcasted_iota(jnp.int32, (size, size), 1)
    return jnp.where(same, 1.0, 0.0).astype(BF)


def prep_kernel(rows_ref, couple_ref, inv_ref, *rest):
    outs, scratch, sems = rest[-7:-4], rest[-4:-1], rest[-1]
    spread_ref, spread_t_ref, inv_t_ref = scratch
    leaves, picked, order = couple_ref.shape
    root = spread_ref.shape[0]
    copies = []
    for n in range(leaves):
        c = couple_ref[n]
        at = slice(n * order, (n + 1) * order)
        rows = rows_ref[n : n + 1, :]
        onehot = lax.broadcasted_iota(jnp.int32, (root, picked), 0) == jnp.broadcast_to(rows, (root, picked))
        onehot = jnp.where(onehot, 1.0, 0.0).astype(BF)
        spread_ref[:, at] = dot(onehot, c).astype(BF)
        spread_t_ref[at, :] = dot_nt(c.T, onehot).astype(BF)
        inv_t_ref[n] = inv_ref[n].T
        places = [(slice(None), pl.ds(n * order, order)), (pl.ds(n * order, order),), (n,)]
        for k, place in enumerate(places):
            copies.append(pltpu.make_async_copy(scratch[k].at[place], outs[k].at[place], sems.at[k, n]))
            copies[-1].start()
    for copy in copies:
        copy.wait()


def prep(rows, couple, inv, root, after):
    leaves, picked, order = couple.shape
    shapes = [(root, leaves * order), (leaves * order, root), (leaves, order, order)]
    return pl.pallas_call(
        prep_kernel,
        in_specs=[vmem_spec()] * 3 + [any_spec()] * len(after),
        out_specs=[any_spec()] * 3,
        out_shape=[jax.ShapeDtypeStruct(shape, BF) for shape in shapes],
        scratch_shapes=[pltpu.VMEM(shape, BF) for shape in shapes] + [pltpu.SemaphoreType.DMA((3, leaves))],
        compiler_params=params(),
        cost_estimate=cost(2 * leaves * picked * order * (2 * root + 2 * order), leaves * order * (4 * root + 6 * order)),
        name="prep",
    )(rows, couple, inv, *after)


def forward_kernel(nodes, chunks, me_ref, inv_ref, spread_ref, *rest):
    blocks, (out_ref, *outs), (held, fwd_ref, sem) = rest[:nodes], rest[nodes:-3], rest[-3:]
    block = blocks[0].shape[0]
    leaves, order, _ = inv_ref.shape
    half = order // 2
    me = me_ref[0]
    for s in range(nodes):
        held[pl.ds(pl.multiple_of((me ^ s) * block, block), block), :] = blocks[s][...]
    for n in range(leaves):
        at = n * order
        x = held[at : at + order, :]
        fwd_ref[at : at + half, :] = dot(inv_ref[n, :half, :half], x[:half]).astype(BF)
        fwd_ref[at + half : at + order, :] = dot(inv_ref[n, half:, :], x).astype(BF)
    copy = pltpu.make_async_copy(fwd_ref, out_ref, sem)
    copy.start()
    root = spread_ref.shape[0]
    tile = min(256, root)
    for t in range(root // tile):
        at = slice(t * tile, (t + 1) * tile)
        part = dot(spread_ref[at, :], fwd_ref[...])
        for c in range(chunks):
            piece = part[:, c * LANES : (c + 1) * LANES]
            outs[c][at, :] = piece.astype(BF)
            outs[chunks + c][at, :] = piece
    copy.wait()


def forward(nodes, me, inv, spread, blocks):
    leaves, order, _ = inv.shape
    root = spread.shape[0]
    width = blocks[0].shape[1]
    chunks = width // LANES
    return pl.pallas_call(
        functools.partial(forward_kernel, nodes, chunks),
        in_specs=[smem_spec()] + [vmem_spec()] * (2 + nodes),
        out_specs=[any_spec()] + [vmem_spec()] * (2 * chunks),
        out_shape=[jax.ShapeDtypeStruct((leaves * order, width), BF)]
        + [jax.ShapeDtypeStruct((root, LANES), BF)] * chunks
        + [jax.ShapeDtypeStruct((root, LANES), F32)] * chunks,
        scratch_shapes=[pltpu.VMEM((leaves * order, width), BF)] * 2 + [pltpu.SemaphoreType.DMA],
        compiler_params=params(),
        cost_estimate=cost(
            2 * leaves * order * width * (order + root),
            2 * leaves * order * (order + root + 3 * width) + 6 * root * width,
        ),
        name="forward",
    )(me, inv, spread, *blocks)


def piece_kernel(width, mine_ref, inv_ref, *rest):
    out_ref, sem = rest[-2:]
    start = pl.multiple_of(mine_ref[0] * width, width)
    copy = pltpu.make_async_copy(inv_ref.at[:, pl.ds(start, width)], out_ref, sem)
    copy.start()
    copy.wait()


def take_piece(mine, root_inv, count, after):
    rows, root = root_inv.shape
    width = root // count
    return pl.pallas_call(
        functools.partial(piece_kernel, width),
        in_specs=[smem_spec()] + [any_spec()] * (1 + len(after)),
        out_specs=any_spec(),
        out_shape=jax.ShapeDtypeStruct((rows, width), BF),
        scratch_shapes=[pltpu.SemaphoreType.DMA],
        compiler_params=params(),
        cost_estimate=cost(0, 4 * rows * width),
        name="piece",
    )(mine, root_inv, *after)


def gather_kernel(nodes, me_ref, *rest):
    pieces, (out_ref, sems) = rest[:nodes], rest[-2:]
    rows = pieces[0].shape[0]
    copies = []
    for s in range(nodes):
        at = pl.ds(pl.multiple_of((me_ref[0] ^ s) * rows, rows), rows)
        copies.append(pltpu.make_async_copy(pieces[s], out_ref.at[at], sems.at[s]))
        copies[-1].start()
    for copy in copies:
        copy.wait()


def gather_rows(nodes, me, pieces, after):
    rows, width = pieces[0].shape
    return pl.pallas_call(
        functools.partial(gather_kernel, nodes),
        in_specs=[smem_spec()] + [any_spec()] * (nodes + len(after)),
        out_specs=any_spec(),
        out_shape=jax.ShapeDtypeStruct((nodes * rows, width), BF),
        scratch_shapes=[pltpu.SemaphoreType.DMA((nodes,))],
        compiler_params=params(),
        cost_estimate=cost(0, 4 * nodes * rows * width),
        name="gather_rows",
    )(me, *pieces, *after)


def root_prep_kernel(places, count, mine_ref, pieces_ref, *rest):
    whole_ref, whole_t_ref = rest[-2:]
    root = whole_ref.shape[0]
    width, rows = root // count, root // len(places)
    for q in range(count):
        at = pl.ds(pl.multiple_of((mine_ref[0] ^ q) * width, width), width)
        for k, place in enumerate(places):
            start = q * root + k * rows
            whole_ref[place * rows : (place + 1) * rows, at] = pieces_ref[start : start + rows, :]
    for t in range(count):
        whole_t_ref[t * width : (t + 1) * width, :] = whole_ref[:, t * width : (t + 1) * width].T


def root_prep(mine, places, count, pieces, after):
    root = pieces.shape[1] * count
    return pl.pallas_call(
        functools.partial(root_prep_kernel, places, count),
        in_specs=[smem_spec(), vmem_spec()] + [any_spec()] * len(after),
        out_specs=[vmem_spec()] * 2,
        out_shape=[jax.ShapeDtypeStruct((root, root), BF)] * 2,
        compiler_params=params(),
        cost_estimate=cost(root * root, 6 * root * root),
        name="root_prep",
    )(mine, pieces, *after)


def root_kernel(first, whole_ref, whole_t_ref, loads_ref, one_ref, two_ref, *rest):
    out_ref, reduced, solved = rest[-3:]
    root = whole_ref.shape[0]
    tile = min(256, root)
    update = one_ref[...].astype(F32) + two_ref[...].astype(F32)
    reduced[...] = (loads_ref[:, first : first + out_ref.shape[1]].astype(F32) - update).astype(BF)
    for t in range(root // tile):
        at = slice(t * tile, (t + 1) * tile)
        solved[at, :] = dot(whole_ref[at, : (t + 1) * tile], reduced[: (t + 1) * tile, :]).astype(BF)
    for t in range(root // tile):
        at = slice(t * tile, (t + 1) * tile)
        out_ref[at, :] = dot(whole_t_ref[at, t * tile :], solved[t * tile :, :]).astype(BF)


def root_solve(first, whole, whole_t, root_loads, one, two, after):
    root, width = one.shape
    return pl.pallas_call(
        functools.partial(root_kernel, first),
        in_specs=[vmem_spec()] * 5 + [any_spec()] * len(after),
        out_specs=vmem_spec(),
        out_shape=jax.ShapeDtypeStruct((root, width), BF),
        scratch_shapes=[pltpu.VMEM((root, width), BF)] * 2,
        compiler_params=params(),
        cost_estimate=cost(4 * root * root * width, 4 * root * root + 8 * root * width),
        name="root_solve",
    )(whole, whole_t, root_loads, one, two, *after)


def backward_kernel(first, count, take_ref, fwd_ref, spread_t_ref, inv_t_ref, *rest):
    owns, gots = rest[:count], rest[count : 2 * count]
    out_ref, root_ref, held, solved, sems = rest[-5:]
    leaves, order, _ = inv_t_ref.shape
    half = order // 2
    columns = pl.ds(first, held.shape[1])
    for c in range(count):
        held[:, c * LANES : (c + 1) * LANES] = jnp.where(take_ref[0] > 0, gots[c][...], owns[c][...])
    copies = [pltpu.make_async_copy(held, root_ref.at[:, columns], sems.at[leaves])]
    copies[0].start()
    root_solution = held[...]
    for n in range(leaves):
        at = n * order
        back = dot(spread_t_ref[at : at + order, :], root_solution)
        x = (fwd_ref[at : at + order, first : first + held.shape[1]].astype(F32) - back).astype(BF)
        solved[at : at + half, :] = dot(inv_t_ref[n, :half, :], x).astype(BF)
        solved[at + half : at + order, :] = dot(inv_t_ref[n, half:, half:], x[half:]).astype(BF)
        rows = pl.ds(at, order)
        copy = pltpu.make_async_copy(solved.at[rows], out_ref.at[rows, columns], sems.at[n])
        copy.start()
        copies.append(copy)
    for copy in copies:
        copy.wait()


def backward(first, total, take, owns, gots, fwd, spread_t, inv_t, before):
    leaves, order, _ = inv_t.shape
    count = len(owns)
    root, width = spread_t.shape[1], count * LANES
    inputs = [take, fwd, spread_t, inv_t, *owns, *gots]
    aliases, extra = {}, []
    if before is not None:
        aliases = {len(inputs): 0, len(inputs) + 1: 1}
        extra = list(before)
    return pl.pallas_call(
        functools.partial(backward_kernel, first, count),
        in_specs=[smem_spec()] + [vmem_spec()] * (len(inputs) - 1) + [any_spec()] * len(extra),
        out_specs=[any_spec()] * 2,
        out_shape=[
            jax.ShapeDtypeStruct((leaves * order, total), BF),
            jax.ShapeDtypeStruct((root, total), BF),
        ],
        scratch_shapes=[
            pltpu.VMEM((root, width), BF),
            pltpu.VMEM((leaves * order, width), BF),
            pltpu.SemaphoreType.DMA((leaves + 1,)),
        ],
        input_output_aliases=aliases,
        compiler_params=params(),
        cost_estimate=cost(
            2 * leaves * order * width * (order + root),
            2 * leaves * order * (order + root + 2 * width) + 6 * root * width,
        ),
        name="backward",
    )(*inputs, *extra)


def per_device(sizes, loads, root_loads, send_rows, leaf_inv, couple, couple_rows, root_inv):
    nodes = sizes["node"]
    root, width = root_loads.shape
    total = loads.shape[0]
    chunks = width // LANES
    ups, top = tree(nodes)
    node = lax.axis_index("node")
    me = node.astype(jnp.int32).reshape(1)
    rows = send_rows.reshape(total // 128, 128)

    stages, count = [], 1
    for axis in ("rhs", "shift"):
        if count * sizes[axis] * LANES <= root:
            bits = sizes[axis].bit_length() - 1
            stages = [(axis, bit) for bit in reversed(range(bits))] + stages
            count *= sizes[axis]
    mine = jnp.int32(0)
    for place, (axis, bit) in enumerate(stages):
        mine = mine + (((lax.axis_index(axis).astype(jnp.int32) >> bit) & 1) << place)
    mine = mine.reshape(1)
    places = list(range(nodes))

    piece = take_piece(mine, root_inv, count, [])
    pieces = [piece]
    for s in range(1, nodes):
        pieces.append(lax.ppermute(piece, "node", [(i, i ^ s) for i in range(nodes) if i ^ s in top[0]]))
    sent = pick(nodes, [0], [width], me, rows, loads, [])
    piece = gather_rows(nodes, me, pieces, [sent[0]])
    for axis, bit in stages:
        pairs = [(i, i ^ (1 << bit)) for i in range(sizes[axis])]
        piece = jnp.concatenate([piece, lax.ppermute(piece, axis, pairs)], axis=0)

    blocks = [sent[0]] + [lax.ppermute(sent[s], "node", [(i, i ^ s) for i in range(nodes)]) for s in range(1, nodes)]
    spread, spread_t, inv_t = prep(couple_rows, couple, leaf_inv, root, [sent[0]])
    whole, whole_t = root_prep(mine, places, count, piece, [])
    fwd, *parts = forward(nodes, me, leaf_inv, spread, blocks)
    result, owns, gots = None, [], []
    for c in range(chunks):
        part, wide = parts[c], parts[chunks + c]
        for pairs in ups:
            wide = wide + lax.ppermute(part, "node", pairs).astype(F32)
            part = wide.astype(BF)
        other = lax.ppermute(part, "node", top)
        own = root_solve(c * LANES, whole, whole_t, root_loads, part, other, [])
        got, take = own, jnp.zeros((1,), jnp.int32)
        for level, pairs in enumerate(reversed(ups)):
            if level > 0:
                own = jnp.where(take[0] > 0, got, own)
            got = lax.ppermute(own, "node", [(b, a) for a, b in pairs])
            take = jnp.zeros((1,), jnp.int32)
            for sender, _ in pairs:
                take = take + (node == sender).astype(jnp.int32)
        owns.append(own)
        gots.append(got)
        if len(owns) == GROUP or c == chunks - 1:
            first = (c + 1 - len(owns)) * LANES
            result = backward(first, width, take, owns, gots, fwd, spread_t, inv_t, result)
            owns, gots = [], []
    return tuple(result)


def solution(mesh):
    return jax.shard_map(
        functools.partial(per_device, dict(mesh.shape)),
        mesh=mesh,
        in_specs=(
            P("node", ("shift", "rhs")),
            P(None, ("shift", "rhs")),
            P("node"),
            P("node", None, None),
            P("node", None, None),
            P("node", None),
            P("node", None),
        ),
        out_specs=(P("node", ("shift", "rhs")), P(None, ("shift", "rhs"))),
        check_vma=False,
    )
```

time: 150 us -> 131 us (0.87)
  the two profiles are of different devices: /device:TPU:12 before, /device:TPU:0 now
where the time goes in v2:
time: 131 us
  waiting for transfers between devices  49.9 us (38%)
  starting transfers between devices  39.2 us (30%)
  Pallas kernels  30.6 us (23%)
  local copies, waits for them, and re-layouts  9.08 us (7%)
    ppermute x3, waiting for transfers between devices, per_device(): lax.ppermute(sent[s], 'node', [(i, i ^ s) for i in range(nodes)])  23.4 us
    ppermute x4, starting transfers between devices, per_device(): wide = wide + lax.ppermute(part, 'node', pairs).astype(F32)  15.8 us
    ppermute x4, waiting for transfers between devices, per_device(): wide = wide + lax.ppermute(part, 'node', pairs).astype(F32)  14.1 us
    ppermute x4, waiting for transfers between devices, per_device(): got = lax.ppermute(own, 'node', [(b, a) for a, b in pairs])  10.5 us
    pallas_call x2, Pallas kernels, backward(): pl.pallas_call(functools.partial(backward_kernel, first, count), in_specs...  10.3 us
    unnamed x22, local copies, waits for them, and re-layouts  9.08 us
    ppermute x3, starting transfers between devices, per_device(): lax.ppermute(piece, 'node', [(i, i ^ s) for i in range(nodes) if i ^ s in...  7.9 us
    pallas_call x1, Pallas kernels, prep(): pl.pallas_call(prep_kernel, in_specs=[vmem_spec()] * 3 + [any_spec()] * l...  6.18 us
  transfers between devices with their start and end apart: 21, of which 10 were waited for; matrix products, arithmetic and copies ran while one was open for 0% of the time, Pallas kernels for 19%

profile of v2, /device:TPU:0, one launch (start us, length us, event | category | flops | bytes accessed | tf_op | source)
XLA Modules:
  0.0 130.6 jit_solution(15886636217313493028)
XLA Ops:
  0.6 1.0 copy-done.5
  1.7 4.9 %collective-permute-start.3 = (bf16[256,128]{1,0:T(8,128)(2,1)S(1)}, bf16[256,128]{1,0:T(8,128)(2,1)S(1)}, u32[]{:S(2)}, u32[]{:S(2)}) collective-permute-start(bf16[256,128]{1,0:T(8,128)(2,1)S(1)} %piece.1.rest_0_), channel_id=1, source_target_pairs={{0,4},{12,8},{1,5},{13,9},{2,6},{14,10},{3,7},{15,11},{16,20},{28,... | collective-permute-start | bytes 196616 | tf_op jit(solution)/shard_map/ppermute | solution.py:391
  6.7 2.3 %collective-permute-start.4 = (bf16[256,128]{1,0:T(8,128)(2,1)S(1)}, bf16[256,128]{1,0:T(8,128)(2,1)S(1)}, u32[]{:S(2)}, u32[]{:S(2)}) collective-permute-start(bf16[256,128]{1,0:T(8,128)(2,1)S(1)} %piece.1.rest_0_), channel_id=1, source_target_pairs={{0,8},{12,4},{1,9},{13,5},{2,10},{14,6},{3,11},{15,7},{16,24},{28,... | collective-permute-start | bytes 196616 | tf_op jit(solution)/shard_map/ppermute | solution.py:391
  9.0 0.7 collective-permute-start.5
  9.7 1.6 %copy-done.6 = bf16[2048,512]{1,0:T(8,128)(2,1)S(1)} copy-done((bf16[2048,512]{1,0:T(8,128)(2,1)S(1)}, bf16[2048,512]{1,0:T(8,128)(2,1)}, u32[]{:S(2)}) %copy-start.6) | copy-done | bytes 2097176
  11.2 0.7 copy-done.9
  11.9 4.9 %pick.1 = (bf16[512,512]{1,0:T(8,128)(2,1)S(1)}, bf16[512,512]{1,0:T(8,128)(2,1)S(1)}, bf16[512,512]{1,0:T(8,128)(2,1)S(1)}, bf16[512,512]{1,0:T(8,128)(2,1)S(1)}) custom-call(s32[1]{0:T(128)} %bitcast.1.me_ref, s32[16,128]{1,0:T(8,128)S(1)} %bitcast.4, bf16[2048,512]{1,0:T(8,128)(2,1)S(1)} %copy-done.6), custom_call_target="tpu_custom_call" | custom-call | flops 4294967296 | bytes 4194304 | tf_op jit(solution)/shard_map/pick/pallas_call | solution.py:101
  16.9 0.4 gather_rows.1
  17.3 1.6 %collective-permute-start.6 = (bf16[1024,128]{1,0:T(8,128)(2,1)S(1)}, bf16[1024,128]{1,0:T(8,128)(2,1)S(1)}, u32[]{:S(2)}, u32[]{:S(2)}) collective-permute-start(bf16[1024,128]{1,0:T(8,128)(2,1)S(1)} %gather_rows.1), channel_id=1, source_target_pairs={{0,16},{16,0},{1,17},{17,1},{2,18},{18,2},{3,19},{19,3},{4,20},{20... | collective-permute-start | bytes 786440 | tf_op jit(solution)/shard_map/ppermute | solution.py:396
  18.9 1.2 collective-permute-start
  20.1 0.8 collective-permute-start.1
  20.9 2.4 %collective-permute-start.2 = (bf16[512,512]{1,0:T(8,128)(2,1)S(1)}, bf16[512,512]{1,0:T(8,128)(2,1)S(1)}, u32[]{:S(2)}, u32[]{:S(2)}) collective-permute-start(bf16[512,512]{1,0:T(8,128)(2,1)S(1)} %get-tuple-element.26), channel_id=1, source_target_pairs={{0,12},{4,8},{8,4},{12,0},{1,13},{5,9},{9,5},{13,1},{2,14},{6,10},... | collective-permute-start | bytes 1572872 | tf_op jit(solution)/shard_map/ppermute | solution.py:398
  23.3 1.9 %collective-permute-done.6 = bf16[1024,128]{1,0:T(8,128)(2,1)S(1)} collective-permute-done((bf16[1024,128]{1,0:T(8,128)(2,1)S(1)}, bf16[1024,128]{1,0:T(8,128)(2,1)S(1)}, u32[]{:S(2)}, u32[]{:S(2)}) %collective-permute-start.6) | collective-permute-done | bytes 262176 | tf_op jit(solution)/shard_map/ppermute | solution.py:396
  25.2 1.6 %collective-permute-start.7 = (bf16[2048,128]{1,0:T(8,128)(2,1)S(1)}, bf16[2048,128]{1,0:T(8,128)(2,1)S(1)}, u32[]{:S(2)}, u32[]{:S(2)}) collective-permute-start(bf16[2048,128]{1,0:T(8,128)(2,1)S(1)} %pad_maximum_fusion.2), channel_id=1, source_target_pairs={{0,2},{1,3},{2,0},{3,1},{4,6},{5,7},{6,4},{7,5},{8,10},{9,11},{10,... | collective-permute-start | bytes 1572872 | tf_op jit(solution)/shard_map/ppermute | solution.py:396
  26.7 6.2 %prep.1 = (bf16[1024,2048]{1,0:T(8,128)(2,1)S(1)}, bf16[2048,1024]{1,0:T(8,128)(2,1)S(1)}, bf16[4,512,512]{2,1,0:T(8,128)(2,1)S(1)}) custom-call(s32[4,512]{1,0:T(4,128)S(1)} %copy-done.10, bf16[4,512,512]{2,1,0:T(8,128)(2,1)S(1)} %copy-done.7, bf16[4,512,512]{2,1,0:T(8,128)(2,1)S(1)} %copy-done.8, bf16[512,512]{1,0:T(8,128)(2,1)S(1)} %get-tuple-element.22.rest_0_.rest_4_), custom_call_target="tpu_custom_call" | custom-call | flops 6442450944 | bytes 14680064 | tf_op jit(solution)/shard_map/prep/pallas_call | solution.py:145
  32.9 2.0 %copy-done = bf16[2048,1024]{1,0:T(8,128)(2,1)} copy-done((bf16[2048,1024]{1,0:T(8,128)(2,1)}, bf16[2048,1024]{1,0:T(8,128)(2,1)S(1)}, u32[]{:S(2)}) %copy-start) | copy-done | bytes 4194328
  34.9 6.7 %collective-permute-done.rest_1_ = bf16[512,512]{1,0:T(8,128)(2,1)S(1)} collective-permute-done((bf16[512,512]{1,0:T(8,128)(2,1)S(1)}, bf16[512,512]{1,0:T(8,128)(2,1)S(1)}, u32[]{:S(2)}, u32[]{:S(2)}) %collective-permute-start) | collective-permute-done | bytes 524320 | tf_op jit(solution)/shard_map/ppermute | solution.py:398
  41.6 16.7 %collective-permute-done.1.rest_2_ = bf16[512,512]{1,0:T(8,128)(2,1)S(1)} collective-permute-done((bf16[512,512]{1,0:T(8,128)(2,1)S(1)}, bf16[512,512]{1,0:T(8,128)(2,1)S(1)}, u32[]{:S(2)}, u32[]{:S(2)}) %collective-permute-start.1) | collective-permute-done | bytes 524320 | tf_op jit(solution)/shard_map/ppermute | solution.py:398
  58.3 3.7 %forward.1 = (bf16[2048,512]{1,0:T(8,128)(2,1)S(1)}, bf16[1024,128]{1,0:T(8,128)(2,1)S(1)}, bf16[1024,128]{1,0:T(8,128)(2,1)S(1)}, bf16[1024,128]{1,0:T(8,128)(2...) custom-call(s32[1]{0:T(128)} %bitcast.1.me_ref, ...), custom_call_target="tpu_custom_call" | custom-call | flops 3221225472 | bytes 15728640 | tf_op jit(solution)/shard_map/forward/pallas_call | solution.py:189
  62.1 11.9 %collective-permute-start.9 = (bf16[1024,128]{1,0:T(8,128)(2,1)S(1)}, bf16[1024,128]{1,0:T(8,128)(2,1)S(1)}, u32[]{:S(2)}, u32[]{:S(2)}) collective-permute-start(bf16[1024,128]{1,0:T(8,128)(2,1)S(1)} %get-tuple-element.33), channel_id=1, source_target_pairs={{0,4},{12,8},{1,5},{13,9},{2,6},{14,10},{3,7},{15,11},{16,20},{28,... | collective-permute-start | bytes 786440 | tf_op jit(solution)/shard_map/ppermute | solution.py:406
  74.2 1.3 %collective-permute-start.11 = (bf16[1024,128]{1,0:T(8,128)(2,1)S(1)}, bf16[1024,128]{1,0:T(8,128)(2,1)S(1)}, u32[]{:S(2)}, u32[]{:S(2)}) collective-permute-start(bf16[1024,128]{1,0:T(8,128)(2,1)S(1)} %get-tuple-element.35), channel_id=1, source_target_pairs={{0,4},{12,8},{1,5},{13,9},{2,6},{14,10},{3,7},{15,11},{16,20},{28,... | collective-permute-start | bytes 786440 | tf_op jit(solution)/shard_map/ppermute | solution.py:406
  75.5 1.3 collective-permute-start.15
  76.8 1.3 collective-permute-start.17
  78.1 0.9 collective-permute-done.9
  79.0 0.7 collective-permute-start.10
  79.7 4.9 %collective-permute-done.11 = bf16[1024,128]{1,0:T(8,128)(2,1)S(1)} collective-permute-done((bf16[1024,128]{1,0:T(8,128)(2,1)S(1)}, bf16[1024,128]{1,0:T(8,128)(2,1)S(1)}, u32[]{:S(2)}, u32[]{:S(2)}) %collective-permute-start.11) | collective-permute-done | bytes 262176 | tf_op jit(solution)/shard_map/ppermute | solution.py:406
  84.7 0.7 collective-permute-start.12
  85.3 4.8 %collective-permute-done.15 = bf16[1024,128]{1,0:T(8,128)(2,1)S(1)} collective-permute-done((bf16[1024,128]{1,0:T(8,128)(2,1)S(1)}, bf16[1024,128]{1,0:T(8,128)(2,1)S(1)}, u32[]{:S(2)}, u32[]{:S(2)}) %collective-permute-start.15) | collective-permute-done | bytes 262176 | tf_op jit(solution)/shard_map/ppermute | solution.py:406
  90.3 0.7 collective-permute-start.16
  91.0 3.6 %collective-permute-done.17 = bf16[1024,128]{1,0:T(8,128)(2,1)S(1)} collective-permute-done((bf16[1024,128]{1,0:T(8,128)(2,1)S(1)}, bf16[1024,128]{1,0:T(8,128)(2,1)S(1)}, u32[]{:S(2)}, u32[]{:S(2)}) %collective-permute-start.17) | collective-permute-done | bytes 262176 | tf_op jit(solution)/shard_map/ppermute | solution.py:406
  94.6 0.7 collective-permute-start.18
  95.3 0.1 pad_maximum_fusion.pieces_ref
  95.5 1.2 root_prep.1
  96.7 1.0 root_solve.6.rest_0_
  97.7 1.3 collective-permute-start.19
  99.0 1.0 root_solve.7.rest_1_
  100.0 1.3 collective-permute-start.20
  101.3 1.0 root_solve.4.rest_0_
  102.3 1.3 collective-permute-start.13
  103.6 1.0 root_solve.5.rest_1_
  104.5 1.3 collective-permute-start.14
  105.9 2.3 %collective-permute-done.19.rest_2_ = bf16[1024,128]{1,0:T(8,128)(2,1)S(1)} collective-permute-done((bf16[1024,128]{1,0:T(8,128)(2,1)S(1)}, bf16[1024,128]{1,0:T(8,128)(2,1)S(1)}, u32[]{:S(2)}, u32[]{:S(2)}) %collective-permute-start.19) | collective-permute-done | bytes 262176 | tf_op jit(solution)/shard_map/ppermute | solution.py:414
  108.2 8.0 %collective-permute-done.20.rest_3_ = bf16[1024,128]{1,0:T(8,128)(2,1)} collective-permute-done((bf16[1024,128]{1,0:T(8,128)(2,1)S(1)}, bf16[1024,128]{1,0:T(8,128)(2,1)}, u32[]{:S(2)}, u32[]{:S(2)}) %collective-permute-start.20) | collective-permute-done | bytes 262176 | tf_op jit(solution)/shard_map/ppermute | solution.py:414
  116.2 2.2 %copy-done.1 = bf16[2048,1024]{1,0:T(8,128)(2,1)S(1)} copy-done((bf16[2048,1024]{1,0:T(8,128)(2,1)S(1)}, bf16[2048,1024]{1,0:T(8,128)(2,1)}, u32[]{:S(2)}) %copy-start.1) | copy-done | bytes 4194328
  118.4 1.6 %copy-done.4 = bf16[2048,512]{1,0:T(8,128)(2,1)S(1)} copy-done((bf16[2048,512]{1,0:T(8,128)(2,1)S(1)}, bf16[2048,512]{1,0:T(8,128)(2,1)}, u32[]{:S(2)}) %copy-start.4) | copy-done | bytes 2097176
  120.0 5.1 %backward.2 = (bf16[2048,512]{1,0:T(8,128)(2,1)}, bf16[1024,512]{1,0:T(8,128)(2,1)}) custom-call(s32[1]{0:T(128)} %bitcast.take_ref, bf16[2048,512]{1,0:T(8,128)(2,1)S(1)} %copy-done.4, bf16[2048,1024]{1,0:T(8,128)(2,1)S(1)} %copy-done.1, bf16[4,512,512]{2,1,0:T(8,128)(2,1)S(1)} %get-tuple-element.29.inv_t_ref, bf16[1024,128]{1,0:T(8,128)(2,1)S(1)} %root_solve.6.rest_0_, ...), custom_call_target="tpu_custom_call" | custom-call | flops 1610612736 | bytes 9961472 | tf_op jit(solution)/shard_map/backward/pallas_call | solution.py:343
  125.1 0.1 collective-permute-done.14.rest_3_
  125.2 5.2 %backward.3 = (bf16[2048,512]{1,0:T(8,128)(2,1)}, bf16[1024,512]{1,0:T(8,128)(2,1)}) custom-call(s32[1]{0:T(128)} %bitcast.take_ref, bf16[2048,512]{1,0:T(8,128)(2,1)S(1)} %copy-done.4, bf16[2048,1024]{1,0:T(8,128)(2,1)S(1)} %copy-done.1, bf16[4,512,512]{2,1,0:T(8,128)(2,1)S(1)} %get-tuple-element.29.inv_t_ref, ...), custom_call_target="tpu_custom_call", output_to_operand_aliasing={{0}: (8, {}), {1}: (9, {})} | custom-call | flops 1610612736 | bytes 9961472 | tf_op jit(solution)/shard_map/backward/pallas_call | solution.py:343
  (35 shorter events, 0.6 us)
Async XLA Ops:
  0.6 1.0 copy-start.5
  1.7 15.1 %collective-permute-start.3 = (bf16[256,128]{1,0:T(8,128)(2,1)S(1)}, bf16[256,128]{1,0:T(8,128)(2,1)S(1)}, u32[]{:S(2)}, u32[]{:S(2)}) collective-permute-start(bf16[256,128]{1,0:T(8,128)(2,1)S(1)} %piece.1.rest_0_), channel_id=1, source_target_pairs={{0,4},{12,8},{1,5},{13,9},{2,6},{14,10},{3,7},{15,11},{16,20},{28,... | collective-permute-start | bytes 196616 | tf_op jit(solution)/shard_map/ppermute | solution.py:391
  6.7 10.2 %collective-permute-start.4 = (bf16[256,128]{1,0:T(8,128)(2,1)S(1)}, bf16[256,128]{1,0:T(8,128)(2,1)S(1)}, u32[]{:S(2)}, u32[]{:S(2)}) collective-permute-start(bf16[256,128]{1,0:T(8,128)(2,1)S(1)} %piece.1.rest_0_), channel_id=1, source_target_pairs={{0,8},{12,4},{1,9},{13,5},{2,10},{14,6},{3,11},{15,7},{16,24},{28,... | collective-permute-start | bytes 196616 | tf_op jit(solution)/shard_map/ppermute | solution.py:391
  9.0 7.9 %collective-permute-start.5 = (bf16[256,128]{1,0:T(8,128)(2,1)S(1)}, bf16[256,128]{1,0:T(8,128)(2,1)S(1)}, u32[]{:S(2)}, u32[]{:S(2)}) collective-permute-start(bf16[256,128]{1,0:T(8,128)(2,1)S(1)} %piece.1.rest_0_), channel_id=1, source_target_pairs={{4,8},{8,4},{5,9},{9,5},{6,10},{10,6},{7,11},{11,7},{20,24},{24,20... | collective-permute-start | bytes 196616 | tf_op jit(solution)/shard_map/ppermute | solution.py:391
  9.6 1.6 %copy-start.6 = (bf16[2048,512]{1,0:T(8,128)(2,1)S(1)}, bf16[2048,512]{1,0:T(8,128)(2,1)}, u32[]{:S(2)}) copy-start(bf16[2048,512]{1,0:T(8,128)(2,1)} %loads_ref.5) | copy-start | bytes 6291460
  11.2 0.7 copy-start.9
  11.9 14.8 %copy-start.8 = (bf16[4,512,512]{2,1,0:T(8,128)(2,1)S(1)}, bf16[4,512,512]{2,1,0:T(8,128)(2,1)}, u32[]{:S(2)}) copy-start(bf16[4,512,512]{2,1,0:T(8,128)(2,1)} %inv_ref.4) | copy-start | bytes 6291460
  16.8 9.9 %copy-start.7 = (bf16[4,512,512]{2,1,0:T(8,128)(2,1)S(1)}, bf16[4,512,512]{2,1,0:T(8,128)(2,1)}, u32[]{:S(2)}) copy-start(bf16[4,512,512]{2,1,0:T(8,128)(2,1)} %couple_ref.1) | copy-start | bytes 6291460
  16.8 9.9 %copy-start.10 = (s32[4,512]{1,0:T(4,128)S(1)}, s32[4,512]{1,0:T(4,128)}, u32[]{:S(2)}) copy-start(s32[4,512]{1,0:T(4,128)} %rows_ref.1) | copy-start | bytes 24580
  17.3 7.8 %collective-permute-start.6 = (bf16[1024,128]{1,0:T(8,128)(2,1)S(1)}, bf16[1024,128]{1,0:T(8,128)(2,1)S(1)}, u32[]{:S(2)}, u32[]{:S(2)}) collective-permute-start(bf16[1024,128]{1,0:T(8,128)(2,1)S(1)} %gather_rows.1), channel_id=1, source_target_pairs={{0,16},{16,0},{1,17},{17,1},{2,18},{18,2},{3,19},{19,3},{4,20},{20... | collective-permute-start | bytes 786440 | tf_op jit(solution)/shard_map/ppermute | solution.py:396
  18.9 22.7 %collective-permute-start = (bf16[512,512]{1,0:T(8,128)(2,1)S(1)}, bf16[512,512]{1,0:T(8,128)(2,1)S(1)}, u32[]{:S(2)}, u32[]{:S(2)}) collective-permute-start(bf16[512,512]{1,0:T(8,128)(2,1)S(1)} %get-tuple-element.24), channel_id=1, source_target_pairs={{0,4},{4,0},{8,12},{12,8},{1,5},{5,1},{9,13},{13,9},{2,6},{6,2},{1... | collective-permute-start | bytes 1572872 | tf_op jit(solution)/shard_map/ppermute | solution.py:398
  20.1 38.2 %collective-permute-start.1 = (bf16[512,512]{1,0:T(8,128)(2,1)S(1)}, bf16[512,512]{1,0:T(8,128)(2,1)S(1)}, u32[]{:S(2)}, u32[]{:S(2)}) collective-permute-start(bf16[512,512]{1,0:T(8,128)(2,1)S(1)} %get-tuple-element.25), channel_id=1, source_target_pairs={{0,8},{4,12},{8,0},{12,4},{1,9},{5,13},{9,1},{13,5},{2,10},{6,14},... | collective-permute-start | bytes 1572872 | tf_op jit(solution)/shard_map/ppermute | solution.py:398
  20.9 37.4 %collective-permute-start.2 = (bf16[512,512]{1,0:T(8,128)(2,1)S(1)}, bf16[512,512]{1,0:T(8,128)(2,1)S(1)}, u32[]{:S(2)}, u32[]{:S(2)}) collective-permute-start(bf16[512,512]{1,0:T(8,128)(2,1)S(1)} %get-tuple-element.26), channel_id=1, source_target_pairs={{0,12},{4,8},{8,4},{12,0},{1,13},{5,9},{9,5},{13,1},{2,14},{6,10},... | collective-permute-start | bytes 1572872 | tf_op jit(solution)/shard_map/ppermute | solution.py:398
  25.2 48.8 %collective-permute-start.7 = (bf16[2048,128]{1,0:T(8,128)(2,1)S(1)}, bf16[2048,128]{1,0:T(8,128)(2,1)S(1)}, u32[]{:S(2)}, u32[]{:S(2)}) collective-permute-start(bf16[2048,128]{1,0:T(8,128)(2,1)S(1)} %pad_maximum_fusion.2), channel_id=1, source_target_pairs={{0,2},{1,3},{2,0},{3,1},{4,6},{5,7},{6,4},{7,5},{8,10},{9,11},{10,... | collective-permute-start | bytes 1572872 | tf_op jit(solution)/shard_map/ppermute | solution.py:396
  32.9 2.0 %copy-start = (bf16[2048,1024]{1,0:T(8,128)(2,1)}, bf16[2048,1024]{1,0:T(8,128)(2,1)S(1)}, u32[]{:S(2)}) copy-start(bf16[2048,1024]{1,0:T(8,128)(2,1)S(1)} %get-tuple-element.28.spread_t_ref) | copy-start | bytes 12582916
  62.1 22.6 %copy-start.3 = (bf16[2048,512]{1,0:T(8,128)(2,1)}, bf16[2048,512]{1,0:T(8,128)(2,1)S(1)}, u32[]{:S(2)}) copy-start(bf16[2048,512]{1,0:T(8,128)(2,1)S(1)} %get-tuple-element.27.fwd_ref) | copy-start | bytes 6291460
  62.1 16.9 %collective-permute-start.9 = (bf16[1024,128]{1,0:T(8,128)(2,1)S(1)}, bf16[1024,128]{1,0:T(8,128)(2,1)S(1)}, u32[]{:S(2)}, u32[]{:S(2)}) collective-permute-start(bf16[1024,128]{1,0:T(8,128)(2,1)S(1)} %get-tuple-element.33), channel_id=1, source_target_pairs={{0,4},{12,8},{1,5},{13,9},{2,6},{14,10},{3,7},{15,11},{16,20},{28,... | collective-permute-start | bytes 786440 | tf_op jit(solution)/shard_map/ppermute | solution.py:406
  74.1 21.2 %collective-permute-start.8 = (bf16[4096,128]{1,0:T(8,128)(2,1)S(1)}, bf16[4096,128]{1,0:T(8,128)(2,1)S(1)}, u32[]{:S(2)}, u32[]{:S(2)}) collective-permute-start(bf16[4096,128]{1,0:T(8,128)(2,1)S(1)} %pad_maximum_fusion.1), channel_id=1, source_target_pairs={{0,1},{1,0},{2,3},{3,2},{4,5},{5,4},{6,7},{7,6},{8,9},{9,8},{10,11... | collective-permute-start | bytes 3145736 | tf_op jit(solution)/shard_map/ppermute | solution.py:396
  74.2 10.4 %collective-permute-start.11 = (bf16[1024,128]{1,0:T(8,128)(2,1)S(1)}, bf16[1024,128]{1,0:T(8,128)(2,1)S(1)}, u32[]{:S(2)}, u32[]{:S(2)}) collective-permute-start(bf16[1024,128]{1,0:T(8,128)(2,1)S(1)} %get-tuple-element.35), channel_id=1, source_target_pairs={{0,4},{12,8},{1,5},{13,9},{2,6},{14,10},{3,7},{15,11},{16,20},{28,... | collective-permute-start | bytes 786440 | tf_op jit(solution)/shard_map/ppermute | solution.py:406
  75.5 14.7 %collective-permute-start.15 = (bf16[1024,128]{1,0:T(8,128)(2,1)S(1)}, bf16[1024,128]{1,0:T(8,128)(2,1)S(1)}, u32[]{:S(2)}, u32[]{:S(2)}) collective-permute-start(bf16[1024,128]{1,0:T(8,128)(2,1)S(1)} %get-tuple-element.37), channel_id=1, source_target_pairs={{0,4},{12,8},{1,5},{13,9},{2,6},{14,10},{3,7},{15,11},{16,20},{28,... | collective-permute-start | bytes 786440 | tf_op jit(solution)/shard_map/ppermute | solution.py:406
  76.8 17.7 %collective-permute-start.17 = (bf16[1024,128]{1,0:T(8,128)(2,1)S(1)}, bf16[1024,128]{1,0:T(8,128)(2,1)S(1)}, u32[]{:S(2)}, u32[]{:S(2)}) collective-permute-start(bf16[1024,128]{1,0:T(8,128)(2,1)S(1)} %get-tuple-element.39), channel_id=1, source_target_pairs={{0,4},{12,8},{1,5},{13,9},{2,6},{14,10},{3,7},{15,11},{16,20},{28,... | collective-permute-start | bytes 786440 | tf_op jit(solution)/shard_map/ppermute | solution.py:406
  79.0 22.3 %collective-permute-start.10 = (bf16[1024,128]{1,0:T(8,128)(2,1)S(1)}, bf16[1024,128]{1,0:T(8,128)(2,1)S(1)}, u32[]{:S(2)}, u32[]{:S(2)}) collective-permute-start(bf16[1024,128]{1,0:T(8,128)(2,1)S(1)} %add_convert_fusion.3.one_ref), channel_id=1, source_target_pairs={{4,8},{8,4},{5,9},{9,5},{6,10},{10,6},{7,11},{11,7},{20,24},{24,20... | collective-permute-start | bytes 786440 | tf_op jit(solution)/shard_map/ppermute | solution.py:408
  84.7 18.9 %collective-permute-start.12 = (bf16[1024,128]{1,0:T(8,128)(2,1)S(1)}, bf16[1024,128]{1,0:T(8,128)(2,1)S(1)}, u32[]{:S(2)}, u32[]{:S(2)}) collective-permute-start(bf16[1024,128]{1,0:T(8,128)(2,1)S(1)} %add_convert_fusion.2.one_ref), channel_id=1, source_target_pairs={{4,8},{8,4},{5,9},{9,5},{6,10},{10,6},{7,11},{11,7},{20,24},{24,20... | collective-permute-start | bytes 786440 | tf_op jit(solution)/shard_map/ppermute | solution.py:408
  90.3 6.4 %collective-permute-start.16 = (bf16[1024,128]{1,0:T(8,128)(2,1)S(1)}, bf16[1024,128]{1,0:T(8,128)(2,1)S(1)}, u32[]{:S(2)}, u32[]{:S(2)}) collective-permute-start(bf16[1024,128]{1,0:T(8,128)(2,1)S(1)} %add_convert_fusion.1.one_ref), channel_id=1, source_target_pairs={{4,8},{8,4},{5,9},{9,5},{6,10},{10,6},{7,11},{11,7},{20,24},{24,20... | collective-permute-start | bytes 786440 | tf_op jit(solution)/shard_map/ppermute | solution.py:408
  94.6 4.4 %collective-permute-start.18 = (bf16[1024,128]{1,0:T(8,128)(2,1)S(1)}, bf16[1024,128]{1,0:T(8,128)(2,1)S(1)}, u32[]{:S(2)}, u32[]{:S(2)}) collective-permute-start(bf16[1024,128]{1,0:T(8,128)(2,1)S(1)} %add_convert_fusion.one_ref), channel_id=1, source_target_pairs={{4,8},{8,4},{5,9},{9,5},{6,10},{10,6},{7,11},{11,7},{20,24},{24,20... | collective-permute-start | bytes 786440 | tf_op jit(solution)/shard_map/ppermute | solution.py:408
  95.4 1.3 copy-start.2
  97.7 10.5 %collective-permute-start.19 = (bf16[1024,128]{1,0:T(8,128)(2,1)S(1)}, bf16[1024,128]{1,0:T(8,128)(2,1)S(1)}, u32[]{:S(2)}, u32[]{:S(2)}) collective-permute-start(bf16[1024,128]{1,0:T(8,128)(2,1)S(1)} %root_solve.6.rest_0_), channel_id=1, source_target_pairs={{4,0},{8,12},{5,1},{9,13},{6,2},{10,14},{7,3},{11,15},{20,16},{24,... | collective-permute-start | bytes 786440 | tf_op jit(solution)/shard_map/ppermute | solution.py:414
  100.0 16.3 %collective-permute-start.20 = (bf16[1024,128]{1,0:T(8,128)(2,1)S(1)}, bf16[1024,128]{1,0:T(8,128)(2,1)}, u32[]{:S(2)}, u32[]{:S(2)}) collective-permute-start(bf16[1024,128]{1,0:T(8,128)(2,1)S(1)} %root_solve.7.rest_1_), channel_id=1, source_target_pairs={{4,0},{8,12},{5,1},{9,13},{6,2},{10,14},{7,3},{11,15},{20,16},{24,... | collective-permute-start | bytes 786440 | tf_op jit(solution)/shard_map/ppermute | solution.py:414
  102.3 22.9 %collective-permute-start.13 = (bf16[1024,128]{1,0:T(8,128)(2,1)S(1)}, bf16[1024,128]{1,0:T(8,128)(2,1)}, u32[]{:S(2)}, u32[]{:S(2)}) collective-permute-start(bf16[1024,128]{1,0:T(8,128)(2,1)S(1)} %root_solve.4.rest_0_), channel_id=1, source_target_pairs={{4,0},{8,12},{5,1},{9,13},{6,2},{10,14},{7,3},{11,15},{20,16},{24,... | collective-permute-start | bytes 786440 | tf_op jit(solution)/shard_map/ppermute | solution.py:414
  104.5 20.7 %collective-permute-start.14 = (bf16[1024,128]{1,0:T(8,128)(2,1)S(1)}, bf16[1024,128]{1,0:T(8,128)(2,1)}, u32[]{:S(2)}, u32[]{:S(2)}) collective-permute-start(bf16[1024,128]{1,0:T(8,128)(2,1)S(1)} %root_solve.5.rest_1_), channel_id=1, source_target_pairs={{4,0},{8,12},{5,1},{9,13},{6,2},{10,14},{7,3},{11,15},{20,16},{24,... | collective-permute-start | bytes 786440 | tf_op jit(solution)/shard_map/ppermute | solution.py:414
  116.2 2.2 %copy-start.1 = (bf16[2048,1024]{1,0:T(8,128)(2,1)S(1)}, bf16[2048,1024]{1,0:T(8,128)(2,1)}, u32[]{:S(2)}) copy-start(bf16[2048,1024]{1,0:T(8,128)(2,1)} %copy-done) | copy-start | bytes 12582916
  118.4 1.6 %copy-start.4 = (bf16[2048,512]{1,0:T(8,128)(2,1)S(1)}, bf16[2048,512]{1,0:T(8,128)(2,1)}, u32[]{:S(2)}) copy-start(bf16[2048,512]{1,0:T(8,128)(2,1)} %copy-done.3) | copy-start | bytes 6291460

commit v3 on v2

--- a/solution.py
+++ b/solution.py
@@ -196,8 +196,8 @@
         scratch_shapes=[pltpu.VMEM((leaves * order, width), BF)] * 2 + [pltpu.SemaphoreType.DMA],
         compiler_params=params(),
         cost_estimate=cost(
-            2 * leaves * order * width * (order + root),
-            2 * leaves * order * (order + root + 3 * width) + 6 * root * width,
+            40 * leaves * order * width * (order + root),
+            40 * leaves * order * (order + root + 3 * width) + 6 * root * width,
         ),
         name="forward",
     )(me, inv, spread, *blocks)
@@ -320,7 +320,7 @@
     for n in range(leaves):
         at = n * order
         back = dot(spread_t_ref[at : at + order, :], root_solution)
-        x = (fwd_ref[at : at + order, first : first + held.shape[1]].astype(F32) - back).astype(BF)
+        x = (fwd_ref[at : at + order, :].astype(F32) - back).astype(BF)
         solved[at : at + half, :] = dot(inv_t_ref[n, :half, :], x).astype(BF)
         solved[at + half : at + order, :] = dot(inv_t_ref[n, half:, half:], x[half:]).astype(BF)
         rows = pl.ds(at, order)
@@ -367,7 +367,6 @@
     nodes = sizes["node"]
     root, width = root_loads.shape
     total = loads.shape[0]
-    chunks = width // LANES
     ups, top = tree(nodes)
     node = lax.axis_index("node")
     me = node.astype(jnp.int32).reshape(1)
@@ -385,42 +384,48 @@
     mine = mine.reshape(1)
     places = list(range(nodes))
 
-    piece = take_piece(mine, root_inv, count, [])
+    sizes_of = [min(GROUP * LANES, width - first) for first in range(0, width, GROUP * LANES)]
+    firsts = [sum(sizes_of[:g]) for g in range(len(sizes_of))]
+    sent = pick(nodes, firsts, sizes_of, me, rows, loads, [])
+    piece = take_piece(mine, root_inv, count, [sent[0]])
     pieces = [piece]
     for s in range(1, nodes):
         pieces.append(lax.ppermute(piece, "node", [(i, i ^ s) for i in range(nodes) if i ^ s in top[0]]))
-    sent = pick(nodes, [0], [width], me, rows, loads, [])
     piece = gather_rows(nodes, me, pieces, [sent[0]])
     for axis, bit in stages:
         pairs = [(i, i ^ (1 << bit)) for i in range(sizes[axis])]
         piece = jnp.concatenate([piece, lax.ppermute(piece, axis, pairs)], axis=0)
 
-    blocks = [sent[0]] + [lax.ppermute(sent[s], "node", [(i, i ^ s) for i in range(nodes)]) for s in range(1, nodes)]
+    blocks = []
+    for g in range(len(sizes_of)):
+        own = sent[g * nodes : (g + 1) * nodes]
+        pairs = [[(i, i ^ s) for i in range(nodes)] for s in range(nodes)]
+        blocks.append([own[0]] + [lax.ppermute(own[s], "node", pairs[s]) for s in range(1, nodes)])
     spread, spread_t, inv_t = prep(couple_rows, couple, leaf_inv, root, [sent[0]])
     whole, whole_t = root_prep(mine, places, count, piece, [])
-    fwd, *parts = forward(nodes, me, leaf_inv, spread, blocks)
-    result, owns, gots = None, [], []
-    for c in range(chunks):
-        part, wide = parts[c], parts[chunks + c]
-        for pairs in ups:
-            wide = wide + lax.ppermute(part, "node", pairs).astype(F32)
-            part = wide.astype(BF)
-        other = lax.ppermute(part, "node", top)
-        own = root_solve(c * LANES, whole, whole_t, root_loads, part, other, [])
-        got, take = own, jnp.zeros((1,), jnp.int32)
-        for level, pairs in enumerate(reversed(ups)):
-            if level > 0:
-                own = jnp.where(take[0] > 0, got, own)
-            got = lax.ppermute(own, "node", [(b, a) for a, b in pairs])
-            take = jnp.zeros((1,), jnp.int32)
-            for sender, _ in pairs:
-                take = take + (node == sender).astype(jnp.int32)
-        owns.append(own)
-        gots.append(got)
-        if len(owns) == GROUP or c == chunks - 1:
-            first = (c + 1 - len(owns)) * LANES
-            result = backward(first, width, take, owns, gots, fwd, spread_t, inv_t, result)
-            owns, gots = [], []
+    result = None
+    for g in range(len(sizes_of)):
+        fwd, *parts = forward(nodes, me, leaf_inv, spread, blocks[g])
+        owns, gots = [], []
+        chunks = sizes_of[g] // LANES
+        for c in range(chunks):
+            part, wide = parts[c], parts[chunks + c]
+            for pairs in ups:
+                wide = wide + lax.ppermute(part, "node", pairs).astype(F32)
+                part = wide.astype(BF)
+            other = lax.ppermute(part, "node", top)
+            own = root_solve(firsts[g] + c * LANES, whole, whole_t, root_loads, part, other, [])
+            got, take = own, jnp.zeros((1,), jnp.int32)
+            for level, pairs in enumerate(reversed(ups)):
+                if level > 0:
+                    own = jnp.where(take[0] > 0, got, own)
+                got = lax.ppermute(own, "node", [(b, a) for a, b in pairs])
+                take = jnp.zeros((1,), jnp.int32)
+                for sender, _ in pairs:
+                    take = take + (node == sender).astype(jnp.int32)
+            owns.append(own)
+            gots.append(got)
+        result = backward(firsts[g], width, take, owns, gots, fwd, spread_t, inv_t, result)
     return tuple(result)
 
 

time: 131 us -> 122 us (0.931)
  waiting for transfers between devices: 49.9 us -> 24.7 us
  starting transfers between devices: 39.2 us -> 54.3 us
  Pallas kernels: 30.6 us -> 33.4 us
  local copies, waits for them, and re-layouts: 9.08 us -> 7.69 us
    ppermute x3 -> x6, waiting for transfers between devices: 23.4 us -> 3.64 us  [per_device(): lax.ppermute(own[s], 'node', pairs[s])]
    ppermute x4, starting transfers between devices: 15.8 us -> 26.5 us  [per_device(): wide = wide + lax.ppermute(part, 'node', pairs).astype(F32)]
    ppermute x4, waiting for transfers between devices: 14.1 us -> 6.23 us  [per_device(): wide = wide + lax.ppermute(part, 'node', pairs).astype(F32)]
    ppermute x3 -> x6, starting transfers between devices: 4.39 us -> 8.9 us  [per_device(): lax.ppermute(own[s], 'node', pairs[s])]
    ppermute x4, waiting for transfers between devices: 10.5 us -> 14.8 us  [per_device(): got = lax.ppermute(own, 'node', [(b, a) for a, b in pairs])]
    pallas_call x4, Pallas kernels: 3.89 us -> 6.01 us  [root_solve(): pl.pallas_call(functools.partial(root_kernel, first), in_specs=[vmem_spec...]
    ppermute x3, waiting for transfers between devices: 1.86 us -> 0.01 us  [per_device(): piece = jnp.concatenate([piece, lax.ppermute(piece, axis, pairs)], axis=0)]
    unnamed x22, local copies, waits for them, and re-layouts: 9.08 us -> 7.69 us
  transfers between devices with their start and end apart: 21 -> 24, of which waited for: 10 -> 6; matrix products, arithmetic and copies ran while one was open for 0% -> 0% of each run, Pallas kernels for 19% -> 19%
where the time goes in v3:
time: 122 us
  starting transfers between devices  54.3 us (45%)
  Pallas kernels  33.4 us (27%)
  waiting for transfers between devices  24.7 us (20%)
  local copies, waits for them, and re-layouts  7.69 us (6%)
  between operations  1.22 us (1%)
    ppermute x4, starting transfers between devices, per_device(): wide = wide + lax.ppermute(part, 'node', pairs).astype(F32)  26.5 us
    ppermute x4, waiting for transfers between devices, per_device(): got = lax.ppermute(own, 'node', [(b, a) for a, b in pairs])  14.8 us
    pallas_call x2, Pallas kernels, backward(): pl.pallas_call(functools.partial(backward_kernel, first, count), in_specs...  10.6 us
    ppermute x6, starting transfers between devices, per_device(): lax.ppermute(own[s], 'node', pairs[s])  8.9 us
    ppermute x3, starting transfers between devices, per_device(): lax.ppermute(piece, 'node', [(i, i ^ s) for i in range(nodes) if i ^ s in...  7.91 us
    unnamed x22, local copies, waits for them, and re-layouts  7.69 us
    ppermute x4, waiting for transfers between devices, per_device(): wide = wide + lax.ppermute(part, 'node', pairs).astype(F32)  6.23 us
    pallas_call x1, Pallas kernels, prep(): pl.pallas_call(prep_kernel, in_specs=[vmem_spec()] * 3 + [any_spec()] * l...  6.14 us
  transfers between devices with their start and end apart: 24, of which 6 were waited for; matrix products, arithmetic and copies ran while one was open for 0% of the time, Pallas kernels for 19%

profile of v3, /device:TPU:0, one launch (start us, length us, event | category | flops | bytes accessed | tf_op | source)
XLA Modules:
  0.0 121.7 jit_solution(4251734935099892262)
XLA Ops:
  0.7 1.6 %copy-done.6 = bf16[2048,512]{1,0:T(8,128)(2,1)S(1)} copy-done((bf16[2048,512]{1,0:T(8,128)(2,1)S(1)}, bf16[2048,512]{1,0:T(8,128)(2,1)}, u32[]{:S(2)}) %copy-start.6) | copy-done | bytes 2097176
  2.2 0.7 copy-done.9
  2.9 4.9 %pick.1 = (bf16[512,256]{1,0:T(8,128)(2,1)S(1)}, bf16[512,256]{1,0:T(8,128)(2,1)S(1)}, bf16[512,256]{1,0:T(8,128)(2,1)S(1)}, bf16[512,256]{1,0:T(8,128)(2,1)S(1)...) custom-call(s32[1]{0:T(128)} %bitcast.1.me_ref, ...), custom_call_target="tpu_custom_call" | custom-call | flops 4294967296 | bytes 4194304 | tf_op jit(solution)/shard_map/pick/pallas_call | solution.py:101
  7.9 4.9 %collective-permute-start.3 = (bf16[256,128]{1,0:T(8,128)(2,1)S(1)}, bf16[256,128]{1,0:T(8,128)(2,1)S(1)}, u32[]{:S(2)}, u32[]{:S(2)}) collective-permute-start(bf16[256,128]{1,0:T(8,128)(2,1)S(1)} %piece.1.rest_0_), channel_id=1, source_target_pairs={{0,4},{12,8},{1,5},{13,9},{2,6},{14,10},{3,7},{15,11},{16,20},{28,... | collective-permute-start | bytes 196616 | tf_op jit(solution)/shard_map/ppermute | solution.py:393
  12.9 2.3 %collective-permute-start.4 = (bf16[256,128]{1,0:T(8,128)(2,1)S(1)}, bf16[256,128]{1,0:T(8,128)(2,1)S(1)}, u32[]{:S(2)}, u32[]{:S(2)}) collective-permute-start(bf16[256,128]{1,0:T(8,128)(2,1)S(1)} %piece.1.rest_0_), channel_id=1, source_target_pairs={{0,8},{12,4},{1,9},{13,5},{2,10},{14,6},{3,11},{15,7},{16,24},{28,... | collective-permute-start | bytes 196616 | tf_op jit(solution)/shard_map/ppermute | solution.py:393
  15.2 0.7 collective-permute-start.5
  15.9 1.3 %collective-permute-start = (bf16[512,256]{1,0:T(8,128)(2,1)S(1)}, bf16[512,256]{1,0:T(8,128)(2,1)S(1)}, u32[]{:S(2)}, u32[]{:S(2)}) collective-permute-start(bf16[512,256]{1,0:T(8,128)(2,1)S(1)} %get-tuple-element.30), channel_id=1, source_target_pairs={{0,4},{4,0},{8,12},{12,8},{1,5},{5,1},{9,13},{13,9},{2,6},{6,2},{1... | collective-permute-start | bytes 786440 | tf_op jit(solution)/shard_map/ppermute | solution.py:403
  17.1 0.8 collective-permute-start.1
  18.0 2.4 %collective-permute-start.2 = (bf16[512,256]{1,0:T(8,128)(2,1)S(1)}, bf16[512,256]{1,0:T(8,128)(2,1)S(1)}, u32[]{:S(2)}, u32[]{:S(2)}) collective-permute-start(bf16[512,256]{1,0:T(8,128)(2,1)S(1)} %get-tuple-element.32), channel_id=1, source_target_pairs={{0,12},{4,8},{8,4},{12,0},{1,13},{5,9},{9,5},{13,1},{2,14},{6,10},... | collective-permute-start | bytes 786440 | tf_op jit(solution)/shard_map/ppermute | solution.py:403
  20.3 0.3 collective-permute-start.15
  20.6 0.4 gather_rows.1
  21.0 1.6 %collective-permute-start.6 = (bf16[1024,128]{1,0:T(8,128)(2,1)S(1)}, bf16[1024,128]{1,0:T(8,128)(2,1)S(1)}, u32[]{:S(2)}, u32[]{:S(2)}) collective-permute-start(bf16[1024,128]{1,0:T(8,128)(2,1)S(1)} %gather_rows.1), channel_id=1, source_target_pairs={{0,16},{16,0},{1,17},{17,1},{2,18},{18,2},{3,19},{19,3},{4,20},{20... | collective-permute-start | bytes 786440 | tf_op jit(solution)/shard_map/ppermute | solution.py:397
  22.6 6.1 %prep.1 = (bf16[1024,2048]{1,0:T(8,128)(2,1)S(1)}, bf16[2048,1024]{1,0:T(8,128)(2,1)S(1)}, bf16[4,512,512]{2,1,0:T(8,128)(2,1)S(1)}) custom-call(s32[4,512]{1,0:T(4,128)S(1)} %copy-done.10, bf16[4,512,512]{2,1,0:T(8,128)(2,1)S(1)} %copy-done.7, bf16[4,512,512]{2,1,0:T(8,128)(2,1)S(1)} %copy-done.8, bf16[512,256]{1,0:T(8,128)(2,1)S(1)} %get-tuple-element.27.rest_0_.rest_4_), custom_call_target="tpu_custom_call" | custom-call | flops 6442450944 | bytes 14680064 | tf_op jit(solution)/shard_map/prep/pallas_call | solution.py:145
  28.8 2.0 %copy-done = bf16[2048,1024]{1,0:T(8,128)(2,1)} copy-done((bf16[2048,1024]{1,0:T(8,128)(2,1)}, bf16[2048,1024]{1,0:T(8,128)(2,1)S(1)}, u32[]{:S(2)}) %copy-start) | copy-done | bytes 4194328
  30.7 1.7 %collective-permute-start.16 = (bf16[512,256]{1,0:T(8,128)(2,1)S(1)}, bf16[512,256]{1,0:T(8,128)(2,1)S(1)}, u32[]{:S(2)}, u32[]{:S(2)}) collective-permute-start(bf16[512,256]{1,0:T(8,128)(2,1)S(1)} %get-tuple-element.43), channel_id=1, source_target_pairs={{0,8},{4,12},{8,0},{12,4},{1,9},{5,13},{9,1},{13,5},{2,10},{6,14},... | collective-permute-start | bytes 786440 | tf_op jit(solution)/shard_map/ppermute | solution.py:403
  32.5 2.4 %collective-permute-start.17 = (bf16[512,256]{1,0:T(8,128)(2,1)S(1)}, bf16[512,256]{1,0:T(8,128)(2,1)S(1)}, u32[]{:S(2)}, u32[]{:S(2)}) collective-permute-start(bf16[512,256]{1,0:T(8,128)(2,1)S(1)} %get-tuple-element.44), channel_id=1, source_target_pairs={{0,12},{4,8},{8,4},{12,0},{1,13},{5,9},{9,5},{13,1},{2,14},{6,10},... | collective-permute-start | bytes 786440 | tf_op jit(solution)/shard_map/ppermute | solution.py:403
  34.9 3.6 %collective-permute-done.1.rest_2_ = bf16[512,256]{1,0:T(8,128)(2,1)S(1)} collective-permute-done((bf16[512,256]{1,0:T(8,128)(2,1)S(1)}, bf16[512,256]{1,0:T(8,128)(2,1)S(1)}, u32[]{:S(2)}, u32[]{:S(2)}) %collective-permute-start.1) | collective-permute-done | bytes 262176 | tf_op jit(solution)/shard_map/ppermute | solution.py:403
  38.6 1.5 %collective-permute-start.7 = (bf16[2048,128]{1,0:T(8,128)(2,1)S(1)}, bf16[2048,128]{1,0:T(8,128)(2,1)S(1)}, u32[]{:S(2)}, u32[]{:S(2)}) collective-permute-start(bf16[2048,128]{1,0:T(8,128)(2,1)S(1)} %pad_maximum_fusion.2), channel_id=1, source_target_pairs={{0,2},{1,3},{2,0},{3,1},{4,6},{5,7},{6,4},{7,5},{8,10},{9,11},{10,... | collective-permute-start | bytes 1572872 | tf_op jit(solution)/shard_map/ppermute | solution.py:397
  40.0 2.0 %forward.2 = (bf16[2048,256]{1,0:T(8,128)(2,1)S(1)}, bf16[1024,128]{1,0:T(8,128)(2,1)S(1)}, bf16[1024,128]{1,0:T(8,128)(2,1)S(1)}, f32[1024,128]{1,0:T(8,128)S(1)}, f32[1024,128]{1,0:T(8,128)S(1)}) custom-call(s32[1]{0:T(128)} %bitcast.1.me_ref, bf16[4,512,512]{2,1,0:T(8,128)(2,1)S(1)} %copy-done.8, bf16[1024,2048]{1,0:T(8,128)(2,1)S(1)} %get-tuple-element.28.spread_ref, ...), custom_call_target="tpu_custom_call" | custom-call | flops 32212254720 | bytes 190316544 | tf_op jit(solution)/shard_map/forward/pallas_call | solution.py:189
  42.1 17.9 %collective-permute-start.9 = (bf16[1024,128]{1,0:T(8,128)(2,1)S(1)}, bf16[1024,128]{1,0:T(8,128)(2,1)S(1)}, u32[]{:S(2)}, u32[]{:S(2)}) collective-permute-start(bf16[1024,128]{1,0:T(8,128)(2,1)S(1)} %get-tuple-element.39), channel_id=1, source_target_pairs={{0,4},{12,8},{1,5},{13,9},{2,6},{14,10},{3,7},{15,11},{16,20},{28,... | collective-permute-start | bytes 786440 | tf_op jit(solution)/shard_map/ppermute | solution.py:414
  59.9 1.5 %collective-permute-start.11 = (bf16[1024,128]{1,0:T(8,128)(2,1)S(1)}, bf16[1024,128]{1,0:T(8,128)(2,1)S(1)}, u32[]{:S(2)}, u32[]{:S(2)}) collective-permute-start(bf16[1024,128]{1,0:T(8,128)(2,1)S(1)} %get-tuple-element.41), channel_id=1, source_target_pairs={{0,4},{12,8},{1,5},{13,9},{2,6},{14,10},{3,7},{15,11},{16,20},{28,... | collective-permute-start | bytes 786440 | tf_op jit(solution)/shard_map/ppermute | solution.py:414
  61.5 0.1 collective-permute-start.8
  61.6 2.0 %forward.3 = (bf16[2048,256]{1,0:T(8,128)(2,1)S(1)}, bf16[1024,128]{1,0:T(8,128)(2,1)S(1)}, bf16[1024,128]{1,0:T(8,128)(2,1)S(1)}, f32[1024,128]{1,0:T(8,128)S(1)}, f32[1024,128]{1,0:T(8,128)S(1)}) custom-call(s32[1]{0:T(128)} %bitcast.1.me_ref, bf16[4,512,512]{2,1,0:T(8,128)(2,1)S(1)} %copy-done.8, bf16[1024,2048]{1,0:T(8,128)(2,1)S(1)} %get-tuple-element.28.spread_ref, ...), custom_call_target="tpu_custom_call" | custom-call | flops 32212254720 | bytes 190316544 | tf_op jit(solution)/shard_map/forward/pallas_call | solution.py:189
  63.7 5.9 %collective-permute-start.18 = (bf16[1024,128]{1,0:T(8,128)(2,1)S(1)}, bf16[1024,128]{1,0:T(8,128)(2,1)S(1)}, u32[]{:S(2)}, u32[]{:S(2)}) collective-permute-start(bf16[1024,128]{1,0:T(8,128)(2,1)S(1)} %get-tuple-element.47), channel_id=1, source_target_pairs={{0,4},{12,8},{1,5},{13,9},{2,6},{14,10},{3,7},{15,11},{16,20},{28,... | collective-permute-start | bytes 786440 | tf_op jit(solution)/shard_map/ppermute | solution.py:414
  69.6 1.3 %collective-permute-start.20 = (bf16[1024,128]{1,0:T(8,128)(2,1)S(1)}, bf16[1024,128]{1,0:T(8,128)(2,1)S(1)}, u32[]{:S(2)}, u32[]{:S(2)}) collective-permute-start(bf16[1024,128]{1,0:T(8,128)(2,1)S(1)} %get-tuple-element.49), channel_id=1, source_target_pairs={{0,4},{12,8},{1,5},{13,9},{2,6},{14,10},{3,7},{15,11},{16,20},{28,... | collective-permute-start | bytes 786440 | tf_op jit(solution)/shard_map/ppermute | solution.py:414
  71.0 0.7 collective-permute-start.10
  71.7 0.7 collective-permute-start.12
  72.4 3.9 %collective-permute-done.18 = bf16[1024,128]{1,0:T(8,128)(2,1)S(1)} collective-permute-done((bf16[1024,128]{1,0:T(8,128)(2,1)S(1)}, bf16[1024,128]{1,0:T(8,128)(2,1)S(1)}, u32[]{:S(2)}, u32[]{:S(2)}) %collective-permute-start.18) | collective-permute-done | bytes 262176 | tf_op jit(solution)/shard_map/ppermute | solution.py:414
  76.3 0.7 collective-permute-start.19
  77.0 2.3 %collective-permute-done.20 = bf16[1024,128]{1,0:T(8,128)(2,1)S(1)} collective-permute-done((bf16[1024,128]{1,0:T(8,128)(2,1)S(1)}, bf16[1024,128]{1,0:T(8,128)(2,1)S(1)}, u32[]{:S(2)}, u32[]{:S(2)}) %collective-permute-start.20) | collective-permute-done | bytes 262176 | tf_op jit(solution)/shard_map/ppermute | solution.py:414
  79.4 0.7 collective-permute-start.21
  80.1 0.1 pad_maximum_fusion.pieces_ref
  80.3 1.2 %root_prep.1 = (bf16[1024,1024]{1,0:T(8,128)(2,1)S(1)}, bf16[1024,1024]{1,0:T(8,128)(2,1)S(1)}) custom-call(s32[1]{0:T(128)} %bitcast.3.mine_ref, bf16[8192,128]{1,0:T(8,128)(2,1)S(1)} %pad_maximum_fusion.pieces_ref), custom_call_target="tpu_custom_call" | custom-call | flops 1048576 | bytes 6291456 | tf_op jit(solution)/shard_map/root_prep/pallas_call | solution.py:270
  81.5 1.0 root_solve.6.rest_0_
  82.5 1.3 %collective-permute-start.22 = (bf16[1024,128]{1,0:T(8,128)(2,1)S(1)}, bf16[1024,128]{1,0:T(8,128)(2,1)}, u32[]{:S(2)}, u32[]{:S(2)}) collective-permute-start(bf16[1024,128]{1,0:T(8,128)(2,1)S(1)} %root_solve.6.rest_0_), channel_id=1, source_target_pairs={{4,0},{8,12},{5,1},{9,13},{6,2},{10,14},{7,3},{11,15},{20,16},{24,... | collective-permute-start | bytes 786440 | tf_op jit(solution)/shard_map/ppermute | solution.py:422
  83.8 1.7 %root_solve.7.rest_1_ = bf16[1024,128]{1,0:T(8,128)(2,1)} custom-call(bf16[1024,1024]{1,0:T(8,128)(2,1)S(1)} %get-tuple-element.36.whole_ref, bf16[1024,1024]{1,0:T(8,128)(2,1)S(1)} %get-tuple-element.37.whole_t_ref, bf16[1024,512]{1,0:T(8,128)(2,1)S(1)} %copy-done.2, bf16[1024,128]{1,0:T(8,128)(2,1)S(1)} %add_convert_fusion.one_ref, ...), custom_call_target="tpu_custom_call" | custom-call | flops 536870912 | bytes 5242880 | tf_op jit(solution)/shard_map/root_solve/pallas_call | solution.py:297
  85.5 1.3 %collective-permute-start.23 = (bf16[1024,128]{1,0:T(8,128)(2,1)}, bf16[1024,128]{1,0:T(8,128)(2,1)}, u32[]{:S(2)}, u32[]{:S(2)}) collective-permute-start(bf16[1024,128]{1,0:T(8,128)(2,1)} %root_solve.7.rest_1_), channel_id=1, source_target_pairs={{4,0},{8,12},{5,1},{9,13},{6,2},{10,14},{7,3},{11,15},{20,16},{24,... | collective-permute-start | bytes 786440 | tf_op jit(solution)/shard_map/ppermute | solution.py:422
  86.8 1.7 %root_solve.4.rest_0_ = bf16[1024,128]{1,0:T(8,128)(2,1)} custom-call(bf16[1024,1024]{1,0:T(8,128)(2,1)S(1)} %get-tuple-element.36.whole_ref, bf16[1024,1024]{1,0:T(8,128)(2,1)S(1)} %get-tuple-element.37.whole_t_ref, bf16[1024,512]{1,0:T(8,128)(2,1)S(1)} %copy-done.2, bf16[1024,128]{1,0:T(8,128)(2,1)S(1)} %add_convert_fusion.3.one_ref, ...), custom_call_target="tpu_custom_call" | custom-call | flops 536870912 | bytes 5242880 | tf_op jit(solution)/shard_map/root_solve/pallas_call | solution.py:297
  88.5 1.3 %collective-permute-start.13 = (bf16[1024,128]{1,0:T(8,128)(2,1)}, bf16[1024,128]{1,0:T(8,128)(2,1)}, u32[]{:S(2)}, u32[]{:S(2)}) collective-permute-start(bf16[1024,128]{1,0:T(8,128)(2,1)} %root_solve.4.rest_0_), channel_id=1, source_target_pairs={{4,0},{8,12},{5,1},{9,13},{6,2},{10,14},{7,3},{11,15},{20,16},{24,... | collective-permute-start | bytes 786440 | tf_op jit(solution)/shard_map/ppermute | solution.py:422
  89.8 1.7 %root_solve.5.rest_1_ = bf16[1024,128]{1,0:T(8,128)(2,1)} custom-call(bf16[1024,1024]{1,0:T(8,128)(2,1)S(1)} %get-tuple-element.36.whole_ref, bf16[1024,1024]{1,0:T(8,128)(2,1)S(1)} %get-tuple-element.37.whole_t_ref, bf16[1024,512]{1,0:T(8,128)(2,1)S(1)} %copy-done.2, bf16[1024,128]{1,0:T(8,128)(2,1)S(1)} %add_convert_fusion.2.one_ref, ...), custom_call_target="tpu_custom_call" | custom-call | flops 536870912 | bytes 5242880 | tf_op jit(solution)/shard_map/root_solve/pallas_call | solution.py:297
  91.5 1.3 %collective-permute-start.14 = (bf16[1024,128]{1,0:T(8,128)(2,1)}, bf16[1024,128]{1,0:T(8,128)(2,1)}, u32[]{:S(2)}, u32[]{:S(2)}) collective-permute-start(bf16[1024,128]{1,0:T(8,128)(2,1)} %root_solve.5.rest_1_), channel_id=1, source_target_pairs={{4,0},{8,12},{5,1},{9,13},{6,2},{10,14},{7,3},{11,15},{20,16},{24,... | collective-permute-start | bytes 786440 | tf_op jit(solution)/shard_map/ppermute | solution.py:422
  92.8 7.7 %collective-permute-done.22.rest_2_ = bf16[1024,128]{1,0:T(8,128)(2,1)} collective-permute-done((bf16[1024,128]{1,0:T(8,128)(2,1)S(1)}, bf16[1024,128]{1,0:T(8,128)(2,1)}, u32[]{:S(2)}, u32[]{:S(2)}) %collective-permute-start.22) | collective-permute-done | bytes 262176 | tf_op jit(solution)/shard_map/ppermute | solution.py:422
  100.5 6.2 %collective-permute-done.23.rest_3_ = bf16[1024,128]{1,0:T(8,128)(2,1)} collective-permute-done((bf16[1024,128]{1,0:T(8,128)(2,1)}, bf16[1024,128]{1,0:T(8,128)(2,1)}, u32[]{:S(2)}, u32[]{:S(2)}) %collective-permute-start.23) | collective-permute-done | bytes 262176 | tf_op jit(solution)/shard_map/ppermute | solution.py:422
  106.6 2.2 %copy-done.1 = bf16[2048,1024]{1,0:T(8,128)(2,1)S(1)} copy-done((bf16[2048,1024]{1,0:T(8,128)(2,1)S(1)}, bf16[2048,1024]{1,0:T(8,128)(2,1)}, u32[]{:S(2)}) %copy-start.1) | copy-done | bytes 4194328
  108.8 1.2 %copy-done.4 = bf16[2048,256]{1,0:T(8,128)(2,1)S(1)} copy-done((bf16[2048,256]{1,0:T(8,128)(2,1)S(1)}, bf16[2048,256]{1,0:T(8,128)(2,1)}, u32[]{:S(2)}) %copy-start.4) | copy-done | bytes 1048600
  110.0 5.3 %backward.2 = (bf16[2048,512]{1,0:T(8,128)(2,1)}, bf16[1024,512]{1,0:T(8,128)(2,1)}) custom-call(s32[1]{0:T(128)} %bitcast.take_ref, bf16[2048,256]{1,0:T(8,128)(2,1)S(1)} %copy-done.4, bf16[2048,1024]{1,0:T(8,128)(2,1)S(1)} %copy-done.1, bf16[4,512,512]{2,1,0:T(8,128)(2,1)S(1)} %get-tuple-element.35.inv_t_ref, bf16[1024,128]{1,0:T(8,128)(2,1)S(1)} %root_solve.6.rest_0_, ...), custom_call_target="tpu_custom_call" | custom-call | flops 1610612736 | bytes 9961472 | tf_op jit(solution)/shard_map/backward/pallas_call | solution.py:343
  115.3 0.9 collective-permute-done.14.rest_3_
  116.2 5.3 %backward.3 = (bf16[2048,512]{1,0:T(8,128)(2,1)}, bf16[1024,512]{1,0:T(8,128)(2,1)}) custom-call(s32[1]{0:T(128)} %bitcast.take_ref, bf16[2048,256]{1,0:T(8,128)(2,1)S(1)} %get-tuple-element.33.fwd_ref, bf16[2048,1024]{1,0:T(8,128)(2,1)S(1)} %copy-done.1, ...), custom_call_target="tpu_custom_call", output_to_operand_aliasing={{0}: (8, {}), {1}: (9, {})} | custom-call | flops 1610612736 | bytes 9961472 | tf_op jit(solution)/shard_map/backward/pallas_call | solution.py:343
  (42 shorter events, 0.5 us)
Async XLA Ops:
  0.6 1.6 %copy-start.6 = (bf16[2048,512]{1,0:T(8,128)(2,1)S(1)}, bf16[2048,512]{1,0:T(8,128)(2,1)}, u32[]{:S(2)}) copy-start(bf16[2048,512]{1,0:T(8,128)(2,1)} %loads_ref.5) | copy-start | bytes 6291460
  2.2 0.7 copy-start.9
  2.9 5.0 %copy-start.5 = (bf16[256,1024]{1,0:T(8,128)(2,1)S(1)}, bf16[256,1024]{1,0:T(8,128)(2,1)}, u32[]{:S(2)}) copy-start(bf16[256,1024]{1,0:T(8,128)(2,1)} %inv_ref.6) | copy-start | bytes 1572868
  2.9 19.7 %copy-start.7 = (bf16[4,512,512]{2,1,0:T(8,128)(2,1)S(1)}, bf16[4,512,512]{2,1,0:T(8,128)(2,1)}, u32[]{:S(2)}) copy-start(bf16[4,512,512]{2,1,0:T(8,128)(2,1)} %couple_ref.1) | copy-start | bytes 6291460
  2.9 19.7 %copy-start.8 = (bf16[4,512,512]{2,1,0:T(8,128)(2,1)S(1)}, bf16[4,512,512]{2,1,0:T(8,128)(2,1)}, u32[]{:S(2)}) copy-start(bf16[4,512,512]{2,1,0:T(8,128)(2,1)} %inv_ref.7) | copy-start | bytes 6291460
  2.9 19.7 %copy-start.10 = (s32[4,512]{1,0:T(4,128)S(1)}, s32[4,512]{1,0:T(4,128)}, u32[]{:S(2)}) copy-start(s32[4,512]{1,0:T(4,128)} %rows_ref.1) | copy-start | bytes 24580
  7.9 10.0 %collective-permute-start.3 = (bf16[256,128]{1,0:T(8,128)(2,1)S(1)}, bf16[256,128]{1,0:T(8,128)(2,1)S(1)}, u32[]{:S(2)}, u32[]{:S(2)}) collective-permute-start(bf16[256,128]{1,0:T(8,128)(2,1)S(1)} %piece.1.rest_0_), channel_id=1, source_target_pairs={{0,4},{12,8},{1,5},{13,9},{2,6},{14,10},{3,7},{15,11},{16,20},{28,... | collective-permute-start | bytes 196616 | tf_op jit(solution)/shard_map/ppermute | solution.py:393
  12.9 7.5 %collective-permute-start.4 = (bf16[256,128]{1,0:T(8,128)(2,1)S(1)}, bf16[256,128]{1,0:T(8,128)(2,1)S(1)}, u32[]{:S(2)}, u32[]{:S(2)}) collective-permute-start(bf16[256,128]{1,0:T(8,128)(2,1)S(1)} %piece.1.rest_0_), channel_id=1, source_target_pairs={{0,8},{12,4},{1,9},{13,5},{2,10},{14,6},{3,11},{15,7},{16,24},{28,... | collective-permute-start | bytes 196616 | tf_op jit(solution)/shard_map/ppermute | solution.py:393
  15.2 5.4 %collective-permute-start.5 = (bf16[256,128]{1,0:T(8,128)(2,1)S(1)}, bf16[256,128]{1,0:T(8,128)(2,1)S(1)}, u32[]{:S(2)}, u32[]{:S(2)}) collective-permute-start(bf16[256,128]{1,0:T(8,128)(2,1)S(1)} %piece.1.rest_0_), channel_id=1, source_target_pairs={{4,8},{8,4},{5,9},{9,5},{6,10},{10,6},{7,11},{11,7},{20,24},{24,20... | collective-permute-start | bytes 196616 | tf_op jit(solution)/shard_map/ppermute | solution.py:393
  15.9 16.6 %collective-permute-start = (bf16[512,256]{1,0:T(8,128)(2,1)S(1)}, bf16[512,256]{1,0:T(8,128)(2,1)S(1)}, u32[]{:S(2)}, u32[]{:S(2)}) collective-permute-start(bf16[512,256]{1,0:T(8,128)(2,1)S(1)} %get-tuple-element.30), channel_id=1, source_target_pairs={{0,4},{4,0},{8,12},{12,8},{1,5},{5,1},{9,13},{13,9},{2,6},{6,2},{1... | collective-permute-start | bytes 786440 | tf_op jit(solution)/shard_map/ppermute | solution.py:403
  17.1 21.4 %collective-permute-start.1 = (bf16[512,256]{1,0:T(8,128)(2,1)S(1)}, bf16[512,256]{1,0:T(8,128)(2,1)S(1)}, u32[]{:S(2)}, u32[]{:S(2)}) collective-permute-start(bf16[512,256]{1,0:T(8,128)(2,1)S(1)} %get-tuple-element.31), channel_id=1, source_target_pairs={{0,8},{4,12},{8,0},{12,4},{1,9},{5,13},{9,1},{13,5},{2,10},{6,14},... | collective-permute-start | bytes 786440 | tf_op jit(solution)/shard_map/ppermute | solution.py:403
  18.0 22.1 %collective-permute-start.2 = (bf16[512,256]{1,0:T(8,128)(2,1)S(1)}, bf16[512,256]{1,0:T(8,128)(2,1)S(1)}, u32[]{:S(2)}, u32[]{:S(2)}) collective-permute-start(bf16[512,256]{1,0:T(8,128)(2,1)S(1)} %get-tuple-element.32), channel_id=1, source_target_pairs={{0,12},{4,8},{8,4},{12,0},{1,13},{5,9},{9,5},{13,1},{2,14},{6,10},... | collective-permute-start | bytes 786440 | tf_op jit(solution)/shard_map/ppermute | solution.py:403
  20.3 41.2 %collective-permute-start.15 = (bf16[512,256]{1,0:T(8,128)(2,1)S(1)}, bf16[512,256]{1,0:T(8,128)(2,1)S(1)}, u32[]{:S(2)}, u32[]{:S(2)}) collective-permute-start(bf16[512,256]{1,0:T(8,128)(2,1)S(1)} %get-tuple-element.42), channel_id=1, source_target_pairs={{0,4},{4,0},{8,12},{12,8},{1,5},{5,1},{9,13},{13,9},{2,6},{6,2},{1... | collective-permute-start | bytes 786440 | tf_op jit(solution)/shard_map/ppermute | solution.py:403
  21.0 9.7 %collective-permute-start.6 = (bf16[1024,128]{1,0:T(8,128)(2,1)S(1)}, bf16[1024,128]{1,0:T(8,128)(2,1)S(1)}, u32[]{:S(2)}, u32[]{:S(2)}) collective-permute-start(bf16[1024,128]{1,0:T(8,128)(2,1)S(1)} %gather_rows.1), channel_id=1, source_target_pairs={{0,16},{16,0},{1,17},{17,1},{2,18},{18,2},{3,19},{19,3},{4,20},{20... | collective-permute-start | bytes 786440 | tf_op jit(solution)/shard_map/ppermute | solution.py:397
  28.7 2.0 %copy-start = (bf16[2048,1024]{1,0:T(8,128)(2,1)}, bf16[2048,1024]{1,0:T(8,128)(2,1)S(1)}, u32[]{:S(2)}) copy-start(bf16[2048,1024]{1,0:T(8,128)(2,1)S(1)} %get-tuple-element.34.spread_t_ref) | copy-start | bytes 12582916
  30.7 30.9 %collective-permute-start.16 = (bf16[512,256]{1,0:T(8,128)(2,1)S(1)}, bf16[512,256]{1,0:T(8,128)(2,1)S(1)}, u32[]{:S(2)}, u32[]{:S(2)}) collective-permute-start(bf16[512,256]{1,0:T(8,128)(2,1)S(1)} %get-tuple-element.43), channel_id=1, source_target_pairs={{0,8},{4,12},{8,0},{12,4},{1,9},{5,13},{9,1},{13,5},{2,10},{6,14},... | collective-permute-start | bytes 786440 | tf_op jit(solution)/shard_map/ppermute | solution.py:403
  32.5 29.1 %collective-permute-start.17 = (bf16[512,256]{1,0:T(8,128)(2,1)S(1)}, bf16[512,256]{1,0:T(8,128)(2,1)S(1)}, u32[]{:S(2)}, u32[]{:S(2)}) collective-permute-start(bf16[512,256]{1,0:T(8,128)(2,1)S(1)} %get-tuple-element.44), channel_id=1, source_target_pairs={{0,12},{4,8},{8,4},{12,0},{1,13},{5,9},{9,5},{13,1},{2,14},{6,10},... | collective-permute-start | bytes 786440 | tf_op jit(solution)/shard_map/ppermute | solution.py:403
  38.6 21.4 %collective-permute-start.7 = (bf16[2048,128]{1,0:T(8,128)(2,1)S(1)}, bf16[2048,128]{1,0:T(8,128)(2,1)S(1)}, u32[]{:S(2)}, u32[]{:S(2)}) collective-permute-start(bf16[2048,128]{1,0:T(8,128)(2,1)S(1)} %pad_maximum_fusion.2), channel_id=1, source_target_pairs={{0,2},{1,3},{2,0},{3,1},{4,6},{5,7},{6,4},{7,5},{8,10},{9,11},{10,... | collective-permute-start | bytes 1572872 | tf_op jit(solution)/shard_map/ppermute | solution.py:397
  42.1 28.8 %collective-permute-start.9 = (bf16[1024,128]{1,0:T(8,128)(2,1)S(1)}, bf16[1024,128]{1,0:T(8,128)(2,1)S(1)}, u32[]{:S(2)}, u32[]{:S(2)}) collective-permute-start(bf16[1024,128]{1,0:T(8,128)(2,1)S(1)} %get-tuple-element.39), channel_id=1, source_target_pairs={{0,4},{12,8},{1,5},{13,9},{2,6},{14,10},{3,7},{15,11},{16,20},{28,... | collective-permute-start | bytes 786440 | tf_op jit(solution)/shard_map/ppermute | solution.py:414
  59.9 11.7 %collective-permute-start.11 = (bf16[1024,128]{1,0:T(8,128)(2,1)S(1)}, bf16[1024,128]{1,0:T(8,128)(2,1)S(1)}, u32[]{:S(2)}, u32[]{:S(2)}) collective-permute-start(bf16[1024,128]{1,0:T(8,128)(2,1)S(1)} %get-tuple-element.41), channel_id=1, source_target_pairs={{0,4},{12,8},{1,5},{13,9},{2,6},{14,10},{3,7},{15,11},{16,20},{28,... | collective-permute-start | bytes 786440 | tf_op jit(solution)/shard_map/ppermute | solution.py:414
  61.5 18.6 %collective-permute-start.8 = (bf16[4096,128]{1,0:T(8,128)(2,1)S(1)}, bf16[4096,128]{1,0:T(8,128)(2,1)S(1)}, u32[]{:S(2)}, u32[]{:S(2)}) collective-permute-start(bf16[4096,128]{1,0:T(8,128)(2,1)S(1)} %pad_maximum_fusion.1), channel_id=1, source_target_pairs={{0,1},{1,0},{2,3},{3,2},{4,5},{5,4},{6,7},{7,6},{8,9},{9,8},{10,11... | collective-permute-start | bytes 3145736 | tf_op jit(solution)/shard_map/ppermute | solution.py:397
  63.7 15.8 %copy-start.3 = (bf16[2048,256]{1,0:T(8,128)(2,1)}, bf16[2048,256]{1,0:T(8,128)(2,1)S(1)}, u32[]{:S(2)}) copy-start(bf16[2048,256]{1,0:T(8,128)(2,1)S(1)} %get-tuple-element.45.fwd_ref) | copy-start | bytes 3145732
  63.7 12.6 %collective-permute-start.18 = (bf16[1024,128]{1,0:T(8,128)(2,1)S(1)}, bf16[1024,128]{1,0:T(8,128)(2,1)S(1)}, u32[]{:S(2)}, u32[]{:S(2)}) collective-permute-start(bf16[1024,128]{1,0:T(8,128)(2,1)S(1)} %get-tuple-element.47), channel_id=1, source_target_pairs={{0,4},{12,8},{1,5},{13,9},{2,6},{14,10},{3,7},{15,11},{16,20},{28,... | collective-permute-start | bytes 786440 | tf_op jit(solution)/shard_map/ppermute | solution.py:414
  69.6 9.8 %collective-permute-start.20 = (bf16[1024,128]{1,0:T(8,128)(2,1)S(1)}, bf16[1024,128]{1,0:T(8,128)(2,1)S(1)}, u32[]{:S(2)}, u32[]{:S(2)}) collective-permute-start(bf16[1024,128]{1,0:T(8,128)(2,1)S(1)} %get-tuple-element.49), channel_id=1, source_target_pairs={{0,4},{12,8},{1,5},{13,9},{2,6},{14,10},{3,7},{15,11},{16,20},{28,... | collective-permute-start | bytes 786440 | tf_op jit(solution)/shard_map/ppermute | solution.py:414
  71.0 15.8 %collective-permute-start.10 = (bf16[1024,128]{1,0:T(8,128)(2,1)S(1)}, bf16[1024,128]{1,0:T(8,128)(2,1)S(1)}, u32[]{:S(2)}, u32[]{:S(2)}) collective-permute-start(bf16[1024,128]{1,0:T(8,128)(2,1)S(1)} %add_convert_fusion.3.one_ref), channel_id=1, source_target_pairs={{4,8},{8,4},{5,9},{9,5},{6,10},{10,6},{7,11},{11,7},{20,24},{24,20... | collective-permute-start | bytes 786440 | tf_op jit(solution)/shard_map/ppermute | solution.py:416
  71.7 18.1 %collective-permute-start.12 = (bf16[1024,128]{1,0:T(8,128)(2,1)S(1)}, bf16[1024,128]{1,0:T(8,128)(2,1)S(1)}, u32[]{:S(2)}, u32[]{:S(2)}) collective-permute-start(bf16[1024,128]{1,0:T(8,128)(2,1)S(1)} %add_convert_fusion.2.one_ref), channel_id=1, source_target_pairs={{4,8},{8,4},{5,9},{9,5},{6,10},{10,6},{7,11},{11,7},{20,24},{24,20... | collective-permute-start | bytes 786440 | tf_op jit(solution)/shard_map/ppermute | solution.py:416
  76.3 5.2 %collective-permute-start.19 = (bf16[1024,128]{1,0:T(8,128)(2,1)S(1)}, bf16[1024,128]{1,0:T(8,128)(2,1)S(1)}, u32[]{:S(2)}, u32[]{:S(2)}) collective-permute-start(bf16[1024,128]{1,0:T(8,128)(2,1)S(1)} %add_convert_fusion.1.one_ref), channel_id=1, source_target_pairs={{4,8},{8,4},{5,9},{9,5},{6,10},{10,6},{7,11},{11,7},{20,24},{24,20... | collective-permute-start | bytes 786440 | tf_op jit(solution)/shard_map/ppermute | solution.py:416
  79.4 4.4 %collective-permute-start.21 = (bf16[1024,128]{1,0:T(8,128)(2,1)S(1)}, bf16[1024,128]{1,0:T(8,128)(2,1)S(1)}, u32[]{:S(2)}, u32[]{:S(2)}) collective-permute-start(bf16[1024,128]{1,0:T(8,128)(2,1)S(1)} %add_convert_fusion.one_ref), channel_id=1, source_target_pairs={{4,8},{8,4},{5,9},{9,5},{6,10},{10,6},{7,11},{11,7},{20,24},{24,20... | collective-permute-start | bytes 786440 | tf_op jit(solution)/shard_map/ppermute | solution.py:416
  80.3 1.3 %copy-start.2 = (bf16[1024,512]{1,0:T(8,128)(2,1)S(1)}, bf16[1024,512]{1,0:T(8,128)(2,1)}, u32[]{:S(2)}) copy-start(bf16[1024,512]{1,0:T(8,128)(2,1)} %loads_ref.9) | copy-start | bytes 3145732
  82.5 18.0 %collective-permute-start.22 = (bf16[1024,128]{1,0:T(8,128)(2,1)S(1)}, bf16[1024,128]{1,0:T(8,128)(2,1)}, u32[]{:S(2)}, u32[]{:S(2)}) collective-permute-start(bf16[1024,128]{1,0:T(8,128)(2,1)S(1)} %root_solve.6.rest_0_), channel_id=1, source_target_pairs={{4,0},{8,12},{5,1},{9,13},{6,2},{10,14},{7,3},{11,15},{20,16},{24,... | collective-permute-start | bytes 786440 | tf_op jit(solution)/shard_map/ppermute | solution.py:422
  85.5 21.1 %collective-permute-start.23 = (bf16[1024,128]{1,0:T(8,128)(2,1)}, bf16[1024,128]{1,0:T(8,128)(2,1)}, u32[]{:S(2)}, u32[]{:S(2)}) collective-permute-start(bf16[1024,128]{1,0:T(8,128)(2,1)} %root_solve.7.rest_1_), channel_id=1, source_target_pairs={{4,0},{8,12},{5,1},{9,13},{6,2},{10,14},{7,3},{11,15},{20,16},{24,... | collective-permute-start | bytes 786440 | tf_op jit(solution)/shard_map/ppermute | solution.py:422
  88.5 26.8 %collective-permute-start.13 = (bf16[1024,128]{1,0:T(8,128)(2,1)}, bf16[1024,128]{1,0:T(8,128)(2,1)}, u32[]{:S(2)}, u32[]{:S(2)}) collective-permute-start(bf16[1024,128]{1,0:T(8,128)(2,1)} %root_solve.4.rest_0_), channel_id=1, source_target_pairs={{4,0},{8,12},{5,1},{9,13},{6,2},{10,14},{7,3},{11,15},{20,16},{24,... | collective-permute-start | bytes 786440 | tf_op jit(solution)/shard_map/ppermute | solution.py:422
  91.5 24.8 %collective-permute-start.14 = (bf16[1024,128]{1,0:T(8,128)(2,1)}, bf16[1024,128]{1,0:T(8,128)(2,1)}, u32[]{:S(2)}, u32[]{:S(2)}) collective-permute-start(bf16[1024,128]{1,0:T(8,128)(2,1)} %root_solve.5.rest_1_), channel_id=1, source_target_pairs={{4,0},{8,12},{5,1},{9,13},{6,2},{10,14},{7,3},{11,15},{20,16},{24,... | collective-permute-start | bytes 786440 | tf_op jit(solution)/shard_map/ppermute | solution.py:422
  106.6 2.2 %copy-start.1 = (bf16[2048,1024]{1,0:T(8,128)(2,1)S(1)}, bf16[2048,1024]{1,0:T(8,128)(2,1)}, u32[]{:S(2)}) copy-start(bf16[2048,1024]{1,0:T(8,128)(2,1)} %copy-done) | copy-start | bytes 12582916
  108.8 1.2 %copy-start.4 = (bf16[2048,256]{1,0:T(8,128)(2,1)S(1)}, bf16[2048,256]{1,0:T(8,128)(2,1)}, u32[]{:S(2)}) copy-start(bf16[2048,256]{1,0:T(8,128)(2,1)} %copy-done.3) | copy-start | bytes 3145732

commit v4 on v3

--- a/solution.py
+++ b/solution.py
@@ -301,7 +301,7 @@
         out_shape=jax.ShapeDtypeStruct((root, width), BF),
         scratch_shapes=[pltpu.VMEM((root, width), BF)] * 2,
         compiler_params=params(),
-        cost_estimate=cost(4 * root * root * width, 4 * root * root + 8 * root * width),
+        cost_estimate=cost(60 * root * root * width, 60 * root * root + 120 * root * width),
         name="root_solve",
     )(whole, whole_t, root_loads, one, two, *after)
 
@@ -319,8 +319,11 @@
     root_solution = held[...]
     for n in range(leaves):
         at = n * order
-        back = dot(spread_t_ref[at : at + order, :], root_solution)
-        x = (fwd_ref[at : at + order, :].astype(F32) - back).astype(BF)
+        parts = []
+        for start in (at, at + half):
+            back = dot(spread_t_ref[start : start + half, :], root_solution)
+            parts.append((fwd_ref[start : start + half, :].astype(F32) - back).astype(BF))
+        x = jnp.concatenate(parts, axis=0)
         solved[at : at + half, :] = dot(inv_t_ref[n, :half, :], x).astype(BF)
         solved[at + half : at + order, :] = dot(inv_t_ref[n, half:, half:], x[half:]).astype(BF)
         rows = pl.ds(at, order)
@@ -356,7 +359,7 @@
         input_output_aliases=aliases,
         compiler_params=params(),
         cost_estimate=cost(
-            2 * leaves * order * width * (order + root),
+            20 * leaves * order * width * (order + root),
             2 * leaves * order * (order + root + 2 * width) + 6 * root * width,
         ),
         name="backward",

time: 122 us -> 121 us (level)
  starting transfers between devices: 54.3 us -> 49.7 us
  Pallas kernels: 33.4 us -> 29.4 us
  local copies, waits for them, and re-layouts: 7.69 us -> 10.8 us
  other arithmetic: 0.47 us -> 3.31 us
    ppermute x4, starting transfers between devices: 26.5 us -> 21.6 us  [per_device(): wide = wide + lax.ppermute(part, 'node', pairs).astype(F32)]
    pallas_call x2, Pallas kernels: 10.6 us -> 5.95 us  [backward(): pl.pallas_call(functools.partial(backward_kernel, first, count), in_specs...]
    ppermute x6, waiting for transfers between devices: 3.64 us -> 0.02 us  [per_device(): lax.ppermute(own[s], 'node', pairs[s])]
    unnamed x22 -> x30, local copies, waits for them, and re-layouts: 7.69 us -> 10.8 us
    concatenate x3, other arithmetic: 0.24 us -> 3.09 us  [per_device(): piece = jnp.concatenate([piece, lax.ppermute(piece, axis, pairs)], axis=0)]
    ppermute x4, waiting for transfers between devices: 6.23 us -> 8.5 us  [per_device(): wide = wide + lax.ppermute(part, 'node', pairs).astype(F32)]
    ppermute x4, waiting for transfers between devices: 14.8 us -> 17 us  [per_device(): got = lax.ppermute(own, 'node', [(b, a) for a, b in pairs])]
    pallas_call x4, Pallas kernels: 6.01 us -> 3.9 us  [root_solve(): pl.pallas_call(functools.partial(root_kernel, first), in_specs=[vmem_spec...]
  transfers between devices with their start and end apart: 24 -> 24, of which waited for: 6 -> 5; matrix products, arithmetic and copies ran while one was open for 0% -> 3% of each run, Pallas kernels for 19% -> 17%
where the time goes in v4:
time: 121 us; the launch traced here: 120 us
  starting transfers between devices  49.7 us (41%)
  Pallas kernels  29.4 us (24%)
  waiting for transfers between devices  25.5 us (21%)
  local copies, waits for them, and re-layouts  10.8 us (9%)
  other arithmetic  3.31 us (3%)
  between operations  1.24 us (1%)
    ppermute x4, starting transfers between devices, per_device(): wide = wide + lax.ppermute(part, 'node', pairs).astype(F32)  21.6 us
    ppermute x4, waiting for transfers between devices, per_device(): got = lax.ppermute(own, 'node', [(b, a) for a, b in pairs])  17 us
    unnamed x30, local copies, waits for them, and re-layouts  10.8 us
    ppermute x6, starting transfers between devices, per_device(): lax.ppermute(own[s], 'node', pairs[s])  8.91 us
    ppermute x4, waiting for transfers between devices, per_device(): wide = wide + lax.ppermute(part, 'node', pairs).astype(F32)  8.5 us
    ppermute x3, starting transfers between devices, per_device(): lax.ppermute(piece, 'node', [(i, i ^ s) for i in range(nodes) if i ^ s in...  7.91 us
    pallas_call x1, Pallas kernels, prep(): pl.pallas_call(prep_kernel, in_specs=[vmem_spec()] * 3 + [any_spec()] * l...  6.14 us
    pallas_call x2, Pallas kernels, forward(): pl.pallas_call(functools.partial(forward_kernel, nodes, chunks), in_specs...  6.07 us
  transfers between devices with their start and end apart: 24, of which 5 were waited for; matrix products, arithmetic and copies ran while one was open for 3% of the time, Pallas kernels for 17%

profile of v4, /device:TPU:0, one launch (start us, length us, event | category | flops | bytes accessed | tf_op | source)
XLA Modules:
  0.0 119.9 jit_solution(11922945660064235462)
XLA Ops:
  0.7 1.6 %copy-done.1 = bf16[2048,512]{1,0:T(8,128)(2,1)S(1)} copy-done((bf16[2048,512]{1,0:T(8,128)(2,1)S(1)}, bf16[2048,512]{1,0:T(8,128)(2,1)}, u32[]{:S(2)}) %copy-start.1) | copy-done | bytes 2097176
  2.2 0.7 copy-done.5
  2.9 5.8 %pick.1 = (bf16[512,256]{1,0:T(8,128)(2,1)S(1)}, bf16[512,256]{1,0:T(8,128)(2,1)S(1)}, bf16[512,256]{1,0:T(8,128)(2,1)S(1)}, bf16[512,256]{1,0:T(8,128)(2,1)S(1)...) custom-call(s32[1]{0:T(128)} %bitcast.1.me_ref, ...), custom_call_target="tpu_custom_call" | custom-call | flops 4294967296 | bytes 4194304 | tf_op jit(solution)/shard_map/pick/pallas_call | solution.py:101
  8.8 4.9 %collective-permute-start.3 = (bf16[256,128]{1,0:T(8,128)(2,1)S(1)}, bf16[256,128]{1,0:T(8,128)(2,1)S(1)}, u32[]{:S(2)}, u32[]{:S(2)}) collective-permute-start(bf16[256,128]{1,0:T(8,128)(2,1)S(1)} %piece.1.rest_0_), channel_id=1, source_target_pairs={{0,4},{12,8},{1,5},{13,9},{2,6},{14,10},{3,7},{15,11},{16,20},{28,... | collective-permute-start | bytes 196616 | tf_op jit(solution)/shard_map/ppermute | solution.py:396
  13.7 2.3 %collective-permute-start.4 = (bf16[256,128]{1,0:T(8,128)(2,1)S(1)}, bf16[256,128]{1,0:T(8,128)(2,1)S(1)}, u32[]{:S(2)}, u32[]{:S(2)}) collective-permute-start(bf16[256,128]{1,0:T(8,128)(2,1)S(1)} %piece.1.rest_0_), channel_id=1, source_target_pairs={{0,8},{12,4},{1,9},{13,5},{2,10},{14,6},{3,11},{15,7},{16,24},{28,... | collective-permute-start | bytes 196616 | tf_op jit(solution)/shard_map/ppermute | solution.py:396
  16.0 0.7 collective-permute-start.5
  16.7 1.3 %collective-permute-start = (bf16[512,256]{1,0:T(8,128)(2,1)}, bf16[512,256]{1,0:T(8,128)(2,1)}, u32[]{:S(2)}, u32[]{:S(2)}) collective-permute-start(bf16[512,256]{1,0:T(8,128)(2,1)} %get-tuple-element.30), channel_id=1, source_target_pairs={{0,4},{4,0},{8,12},{12,8},{1,5},{5,1},{9,13},{13,9},{2,6},{6,2},{1... | collective-permute-start | bytes 786440 | tf_op jit(solution)/shard_map/ppermute | solution.py:406
  18.0 0.8 collective-permute-start.1
  18.8 2.4 %collective-permute-start.2 = (bf16[512,256]{1,0:T(8,128)(2,1)}, bf16[512,256]{1,0:T(8,128)(2,1)}, u32[]{:S(2)}, u32[]{:S(2)}) collective-permute-start(bf16[512,256]{1,0:T(8,128)(2,1)} %get-tuple-element.32), channel_id=1, source_target_pairs={{0,12},{4,8},{8,4},{12,0},{1,13},{5,9},{9,5},{13,1},{2,14},{6,10},... | collective-permute-start | bytes 786440 | tf_op jit(solution)/shard_map/ppermute | solution.py:406
  21.8 1.6 %collective-permute-start.6 = (bf16[1024,128]{1,0:T(8,128)(2,1)S(1)}, bf16[1024,128]{1,0:T(8,128)(2,1)}, u32[]{:S(2)}, u32[]{:S(2)}) collective-permute-start(bf16[1024,128]{1,0:T(8,128)(2,1)S(1)} %gather_rows.1), channel_id=1, source_target_pairs={{0,16},{16,0},{1,17},{17,1},{2,18},{18,2},{3,19},{19,3},{4,20},{20... | collective-permute-start | bytes 786440 | tf_op jit(solution)/shard_map/ppermute | solution.py:400
  23.4 6.1 %prep.1 = (bf16[1024,2048]{1,0:T(8,128)(2,1)S(1)}, bf16[2048,1024]{1,0:T(8,128)(2,1)S(1)}, bf16[4,512,512]{2,1,0:T(8,128)(2,1)S(1)}) custom-call(s32[4,512]{1,0:T(4,128)S(1)} %copy-done.6, bf16[4,512,512]{2,1,0:T(8,128)(2,1)S(1)} %copy-done.2, bf16[4,512,512]{2,1,0:T(8,128)(2,1)S(1)} %copy-done.3, bf16[512,256]{1,0:T(8,128)(2,1)S(1)} %get-tuple-element.27.rest_0_.rest_4_), custom_call_target="tpu_custom_call" | custom-call | flops 6442450944 | bytes 14680064 | tf_op jit(solution)/shard_map/prep/pallas_call | solution.py:145
  29.6 2.0 %copy-done.7 = bf16[2048,1024]{1,0:T(8,128)(2,1)} copy-done((bf16[2048,1024]{1,0:T(8,128)(2,1)}, bf16[2048,1024]{1,0:T(8,128)(2,1)S(1)}, u32[]{:S(2)}) %copy-start.7) | copy-done | bytes 4194328
  31.5 2.0 %copy-done.9 = bf16[1024,2048]{1,0:T(8,128)(2,1)} copy-done((bf16[1024,2048]{1,0:T(8,128)(2,1)}, bf16[1024,2048]{1,0:T(8,128)(2,1)S(1)}, u32[]{:S(2)}) %copy-start.9) | copy-done | bytes 4194328
  33.6 1.3 %copy-done.11 = bf16[4,512,512]{2,1,0:T(8,128)(2,1)} copy-done((bf16[4,512,512]{2,1,0:T(8,128)(2,1)}, bf16[4,512,512]{2,1,0:T(8,128)(2,1)S(1)}, u32[]{:S(2)}) %copy-start.11) | copy-done | bytes 2097176
  34.9 1.7 %collective-permute-start.16 = (bf16[512,256]{1,0:T(8,128)(2,1)S(1)}, bf16[512,256]{1,0:T(8,128)(2,1)S(1)}, u32[]{:S(2)}, u32[]{:S(2)}) collective-permute-start(bf16[512,256]{1,0:T(8,128)(2,1)S(1)} %get-tuple-element.43), channel_id=1, source_target_pairs={{0,8},{4,12},{8,0},{12,4},{1,9},{5,13},{9,1},{13,5},{2,10},{6,14},... | collective-permute-start | bytes 786440 | tf_op jit(solution)/shard_map/ppermute | solution.py:406
  36.6 1.0 pad_maximum_fusion.2
  37.6 2.4 %collective-permute-start.17 = (bf16[512,256]{1,0:T(8,128)(2,1)S(1)}, bf16[512,256]{1,0:T(8,128)(2,1)S(1)}, u32[]{:S(2)}, u32[]{:S(2)}) collective-permute-start(bf16[512,256]{1,0:T(8,128)(2,1)S(1)} %get-tuple-element.44), channel_id=1, source_target_pairs={{0,12},{4,8},{8,4},{12,0},{1,13},{5,9},{9,5},{13,1},{2,14},{6,10},... | collective-permute-start | bytes 786440 | tf_op jit(solution)/shard_map/ppermute | solution.py:406
  40.1 1.5 %collective-permute-start.7 = (bf16[2048,128]{1,0:T(8,128)(2,1)S(1)}, bf16[2048,128]{1,0:T(8,128)(2,1)S(1)}, u32[]{:S(2)}, u32[]{:S(2)}) collective-permute-start(bf16[2048,128]{1,0:T(8,128)(2,1)S(1)} %pad_maximum_fusion.2), channel_id=1, source_target_pairs={{0,2},{1,3},{2,0},{3,1},{4,6},{5,7},{6,4},{7,5},{8,10},{9,11},{10,... | collective-permute-start | bytes 1572872 | tf_op jit(solution)/shard_map/ppermute | solution.py:400
  41.5 2.2 %copy-done.10 = bf16[1024,2048]{1,0:T(8,128)(2,1)S(1)} copy-done((bf16[1024,2048]{1,0:T(8,128)(2,1)S(1)}, bf16[1024,2048]{1,0:T(8,128)(2,1)}, u32[]{:S(2)}) %copy-start.10) | copy-done | bytes 4194328
  43.7 0.9 copy-done.14
  44.7 3.1 %forward.2 = (bf16[2048,256]{1,0:T(8,128)(2,1)S(1)}, bf16[1024,128]{1,0:T(8,128)(2,1)S(1)}, bf16[1024,128]{1,0:T(8,128)(2,1)S(1)}, f32[1024,128]{1,0:T(8,128)S(1)}, f32[1024,128]{1,0:T(8,128)S(1)}) custom-call(s32[1]{0:T(128)} %bitcast.1.me_ref, bf16[4,512,512]{2,1,0:T(8,128)(2,1)S(1)} %copy-done.3, bf16[1024,2048]{1,0:T(8,128)(2,1)S(1)} %copy-done.10, ...), custom_call_target="tpu_custom_call" | custom-call | flops 32212254720 | bytes 190316544 | tf_op jit(solution)/shard_map/forward/pallas_call | solution.py:189
  47.8 17.5 %collective-permute-start.9 = (bf16[1024,128]{1,0:T(8,128)(2,1)S(1)}, bf16[1024,128]{1,0:T(8,128)(2,1)S(1)}, u32[]{:S(2)}, u32[]{:S(2)}) collective-permute-start(bf16[1024,128]{1,0:T(8,128)(2,1)S(1)} %get-tuple-element.39), channel_id=1, source_target_pairs={{0,4},{12,8},{1,5},{13,9},{2,6},{14,10},{3,7},{15,11},{16,20},{28,... | collective-permute-start | bytes 786440 | tf_op jit(solution)/shard_map/ppermute | solution.py:417
  65.3 1.5 %collective-permute-start.11 = (bf16[1024,128]{1,0:T(8,128)(2,1)S(1)}, bf16[1024,128]{1,0:T(8,128)(2,1)S(1)}, u32[]{:S(2)}, u32[]{:S(2)}) collective-permute-start(bf16[1024,128]{1,0:T(8,128)(2,1)S(1)} %get-tuple-element.41), channel_id=1, source_target_pairs={{0,4},{12,8},{1,5},{13,9},{2,6},{14,10},{3,7},{15,11},{16,20},{28,... | collective-permute-start | bytes 786440 | tf_op jit(solution)/shard_map/ppermute | solution.py:417
  66.8 1.0 pad_maximum_fusion.1
  67.9 3.0 %forward.3 = (bf16[2048,256]{1,0:T(8,128)(2,1)S(1)}, bf16[1024,128]{1,0:T(8,128)(2,1)S(1)}, bf16[1024,128]{1,0:T(8,128)(2,1)S(1)}, f32[1024,128]{1,0:T(8,128)S(1)}, f32[1024,128]{1,0:T(8,128)S(1)}) custom-call(s32[1]{0:T(128)} %bitcast.1.me_ref, bf16[4,512,512]{2,1,0:T(8,128)(2,1)S(1)} %copy-done.3, bf16[1024,2048]{1,0:T(8,128)(2,1)S(1)} %copy-done.10, ...), custom_call_target="tpu_custom_call" | custom-call | flops 32212254720 | bytes 190316544 | tf_op jit(solution)/shard_map/forward/pallas_call | solution.py:189
  70.9 1.3 %collective-permute-start.18 = (bf16[1024,128]{1,0:T(8,128)(2,1)S(1)}, bf16[1024,128]{1,0:T(8,128)(2,1)S(1)}, u32[]{:S(2)}, u32[]{:S(2)}) collective-permute-start(bf16[1024,128]{1,0:T(8,128)(2,1)S(1)} %get-tuple-element.47), channel_id=1, source_target_pairs={{0,4},{12,8},{1,5},{13,9},{2,6},{14,10},{3,7},{15,11},{16,20},{28,... | collective-permute-start | bytes 786440 | tf_op jit(solution)/shard_map/ppermute | solution.py:417
  72.2 1.3 %collective-permute-start.20 = (bf16[1024,128]{1,0:T(8,128)(2,1)S(1)}, bf16[1024,128]{1,0:T(8,128)(2,1)S(1)}, u32[]{:S(2)}, u32[]{:S(2)}) collective-permute-start(bf16[1024,128]{1,0:T(8,128)(2,1)S(1)} %get-tuple-element.49), channel_id=1, source_target_pairs={{0,4},{12,8},{1,5},{13,9},{2,6},{14,10},{3,7},{15,11},{16,20},{28,... | collective-permute-start | bytes 786440 | tf_op jit(solution)/shard_map/ppermute | solution.py:417
  73.6 0.7 collective-permute-start.10
  74.4 0.7 collective-permute-start.12
  75.0 3.8 %collective-permute-done.18 = bf16[1024,128]{1,0:T(8,128)(2,1)S(1)} collective-permute-done((bf16[1024,128]{1,0:T(8,128)(2,1)S(1)}, bf16[1024,128]{1,0:T(8,128)(2,1)S(1)}, u32[]{:S(2)}, u32[]{:S(2)}) %collective-permute-start.18) | collective-permute-done | bytes 262176 | tf_op jit(solution)/shard_map/ppermute | solution.py:417
  78.9 0.7 collective-permute-start.19
  79.6 4.7 %collective-permute-done.20 = bf16[1024,128]{1,0:T(8,128)(2,1)S(1)} collective-permute-done((bf16[1024,128]{1,0:T(8,128)(2,1)S(1)}, bf16[1024,128]{1,0:T(8,128)(2,1)S(1)}, u32[]{:S(2)}, u32[]{:S(2)}) %collective-permute-start.20) | collective-permute-done | bytes 262176 | tf_op jit(solution)/shard_map/ppermute | solution.py:417
  84.3 0.7 collective-permute-start.21
  85.0 1.1 pad_maximum_fusion.pieces_ref
  86.1 1.2 %root_prep.1 = (bf16[1024,1024]{1,0:T(8,128)(2,1)S(1)}, bf16[1024,1024]{1,0:T(8,128)(2,1)S(1)}) custom-call(s32[1]{0:T(128)} %bitcast.3.mine_ref, bf16[8192,128]{1,0:T(8,128)(2,1)S(1)} %pad_maximum_fusion.pieces_ref), custom_call_target="tpu_custom_call" | custom-call | flops 1048576 | bytes 6291456 | tf_op jit(solution)/shard_map/root_prep/pallas_call | solution.py:270
  87.4 1.0 root_solve.4.rest_0_
  88.4 1.3 %collective-permute-start.13 = (bf16[1024,128]{1,0:T(8,128)(2,1)S(1)}, bf16[1024,128]{1,0:T(8,128)(2,1)S(1)}, u32[]{:S(2)}, u32[]{:S(2)}) collective-permute-start(bf16[1024,128]{1,0:T(8,128)(2,1)S(1)} %root_solve.4.rest_0_), channel_id=1, source_target_pairs={{4,0},{8,12},{5,1},{9,13},{6,2},{10,14},{7,3},{11,15},{20,16},{24,... | collective-permute-start | bytes 786440 | tf_op jit(solution)/shard_map/ppermute | solution.py:425
  89.7 1.0 root_solve.6.rest_0_
  90.7 1.3 %collective-permute-start.22 = (bf16[1024,128]{1,0:T(8,128)(2,1)S(1)}, bf16[1024,128]{1,0:T(8,128)(2,1)S(1)}, u32[]{:S(2)}, u32[]{:S(2)}) collective-permute-start(bf16[1024,128]{1,0:T(8,128)(2,1)S(1)} %root_solve.6.rest_0_), channel_id=1, source_target_pairs={{4,0},{8,12},{5,1},{9,13},{6,2},{10,14},{7,3},{11,15},{20,16},{24,... | collective-permute-start | bytes 786440 | tf_op jit(solution)/shard_map/ppermute | solution.py:425
  92.0 1.0 root_solve.7.rest_1_
  93.0 1.6 %collective-permute-start.23 = (bf16[1024,128]{1,0:T(8,128)(2,1)S(1)}, bf16[1024,128]{1,0:T(8,128)(2,1)S(1)}, u32[]{:S(2)}, u32[]{:S(2)}) collective-permute-start(bf16[1024,128]{1,0:T(8,128)(2,1)S(1)} %root_solve.7.rest_1_), channel_id=1, source_target_pairs={{4,0},{8,12},{5,1},{9,13},{6,2},{10,14},{7,3},{11,15},{20,16},{24,... | collective-permute-start | bytes 786440 | tf_op jit(solution)/shard_map/ppermute | solution.py:425
  94.5 1.0 root_solve.5.rest_1_
  95.5 1.3 %collective-permute-start.14 = (bf16[1024,128]{1,0:T(8,128)(2,1)S(1)}, bf16[1024,128]{1,0:T(8,128)(2,1)S(1)}, u32[]{:S(2)}, u32[]{:S(2)}) collective-permute-start(bf16[1024,128]{1,0:T(8,128)(2,1)S(1)} %root_solve.5.rest_1_), channel_id=1, source_target_pairs={{4,0},{8,12},{5,1},{9,13},{6,2},{10,14},{7,3},{11,15},{20,16},{24,... | collective-permute-start | bytes 786440 | tf_op jit(solution)/shard_map/ppermute | solution.py:425
  96.8 9.8 %collective-permute-done.22.rest_2_ = bf16[1024,128]{1,0:T(8,128)(2,1)S(1)} collective-permute-done((bf16[1024,128]{1,0:T(8,128)(2,1)S(1)}, bf16[1024,128]{1,0:T(8,128)(2,1)S(1)}, u32[]{:S(2)}, u32[]{:S(2)}) %collective-permute-start.22) | collective-permute-done | bytes 262176 | tf_op jit(solution)/shard_map/ppermute | solution.py:425
  106.6 5.6 %collective-permute-done.23.rest_3_ = bf16[1024,128]{1,0:T(8,128)(2,1)S(1)} collective-permute-done((bf16[1024,128]{1,0:T(8,128)(2,1)S(1)}, bf16[1024,128]{1,0:T(8,128)(2,1)S(1)}, u32[]{:S(2)}, u32[]{:S(2)}) %collective-permute-start.23) | collective-permute-done | bytes 262176 | tf_op jit(solution)/shard_map/ppermute | solution.py:425
  112.3 3.0 %backward.2 = (bf16[2048,512]{1,0:T(8,128)(2,1)}, bf16[1024,512]{1,0:T(8,128)(2,1)}) custom-call(s32[1]{0:T(128)} %bitcast.take_ref, bf16[2048,256]{1,0:T(8,128)(2,1)S(1)} %get-tuple-element.45.fwd_ref, bf16[2048,1024]{1,0:T(8,128)(2,1)S(1)} %copy-done.8, bf16[4,512,512]{2,1,0:T(8,128)(2,1)S(1)} %copy-done.12, bf16[1024,128]{1,0:T(8,128)(2,1)S(1)} %root_solve.6.rest_0_, ...), custom_call_target="tpu_custom_call" | custom-call | flops 16106127360 | bytes 9961472 | tf_op jit(solution)/shard_map/backward/pallas_call | solution.py:346
  115.3 1.5 %collective-permute-done.14.rest_3_ = bf16[1024,128]{1,0:T(8,128)(2,1)S(1)} collective-permute-done((bf16[1024,128]{1,0:T(8,128)(2,1)S(1)}, bf16[1024,128]{1,0:T(8,128)(2,1)S(1)}, u32[]{:S(2)}, u32[]{:S(2)}) %collective-permute-start.14) | collective-permute-done | bytes 262176 | tf_op jit(solution)/shard_map/ppermute | solution.py:425
  116.8 3.0 %backward.3 = (bf16[2048,512]{1,0:T(8,128)(2,1)}, bf16[1024,512]{1,0:T(8,128)(2,1)}) custom-call(s32[1]{0:T(128)} %bitcast.take_ref, bf16[2048,256]{1,0:T(8,128)(2,1)S(1)} %get-tuple-element.33.fwd_ref, bf16[2048,1024]{1,0:T(8,128)(2,1)S(1)} %copy-done.8, bf16[4,512,512]{2,1,0:T(8,128)(2,1)S(1)} %copy-done.12, ...), custom_call_target="tpu_custom_call", output_to_operand_aliasing={{0}: (8, {}), {1}: (9, {})} | custom-call | flops 16106127360 | bytes 9961472 | tf_op jit(solution)/shard_map/backward/pallas_call | solution.py:346
  (50 shorter events, 1.1 us)
Async XLA Ops:
  0.6 1.6 %copy-start.1 = (bf16[2048,512]{1,0:T(8,128)(2,1)S(1)}, bf16[2048,512]{1,0:T(8,128)(2,1)}, u32[]{:S(2)}) copy-start(bf16[2048,512]{1,0:T(8,128)(2,1)} %loads_ref.5) | copy-start | bytes 6291460
  2.2 0.7 copy-start.5
  2.9 5.8 %copy-start = (bf16[256,1024]{1,0:T(8,128)(2,1)S(1)}, bf16[256,1024]{1,0:T(8,128)(2,1)}, u32[]{:S(2)}) copy-start(bf16[256,1024]{1,0:T(8,128)(2,1)} %inv_ref.6) | copy-start | bytes 1572868
  2.9 20.5 %copy-start.2 = (bf16[4,512,512]{2,1,0:T(8,128)(2,1)S(1)}, bf16[4,512,512]{2,1,0:T(8,128)(2,1)}, u32[]{:S(2)}) copy-start(bf16[4,512,512]{2,1,0:T(8,128)(2,1)} %couple_ref.1) | copy-start | bytes 6291460
  2.9 20.5 %copy-start.3 = (bf16[4,512,512]{2,1,0:T(8,128)(2,1)S(1)}, bf16[4,512,512]{2,1,0:T(8,128)(2,1)}, u32[]{:S(2)}) copy-start(bf16[4,512,512]{2,1,0:T(8,128)(2,1)} %inv_ref.7) | copy-start | bytes 6291460
  2.9 20.5 %copy-start.6 = (s32[4,512]{1,0:T(4,128)S(1)}, s32[4,512]{1,0:T(4,128)}, u32[]{:S(2)}) copy-start(s32[4,512]{1,0:T(4,128)} %rows_ref.1) | copy-start | bytes 24580
  8.7 13.1 %copy-start.13 = (bf16[512,256]{1,0:T(8,128)(2,1)}, bf16[512,256]{1,0:T(8,128)(2,1)S(1)}, u32[]{:S(2)}) copy-start(bf16[512,256]{1,0:T(8,128)(2,1)S(1)} %get-tuple-element.29.rest_0_) | copy-start | bytes 786436
  8.8 10.0 %collective-permute-start.3 = (bf16[256,128]{1,0:T(8,128)(2,1)S(1)}, bf16[256,128]{1,0:T(8,128)(2,1)S(1)}, u32[]{:S(2)}, u32[]{:S(2)}) collective-permute-start(bf16[256,128]{1,0:T(8,128)(2,1)S(1)} %piece.1.rest_0_), channel_id=1, source_target_pairs={{0,4},{12,8},{1,5},{13,9},{2,6},{14,10},{3,7},{15,11},{16,20},{28,... | collective-permute-start | bytes 196616 | tf_op jit(solution)/shard_map/ppermute | solution.py:396
  13.7 7.5 %collective-permute-start.4 = (bf16[256,128]{1,0:T(8,128)(2,1)S(1)}, bf16[256,128]{1,0:T(8,128)(2,1)S(1)}, u32[]{:S(2)}, u32[]{:S(2)}) collective-permute-start(bf16[256,128]{1,0:T(8,128)(2,1)S(1)} %piece.1.rest_0_), channel_id=1, source_target_pairs={{0,8},{12,4},{1,9},{13,5},{2,10},{14,6},{3,11},{15,7},{16,24},{28,... | collective-permute-start | bytes 196616 | tf_op jit(solution)/shard_map/ppermute | solution.py:396
  16.0 5.4 %collective-permute-start.5 = (bf16[256,128]{1,0:T(8,128)(2,1)S(1)}, bf16[256,128]{1,0:T(8,128)(2,1)S(1)}, u32[]{:S(2)}, u32[]{:S(2)}) collective-permute-start(bf16[256,128]{1,0:T(8,128)(2,1)S(1)} %piece.1.rest_0_), channel_id=1, source_target_pairs={{4,8},{8,4},{5,9},{9,5},{6,10},{10,6},{7,11},{11,7},{20,24},{24,20... | collective-permute-start | bytes 196616 | tf_op jit(solution)/shard_map/ppermute | solution.py:396
  16.7 20.9 %collective-permute-start = (bf16[512,256]{1,0:T(8,128)(2,1)}, bf16[512,256]{1,0:T(8,128)(2,1)}, u32[]{:S(2)}, u32[]{:S(2)}) collective-permute-start(bf16[512,256]{1,0:T(8,128)(2,1)} %get-tuple-element.30), channel_id=1, source_target_pairs={{0,4},{4,0},{8,12},{12,8},{1,5},{5,1},{9,13},{13,9},{2,6},{6,2},{1... | collective-permute-start | bytes 786440 | tf_op jit(solution)/shard_map/ppermute | solution.py:406
  18.0 22.1 %collective-permute-start.1 = (bf16[512,256]{1,0:T(8,128)(2,1)}, bf16[512,256]{1,0:T(8,128)(2,1)}, u32[]{:S(2)}, u32[]{:S(2)}) collective-permute-start(bf16[512,256]{1,0:T(8,128)(2,1)} %get-tuple-element.31), channel_id=1, source_target_pairs={{0,8},{4,12},{8,0},{12,4},{1,9},{5,13},{9,1},{13,5},{2,10},{6,14},... | collective-permute-start | bytes 786440 | tf_op jit(solution)/shard_map/ppermute | solution.py:406
  18.8 22.8 %collective-permute-start.2 = (bf16[512,256]{1,0:T(8,128)(2,1)}, bf16[512,256]{1,0:T(8,128)(2,1)}, u32[]{:S(2)}, u32[]{:S(2)}) collective-permute-start(bf16[512,256]{1,0:T(8,128)(2,1)} %get-tuple-element.32), channel_id=1, source_target_pairs={{0,12},{4,8},{8,4},{12,0},{1,13},{5,9},{9,5},{13,1},{2,14},{6,10},... | collective-permute-start | bytes 786440 | tf_op jit(solution)/shard_map/ppermute | solution.py:406
  21.2 46.7 %collective-permute-start.15 = (bf16[512,256]{1,0:T(8,128)(2,1)S(1)}, bf16[512,256]{1,0:T(8,128)(2,1)}, u32[]{:S(2)}, u32[]{:S(2)}) collective-permute-start(bf16[512,256]{1,0:T(8,128)(2,1)S(1)} %get-tuple-element.42), channel_id=1, source_target_pairs={{0,4},{4,0},{8,12},{12,8},{1,5},{5,1},{9,13},{13,9},{2,6},{6,2},{1... | collective-permute-start | bytes 786440 | tf_op jit(solution)/shard_map/ppermute | solution.py:406
  21.8 13.1 %collective-permute-start.6 = (bf16[1024,128]{1,0:T(8,128)(2,1)S(1)}, bf16[1024,128]{1,0:T(8,128)(2,1)}, u32[]{:S(2)}, u32[]{:S(2)}) collective-permute-start(bf16[1024,128]{1,0:T(8,128)(2,1)S(1)} %gather_rows.1), channel_id=1, source_target_pairs={{0,16},{16,0},{1,17},{17,1},{2,18},{18,2},{3,19},{19,3},{4,20},{20... | collective-permute-start | bytes 786440 | tf_op jit(solution)/shard_map/ppermute | solution.py:400
  29.6 2.0 %copy-start.7 = (bf16[2048,1024]{1,0:T(8,128)(2,1)}, bf16[2048,1024]{1,0:T(8,128)(2,1)S(1)}, u32[]{:S(2)}) copy-start(bf16[2048,1024]{1,0:T(8,128)(2,1)S(1)} %get-tuple-element.34.spread_t_ref) | copy-start | bytes 12582916
  31.5 2.0 %copy-start.9 = (bf16[1024,2048]{1,0:T(8,128)(2,1)}, bf16[1024,2048]{1,0:T(8,128)(2,1)S(1)}, u32[]{:S(2)}) copy-start(bf16[1024,2048]{1,0:T(8,128)(2,1)S(1)} %get-tuple-element.28.spread_ref) | copy-start | bytes 12582916
  33.6 1.3 %copy-start.11 = (bf16[4,512,512]{2,1,0:T(8,128)(2,1)}, bf16[4,512,512]{2,1,0:T(8,128)(2,1)S(1)}, u32[]{:S(2)}) copy-start(bf16[4,512,512]{2,1,0:T(8,128)(2,1)S(1)} %get-tuple-element.35.inv_t_ref) | copy-start | bytes 6291460
  34.9 33.0 %collective-permute-start.16 = (bf16[512,256]{1,0:T(8,128)(2,1)S(1)}, bf16[512,256]{1,0:T(8,128)(2,1)S(1)}, u32[]{:S(2)}, u32[]{:S(2)}) collective-permute-start(bf16[512,256]{1,0:T(8,128)(2,1)S(1)} %get-tuple-element.43), channel_id=1, source_target_pairs={{0,8},{4,12},{8,0},{12,4},{1,9},{5,13},{9,1},{13,5},{2,10},{6,14},... | collective-permute-start | bytes 786440 | tf_op jit(solution)/shard_map/ppermute | solution.py:406
  37.6 30.3 %collective-permute-start.17 = (bf16[512,256]{1,0:T(8,128)(2,1)S(1)}, bf16[512,256]{1,0:T(8,128)(2,1)S(1)}, u32[]{:S(2)}, u32[]{:S(2)}) collective-permute-start(bf16[512,256]{1,0:T(8,128)(2,1)S(1)} %get-tuple-element.44), channel_id=1, source_target_pairs={{0,12},{4,8},{8,4},{12,0},{1,13},{5,9},{9,5},{13,1},{2,14},{6,10},... | collective-permute-start | bytes 786440 | tf_op jit(solution)/shard_map/ppermute | solution.py:406
  40.1 25.2 %collective-permute-start.7 = (bf16[2048,128]{1,0:T(8,128)(2,1)S(1)}, bf16[2048,128]{1,0:T(8,128)(2,1)S(1)}, u32[]{:S(2)}, u32[]{:S(2)}) collective-permute-start(bf16[2048,128]{1,0:T(8,128)(2,1)S(1)} %pad_maximum_fusion.2), channel_id=1, source_target_pairs={{0,2},{1,3},{2,0},{3,1},{4,6},{5,7},{6,4},{7,5},{8,10},{9,11},{10,... | collective-permute-start | bytes 1572872 | tf_op jit(solution)/shard_map/ppermute | solution.py:400
  41.5 2.2 %copy-start.10 = (bf16[1024,2048]{1,0:T(8,128)(2,1)S(1)}, bf16[1024,2048]{1,0:T(8,128)(2,1)}, u32[]{:S(2)}) copy-start(bf16[1024,2048]{1,0:T(8,128)(2,1)} %copy-done.9) | copy-start | bytes 12582916
  43.7 0.9 copy-start.14
  47.8 25.7 %collective-permute-start.9 = (bf16[1024,128]{1,0:T(8,128)(2,1)S(1)}, bf16[1024,128]{1,0:T(8,128)(2,1)S(1)}, u32[]{:S(2)}, u32[]{:S(2)}) collective-permute-start(bf16[1024,128]{1,0:T(8,128)(2,1)S(1)} %get-tuple-element.39), channel_id=1, source_target_pairs={{0,4},{12,8},{1,5},{13,9},{2,6},{14,10},{3,7},{15,11},{16,20},{28,... | collective-permute-start | bytes 786440 | tf_op jit(solution)/shard_map/ppermute | solution.py:417
  65.3 9.0 %collective-permute-start.11 = (bf16[1024,128]{1,0:T(8,128)(2,1)S(1)}, bf16[1024,128]{1,0:T(8,128)(2,1)S(1)}, u32[]{:S(2)}, u32[]{:S(2)}) collective-permute-start(bf16[1024,128]{1,0:T(8,128)(2,1)S(1)} %get-tuple-element.41), channel_id=1, source_target_pairs={{0,4},{12,8},{1,5},{13,9},{2,6},{14,10},{3,7},{15,11},{16,20},{28,... | collective-permute-start | bytes 786440 | tf_op jit(solution)/shard_map/ppermute | solution.py:417
  67.8 17.2 %collective-permute-start.8 = (bf16[4096,128]{1,0:T(8,128)(2,1)S(1)}, bf16[4096,128]{1,0:T(8,128)(2,1)S(1)}, u32[]{:S(2)}, u32[]{:S(2)}) collective-permute-start(bf16[4096,128]{1,0:T(8,128)(2,1)S(1)} %pad_maximum_fusion.1), channel_id=1, source_target_pairs={{0,1},{1,0},{2,3},{3,2},{4,5},{5,4},{6,7},{7,6},{8,9},{9,8},{10,11... | collective-permute-start | bytes 3145736 | tf_op jit(solution)/shard_map/ppermute | solution.py:400
  70.9 8.0 %collective-permute-start.18 = (bf16[1024,128]{1,0:T(8,128)(2,1)S(1)}, bf16[1024,128]{1,0:T(8,128)(2,1)S(1)}, u32[]{:S(2)}, u32[]{:S(2)}) collective-permute-start(bf16[1024,128]{1,0:T(8,128)(2,1)S(1)} %get-tuple-element.47), channel_id=1, source_target_pairs={{0,4},{12,8},{1,5},{13,9},{2,6},{14,10},{3,7},{15,11},{16,20},{28,... | collective-permute-start | bytes 786440 | tf_op jit(solution)/shard_map/ppermute | solution.py:417
  72.2 12.1 %collective-permute-start.20 = (bf16[1024,128]{1,0:T(8,128)(2,1)S(1)}, bf16[1024,128]{1,0:T(8,128)(2,1)S(1)}, u32[]{:S(2)}, u32[]{:S(2)}) collective-permute-start(bf16[1024,128]{1,0:T(8,128)(2,1)S(1)} %get-tuple-element.49), channel_id=1, source_target_pairs={{0,4},{12,8},{1,5},{13,9},{2,6},{14,10},{3,7},{15,11},{16,20},{28,... | collective-permute-start | bytes 786440 | tf_op jit(solution)/shard_map/ppermute | solution.py:417
  73.6 13.8 %collective-permute-start.10 = (bf16[1024,128]{1,0:T(8,128)(2,1)S(1)}, bf16[1024,128]{1,0:T(8,128)(2,1)S(1)}, u32[]{:S(2)}, u32[]{:S(2)}) collective-permute-start(bf16[1024,128]{1,0:T(8,128)(2,1)S(1)} %add_convert_fusion.3.one_ref), channel_id=1, source_target_pairs={{4,8},{8,4},{5,9},{9,5},{6,10},{10,6},{7,11},{11,7},{20,24},{24,20... | collective-permute-start | bytes 786440 | tf_op jit(solution)/shard_map/ppermute | solution.py:419
  74.4 20.2 %collective-permute-start.12 = (bf16[1024,128]{1,0:T(8,128)(2,1)S(1)}, bf16[1024,128]{1,0:T(8,128)(2,1)S(1)}, u32[]{:S(2)}, u32[]{:S(2)}) collective-permute-start(bf16[1024,128]{1,0:T(8,128)(2,1)S(1)} %add_convert_fusion.2.one_ref), channel_id=1, source_target_pairs={{4,8},{8,4},{5,9},{9,5},{6,10},{10,6},{7,11},{11,7},{20,24},{24,20... | collective-permute-start | bytes 786440 | tf_op jit(solution)/shard_map/ppermute | solution.py:419
  78.9 10.7 %collective-permute-start.19 = (bf16[1024,128]{1,0:T(8,128)(2,1)S(1)}, bf16[1024,128]{1,0:T(8,128)(2,1)S(1)}, u32[]{:S(2)}, u32[]{:S(2)}) collective-permute-start(bf16[1024,128]{1,0:T(8,128)(2,1)S(1)} %add_convert_fusion.1.one_ref), channel_id=1, source_target_pairs={{4,8},{8,4},{5,9},{9,5},{6,10},{10,6},{7,11},{11,7},{20,24},{24,20... | collective-permute-start | bytes 786440 | tf_op jit(solution)/shard_map/ppermute | solution.py:419
  84.3 7.6 %collective-permute-start.21 = (bf16[1024,128]{1,0:T(8,128)(2,1)S(1)}, bf16[1024,128]{1,0:T(8,128)(2,1)S(1)}, u32[]{:S(2)}, u32[]{:S(2)}) collective-permute-start(bf16[1024,128]{1,0:T(8,128)(2,1)S(1)} %add_convert_fusion.one_ref), channel_id=1, source_target_pairs={{4,8},{8,4},{5,9},{9,5},{6,10},{10,6},{7,11},{11,7},{20,24},{24,20... | collective-permute-start | bytes 786440 | tf_op jit(solution)/shard_map/ppermute | solution.py:419
  86.1 1.3 %copy-start.4 = (bf16[1024,512]{1,0:T(8,128)(2,1)S(1)}, bf16[1024,512]{1,0:T(8,128)(2,1)}, u32[]{:S(2)}) copy-start(bf16[1024,512]{1,0:T(8,128)(2,1)} %loads_ref.9) | copy-start | bytes 3145732
  88.4 26.9 %collective-permute-start.13 = (bf16[1024,128]{1,0:T(8,128)(2,1)S(1)}, bf16[1024,128]{1,0:T(8,128)(2,1)S(1)}, u32[]{:S(2)}, u32[]{:S(2)}) collective-permute-start(bf16[1024,128]{1,0:T(8,128)(2,1)S(1)} %root_solve.4.rest_0_), channel_id=1, source_target_pairs={{4,0},{8,12},{5,1},{9,13},{6,2},{10,14},{7,3},{11,15},{20,16},{24,... | collective-permute-start | bytes 786440 | tf_op jit(solution)/shard_map/ppermute | solution.py:425
  90.7 16.0 %collective-permute-start.22 = (bf16[1024,128]{1,0:T(8,128)(2,1)S(1)}, bf16[1024,128]{1,0:T(8,128)(2,1)S(1)}, u32[]{:S(2)}, u32[]{:S(2)}) collective-permute-start(bf16[1024,128]{1,0:T(8,128)(2,1)S(1)} %root_solve.6.rest_0_), channel_id=1, source_target_pairs={{4,0},{8,12},{5,1},{9,13},{6,2},{10,14},{7,3},{11,15},{20,16},{24,... | collective-permute-start | bytes 786440 | tf_op jit(solution)/shard_map/ppermute | solution.py:425
  92.9 19.3 %copy-start.8 = (bf16[2048,1024]{1,0:T(8,128)(2,1)S(1)}, bf16[2048,1024]{1,0:T(8,128)(2,1)}, u32[]{:S(2)}) copy-start(bf16[2048,1024]{1,0:T(8,128)(2,1)} %copy-done.7) | copy-start | bytes 12582916
  93.0 19.3 %copy-start.12 = (bf16[4,512,512]{2,1,0:T(8,128)(2,1)S(1)}, bf16[4,512,512]{2,1,0:T(8,128)(2,1)}, u32[]{:S(2)}) copy-start(bf16[4,512,512]{2,1,0:T(8,128)(2,1)} %copy-done.11) | copy-start | bytes 6291460
  93.0 19.3 %collective-permute-start.23 = (bf16[1024,128]{1,0:T(8,128)(2,1)S(1)}, bf16[1024,128]{1,0:T(8,128)(2,1)S(1)}, u32[]{:S(2)}, u32[]{:S(2)}) collective-permute-start(bf16[1024,128]{1,0:T(8,128)(2,1)S(1)} %root_solve.7.rest_1_), channel_id=1, source_target_pairs={{4,0},{8,12},{5,1},{9,13},{6,2},{10,14},{7,3},{11,15},{20,16},{24,... | collective-permute-start | bytes 786440 | tf_op jit(solution)/shard_map/ppermute | solution.py:425
  95.5 21.3 %collective-permute-start.14 = (bf16[1024,128]{1,0:T(8,128)(2,1)S(1)}, bf16[1024,128]{1,0:T(8,128)(2,1)S(1)}, u32[]{:S(2)}, u32[]{:S(2)}) collective-permute-start(bf16[1024,128]{1,0:T(8,128)(2,1)S(1)} %root_solve.5.rest_1_), channel_id=1, source_target_pairs={{4,0},{8,12},{5,1},{9,13},{6,2},{10,14},{7,3},{11,15},{20,16},{24,... | collective-permute-start | bytes 786440 | tf_op jit(solution)/shard_map/ppermute | solution.py:425

commit v5 on v4

--- a/solution.py
+++ b/solution.py
@@ -390,7 +390,7 @@
     sizes_of = [min(GROUP * LANES, width - first) for first in range(0, width, GROUP * LANES)]
     firsts = [sum(sizes_of[:g]) for g in range(len(sizes_of))]
     sent = pick(nodes, firsts, sizes_of, me, rows, loads, [])
-    piece = take_piece(mine, root_inv, count, [sent[0]])
+    piece = take_piece(mine, root_inv, count, [])
     pieces = [piece]
     for s in range(1, nodes):
         pieces.append(lax.ppermute(piece, "node", [(i, i ^ s) for i in range(nodes) if i ^ s in top[0]]))

time: 121 us -> 120 us (level)
  other arithmetic: 3.31 us -> 0.46 us
    concatenate x3, other arithmetic: 3.09 us -> 0.24 us  [per_device(): piece = jnp.concatenate([piece, lax.ppermute(piece, axis, pairs)], axis=0)]
  transfers between devices with their start and end apart: 24 -> 24, of which waited for: 5 -> 6; matrix products, arithmetic and copies ran while one was open for 3% -> 0% of each run, Pallas kernels for 17% -> 22%
where the time goes in v5:
time: 120 us; the launch traced here: 119 us
  starting transfers between devices  50.2 us (42%)
  Pallas kernels  29.3 us (24%)
  waiting for transfers between devices  26 us (22%)
  local copies, waits for them, and re-layouts  11.8 us (10%)
  between operations  1.25 us (1%)
    ppermute x4, starting transfers between devices, per_device(): wide = wide + lax.ppermute(part, 'node', pairs).astype(F32)  22.1 us
    ppermute x4, waiting for transfers between devices, per_device(): got = lax.ppermute(own, 'node', [(b, a) for a, b in pairs])  17 us
    unnamed x30, local copies, waits for them, and re-layouts  11.8 us
    ppermute x6, starting transfers between devices, per_device(): lax.ppermute(own[s], 'node', pairs[s])  8.89 us
    ppermute x4, waiting for transfers between devices, per_device(): wide = wide + lax.ppermute(part, 'node', pairs).astype(F32)  8.35 us
    ppermute x3, starting transfers between devices, per_device(): lax.ppermute(piece, 'node', [(i, i ^ s) for i in range(nodes) if i ^ s in...  7.9 us
    pallas_call x1, Pallas kernels, prep(): pl.pallas_call(prep_kernel, in_specs=[vmem_spec()] * 3 + [any_spec()] * l...  6.13 us
    pallas_call x2, Pallas kernels, forward(): pl.pallas_call(functools.partial(forward_kernel, nodes, chunks), in_specs...  6.04 us
  transfers between devices with their start and end apart: 24, of which 6 were waited for; matrix products, arithmetic and copies ran while one was open for 0% of the time, Pallas kernels for 22%

profile of v5, /device:TPU:0, one launch (start us, length us, event | category | flops | bytes accessed | tf_op | source)
XLA Modules:
  0.0 118.9 jit_solution(4413330372251920415)
XLA Ops:
  0.6 1.0 copy-done
  1.7 4.9 %collective-permute-start.3 = (bf16[256,128]{1,0:T(8,128)(2,1)S(1)}, bf16[256,128]{1,0:T(8,128)(2,1)S(1)}, u32[]{:S(2)}, u32[]{:S(2)}) collective-permute-start(bf16[256,128]{1,0:T(8,128)(2,1)S(1)} %piece.1.rest_0_), channel_id=1, source_target_pairs={{0,4},{12,8},{1,5},{13,9},{2,6},{14,10},{3,7},{15,11},{16,20},{28,... | collective-permute-start | bytes 196616 | tf_op jit(solution)/shard_map/ppermute | solution.py:396
  6.7 2.3 %collective-permute-start.4 = (bf16[256,128]{1,0:T(8,128)(2,1)S(1)}, bf16[256,128]{1,0:T(8,128)(2,1)S(1)}, u32[]{:S(2)}, u32[]{:S(2)}) collective-permute-start(bf16[256,128]{1,0:T(8,128)(2,1)S(1)} %piece.1.rest_0_), channel_id=1, source_target_pairs={{0,8},{12,4},{1,9},{13,5},{2,10},{14,6},{3,11},{15,7},{16,24},{28,... | collective-permute-start | bytes 196616 | tf_op jit(solution)/shard_map/ppermute | solution.py:396
  9.0 0.7 collective-permute-start.5
  9.7 1.6 %copy-done.1 = bf16[2048,512]{1,0:T(8,128)(2,1)S(1)} copy-done((bf16[2048,512]{1,0:T(8,128)(2,1)S(1)}, bf16[2048,512]{1,0:T(8,128)(2,1)}, u32[]{:S(2)}) %copy-start.1) | copy-done | bytes 2097176
  11.2 0.7 copy-done.5
  11.9 5.8 %pick.1 = (bf16[512,256]{1,0:T(8,128)(2,1)S(1)}, bf16[512,256]{1,0:T(8,128)(2,1)}, bf16[512,256]{1,0:T(8,128)(2,1)S(1)}, bf16[512,256]{1,0:T(8,128)(2,1)S(1)}, b...) custom-call(s32[1]{0:T(128)} %bitcast.1.me_ref, ...), custom_call_target="tpu_custom_call" | custom-call | flops 4294967296 | bytes 4194304 | tf_op jit(solution)/shard_map/pick/pallas_call | solution.py:101
  17.7 1.3 %collective-permute-start = (bf16[512,256]{1,0:T(8,128)(2,1)}, bf16[512,256]{1,0:T(8,128)(2,1)}, u32[]{:S(2)}, u32[]{:S(2)}) collective-permute-start(bf16[512,256]{1,0:T(8,128)(2,1)} %get-tuple-element.30), channel_id=1, source_target_pairs={{0,4},{4,0},{8,12},{12,8},{1,5},{5,1},{9,13},{13,9},{2,6},{6,2},{1... | collective-permute-start | bytes 786440 | tf_op jit(solution)/shard_map/ppermute | solution.py:406
  19.0 0.8 collective-permute-start.1
  19.8 2.4 %collective-permute-start.2 = (bf16[512,256]{1,0:T(8,128)(2,1)}, bf16[512,256]{1,0:T(8,128)(2,1)}, u32[]{:S(2)}, u32[]{:S(2)}) collective-permute-start(bf16[512,256]{1,0:T(8,128)(2,1)} %get-tuple-element.32), channel_id=1, source_target_pairs={{0,12},{4,8},{8,4},{12,0},{1,13},{5,9},{9,5},{13,1},{2,14},{6,10},... | collective-permute-start | bytes 786440 | tf_op jit(solution)/shard_map/ppermute | solution.py:406
  22.5 0.4 gather_rows.1
  22.9 1.6 %collective-permute-start.6 = (bf16[1024,128]{1,0:T(8,128)(2,1)S(1)}, bf16[1024,128]{1,0:T(8,128)(2,1)S(1)}, u32[]{:S(2)}, u32[]{:S(2)}) collective-permute-start(bf16[1024,128]{1,0:T(8,128)(2,1)S(1)} %gather_rows.1), channel_id=1, source_target_pairs={{0,16},{16,0},{1,17},{17,1},{2,18},{18,2},{3,19},{19,3},{4,20},{20... | collective-permute-start | bytes 786440 | tf_op jit(solution)/shard_map/ppermute | solution.py:400
  24.5 6.1 %prep.1 = (bf16[1024,2048]{1,0:T(8,128)(2,1)S(1)}, bf16[2048,1024]{1,0:T(8,128)(2,1)S(1)}, bf16[4,512,512]{2,1,0:T(8,128)(2,1)S(1)}) custom-call(s32[4,512]{1,0:T(4,128)S(1)} %copy-done.6, bf16[4,512,512]{2,1,0:T(8,128)(2,1)S(1)} %copy-done.2, bf16[4,512,512]{2,1,0:T(8,128)(2,1)S(1)} %copy-done.3, bf16[512,256]{1,0:T(8,128)(2,1)S(1)} %get-tuple-element.27.rest_0_.rest_4_), custom_call_target="tpu_custom_call" | custom-call | flops 6442450944 | bytes 14680064 | tf_op jit(solution)/shard_map/prep/pallas_call | solution.py:145
  30.6 2.0 %copy-done.7 = bf16[2048,1024]{1,0:T(8,128)(2,1)} copy-done((bf16[2048,1024]{1,0:T(8,128)(2,1)}, bf16[2048,1024]{1,0:T(8,128)(2,1)S(1)}, u32[]{:S(2)}) %copy-start.7) | copy-done | bytes 4194328
  32.6 2.0 %copy-done.9 = bf16[1024,2048]{1,0:T(8,128)(2,1)} copy-done((bf16[1024,2048]{1,0:T(8,128)(2,1)}, bf16[1024,2048]{1,0:T(8,128)(2,1)S(1)}, u32[]{:S(2)}) %copy-start.9) | copy-done | bytes 4194328
  34.6 1.3 %copy-done.11 = bf16[4,512,512]{2,1,0:T(8,128)(2,1)} copy-done((bf16[4,512,512]{2,1,0:T(8,128)(2,1)}, bf16[4,512,512]{2,1,0:T(8,128)(2,1)S(1)}, u32[]{:S(2)}) %copy-start.11) | copy-done | bytes 2097176
  35.9 1.7 %collective-permute-start.16 = (bf16[512,256]{1,0:T(8,128)(2,1)S(1)}, bf16[512,256]{1,0:T(8,128)(2,1)S(1)}, u32[]{:S(2)}, u32[]{:S(2)}) collective-permute-start(bf16[512,256]{1,0:T(8,128)(2,1)S(1)} %get-tuple-element.43), channel_id=1, source_target_pairs={{0,8},{4,12},{8,0},{12,4},{1,9},{5,13},{9,1},{13,5},{2,10},{6,14},... | collective-permute-start | bytes 786440 | tf_op jit(solution)/shard_map/ppermute | solution.py:406
  37.7 2.4 %collective-permute-start.17 = (bf16[512,256]{1,0:T(8,128)(2,1)S(1)}, bf16[512,256]{1,0:T(8,128)(2,1)S(1)}, u32[]{:S(2)}, u32[]{:S(2)}) collective-permute-start(bf16[512,256]{1,0:T(8,128)(2,1)S(1)} %get-tuple-element.44), channel_id=1, source_target_pairs={{0,12},{4,8},{8,4},{12,0},{1,13},{5,9},{9,5},{13,1},{2,14},{6,10},... | collective-permute-start | bytes 786440 | tf_op jit(solution)/shard_map/ppermute | solution.py:406
  40.1 0.6 collective-permute-done.1.rest_2_
  40.7 1.5 %collective-permute-start.7 = (bf16[2048,128]{1,0:T(8,128)(2,1)S(1)}, bf16[2048,128]{1,0:T(8,128)(2,1)S(1)}, u32[]{:S(2)}, u32[]{:S(2)}) collective-permute-start(bf16[2048,128]{1,0:T(8,128)(2,1)S(1)} %pad_maximum_fusion.2), channel_id=1, source_target_pairs={{0,2},{1,3},{2,0},{3,1},{4,6},{5,7},{6,4},{7,5},{8,10},{9,11},{10,... | collective-permute-start | bytes 1572872 | tf_op jit(solution)/shard_map/ppermute | solution.py:400
  42.2 2.2 %copy-done.10 = bf16[1024,2048]{1,0:T(8,128)(2,1)S(1)} copy-done((bf16[1024,2048]{1,0:T(8,128)(2,1)S(1)}, bf16[1024,2048]{1,0:T(8,128)(2,1)}, u32[]{:S(2)}) %copy-start.10) | copy-done | bytes 4194328
  44.4 0.9 copy-done.14
  45.3 3.1 %forward.2 = (bf16[2048,256]{1,0:T(8,128)(2,1)S(1)}, bf16[1024,128]{1,0:T(8,128)(2,1)S(1)}, bf16[1024,128]{1,0:T(8,128)(2,1)S(1)}, f32[1024,128]{1,0:T(8,128)S(1)}, f32[1024,128]{1,0:T(8,128)S(1)}) custom-call(s32[1]{0:T(128)} %bitcast.1.me_ref, bf16[4,512,512]{2,1,0:T(8,128)(2,1)S(1)} %copy-done.3, bf16[1024,2048]{1,0:T(8,128)(2,1)S(1)} %copy-done.10, ...), custom_call_target="tpu_custom_call" | custom-call | flops 32212254720 | bytes 190316544 | tf_op jit(solution)/shard_map/forward/pallas_call | solution.py:189
  48.5 17.8 %collective-permute-start.9 = (bf16[1024,128]{1,0:T(8,128)(2,1)S(1)}, bf16[1024,128]{1,0:T(8,128)(2,1)S(1)}, u32[]{:S(2)}, u32[]{:S(2)}) collective-permute-start(bf16[1024,128]{1,0:T(8,128)(2,1)S(1)} %get-tuple-element.39), channel_id=1, source_target_pairs={{0,4},{12,8},{1,5},{13,9},{2,6},{14,10},{3,7},{15,11},{16,20},{28,... | collective-permute-start | bytes 786440 | tf_op jit(solution)/shard_map/ppermute | solution.py:417
  66.3 1.5 %collective-permute-start.11 = (bf16[1024,128]{1,0:T(8,128)(2,1)S(1)}, bf16[1024,128]{1,0:T(8,128)(2,1)S(1)}, u32[]{:S(2)}, u32[]{:S(2)}) collective-permute-start(bf16[1024,128]{1,0:T(8,128)(2,1)S(1)} %get-tuple-element.41), channel_id=1, source_target_pairs={{0,4},{12,8},{1,5},{13,9},{2,6},{14,10},{3,7},{15,11},{16,20},{28,... | collective-permute-start | bytes 786440 | tf_op jit(solution)/shard_map/ppermute | solution.py:417
  68.0 2.9 %forward.3 = (bf16[2048,256]{1,0:T(8,128)(2,1)S(1)}, bf16[1024,128]{1,0:T(8,128)(2,1)S(1)}, bf16[1024,128]{1,0:T(8,128)(2,1)S(1)}, f32[1024,128]{1,0:T(8,128)S(1)}, f32[1024,128]{1,0:T(8,128)S(1)}) custom-call(s32[1]{0:T(128)} %bitcast.1.me_ref, bf16[4,512,512]{2,1,0:T(8,128)(2,1)S(1)} %copy-done.3, bf16[1024,2048]{1,0:T(8,128)(2,1)S(1)} %copy-done.10, ...), custom_call_target="tpu_custom_call" | custom-call | flops 32212254720 | bytes 190316544 | tf_op jit(solution)/shard_map/forward/pallas_call | solution.py:189
  70.9 1.5 %collective-permute-start.18 = (bf16[1024,128]{1,0:T(8,128)(2,1)S(1)}, bf16[1024,128]{1,0:T(8,128)(2,1)S(1)}, u32[]{:S(2)}, u32[]{:S(2)}) collective-permute-start(bf16[1024,128]{1,0:T(8,128)(2,1)S(1)} %get-tuple-element.47), channel_id=1, source_target_pairs={{0,4},{12,8},{1,5},{13,9},{2,6},{14,10},{3,7},{15,11},{16,20},{28,... | collective-permute-start | bytes 786440 | tf_op jit(solution)/shard_map/ppermute | solution.py:417
  72.4 1.3 %collective-permute-start.20 = (bf16[1024,128]{1,0:T(8,128)(2,1)S(1)}, bf16[1024,128]{1,0:T(8,128)(2,1)S(1)}, u32[]{:S(2)}, u32[]{:S(2)}) collective-permute-start(bf16[1024,128]{1,0:T(8,128)(2,1)S(1)} %get-tuple-element.49), channel_id=1, source_target_pairs={{0,4},{12,8},{1,5},{13,9},{2,6},{14,10},{3,7},{15,11},{16,20},{28,... | collective-permute-start | bytes 786440 | tf_op jit(solution)/shard_map/ppermute | solution.py:417
  73.8 0.7 collective-permute-start.10
  74.6 0.7 collective-permute-start.12
  75.2 3.7 %collective-permute-done.18 = bf16[1024,128]{1,0:T(8,128)(2,1)S(1)} collective-permute-done((bf16[1024,128]{1,0:T(8,128)(2,1)S(1)}, bf16[1024,128]{1,0:T(8,128)(2,1)S(1)}, u32[]{:S(2)}, u32[]{:S(2)}) %collective-permute-start.18) | collective-permute-done | bytes 262176 | tf_op jit(solution)/shard_map/ppermute | solution.py:417
  79.0 0.7 collective-permute-start.19
  79.7 4.6 %collective-permute-done.20 = bf16[1024,128]{1,0:T(8,128)(2,1)S(1)} collective-permute-done((bf16[1024,128]{1,0:T(8,128)(2,1)S(1)}, bf16[1024,128]{1,0:T(8,128)(2,1)S(1)}, u32[]{:S(2)}, u32[]{:S(2)}) %collective-permute-start.20) | collective-permute-done | bytes 262176 | tf_op jit(solution)/shard_map/ppermute | solution.py:417
  84.4 0.7 collective-permute-start.21
  85.2 1.2 %root_prep.1 = (bf16[1024,1024]{1,0:T(8,128)(2,1)S(1)}, bf16[1024,1024]{1,0:T(8,128)(2,1)S(1)}) custom-call(s32[1]{0:T(128)} %bitcast.3.mine_ref, bf16[8192,128]{1,0:T(8,128)(2,1)S(1)} %pad_maximum_fusion.pieces_ref), custom_call_target="tpu_custom_call" | custom-call | flops 1048576 | bytes 6291456 | tf_op jit(solution)/shard_map/root_prep/pallas_call | solution.py:270
  86.5 1.0 root_solve.4.rest_0_
  87.5 1.3 %collective-permute-start.13 = (bf16[1024,128]{1,0:T(8,128)(2,1)S(1)}, bf16[1024,128]{1,0:T(8,128)(2,1)S(1)}, u32[]{:S(2)}, u32[]{:S(2)}) collective-permute-start(bf16[1024,128]{1,0:T(8,128)(2,1)S(1)} %root_solve.4.rest_0_), channel_id=1, source_target_pairs={{4,0},{8,12},{5,1},{9,13},{6,2},{10,14},{7,3},{11,15},{20,16},{24,... | collective-permute-start | bytes 786440 | tf_op jit(solution)/shard_map/ppermute | solution.py:425
  88.8 1.0 root_solve.6.rest_0_
  89.7 1.3 %collective-permute-start.22 = (bf16[1024,128]{1,0:T(8,128)(2,1)S(1)}, bf16[1024,128]{1,0:T(8,128)(2,1)S(1)}, u32[]{:S(2)}, u32[]{:S(2)}) collective-permute-start(bf16[1024,128]{1,0:T(8,128)(2,1)S(1)} %root_solve.6.rest_0_), channel_id=1, source_target_pairs={{4,0},{8,12},{5,1},{9,13},{6,2},{10,14},{7,3},{11,15},{20,16},{24,... | collective-permute-start | bytes 786440 | tf_op jit(solution)/shard_map/ppermute | solution.py:425
  91.0 0.9 root_solve.7.rest_1_
  92.0 1.6 %collective-permute-start.23 = (bf16[1024,128]{1,0:T(8,128)(2,1)S(1)}, bf16[1024,128]{1,0:T(8,128)(2,1)S(1)}, u32[]{:S(2)}, u32[]{:S(2)}) collective-permute-start(bf16[1024,128]{1,0:T(8,128)(2,1)S(1)} %root_solve.7.rest_1_), channel_id=1, source_target_pairs={{4,0},{8,12},{5,1},{9,13},{6,2},{10,14},{7,3},{11,15},{20,16},{24,... | collective-permute-start | bytes 786440 | tf_op jit(solution)/shard_map/ppermute | solution.py:425
  93.6 1.0 root_solve.5.rest_1_
  94.5 1.3 %collective-permute-start.14 = (bf16[1024,128]{1,0:T(8,128)(2,1)S(1)}, bf16[1024,128]{1,0:T(8,128)(2,1)S(1)}, u32[]{:S(2)}, u32[]{:S(2)}) collective-permute-start(bf16[1024,128]{1,0:T(8,128)(2,1)S(1)} %root_solve.5.rest_1_), channel_id=1, source_target_pairs={{4,0},{8,12},{5,1},{9,13},{6,2},{10,14},{7,3},{11,15},{20,16},{24,... | collective-permute-start | bytes 786440 | tf_op jit(solution)/shard_map/ppermute | solution.py:425
  95.8 9.8 %collective-permute-done.22.rest_2_ = bf16[1024,128]{1,0:T(8,128)(2,1)S(1)} collective-permute-done((bf16[1024,128]{1,0:T(8,128)(2,1)S(1)}, bf16[1024,128]{1,0:T(8,128)(2,1)S(1)}, u32[]{:S(2)}, u32[]{:S(2)}) %collective-permute-start.22) | collective-permute-done | bytes 262176 | tf_op jit(solution)/shard_map/ppermute | solution.py:425
  105.7 5.6 %collective-permute-done.23.rest_3_ = bf16[1024,128]{1,0:T(8,128)(2,1)S(1)} collective-permute-done((bf16[1024,128]{1,0:T(8,128)(2,1)S(1)}, bf16[1024,128]{1,0:T(8,128)(2,1)S(1)}, u32[]{:S(2)}, u32[]{:S(2)}) %collective-permute-start.23) | collective-permute-done | bytes 262176 | tf_op jit(solution)/shard_map/ppermute | solution.py:425
  111.3 2.9 %backward.2 = (bf16[2048,512]{1,0:T(8,128)(2,1)}, bf16[1024,512]{1,0:T(8,128)(2,1)}) custom-call(s32[1]{0:T(128)} %bitcast.take_ref, bf16[2048,256]{1,0:T(8,128)(2,1)S(1)} %get-tuple-element.45.fwd_ref, bf16[2048,1024]{1,0:T(8,128)(2,1)S(1)} %copy-done.8, bf16[4,512,512]{2,1,0:T(8,128)(2,1)S(1)} %copy-done.12, bf16[1024,128]{1,0:T(8,128)(2,1)S(1)} %root_solve.6.rest_0_, ...), custom_call_target="tpu_custom_call" | custom-call | flops 16106127360 | bytes 9961472 | tf_op jit(solution)/shard_map/backward/pallas_call | solution.py:346
  114.3 1.5 %collective-permute-done.14.rest_3_ = bf16[1024,128]{1,0:T(8,128)(2,1)S(1)} collective-permute-done((bf16[1024,128]{1,0:T(8,128)(2,1)S(1)}, bf16[1024,128]{1,0:T(8,128)(2,1)S(1)}, u32[]{:S(2)}, u32[]{:S(2)}) %collective-permute-start.14) | collective-permute-done | bytes 262176 | tf_op jit(solution)/shard_map/ppermute | solution.py:425
  115.8 2.9 %backward.3 = (bf16[2048,512]{1,0:T(8,128)(2,1)}, bf16[1024,512]{1,0:T(8,128)(2,1)}) custom-call(s32[1]{0:T(128)} %bitcast.take_ref, bf16[2048,256]{1,0:T(8,128)(2,1)S(1)} %get-tuple-element.33.fwd_ref, bf16[2048,1024]{1,0:T(8,128)(2,1)S(1)} %copy-done.8, bf16[4,512,512]{2,1,0:T(8,128)(2,1)S(1)} %copy-done.12, ...), custom_call_target="tpu_custom_call", output_to_operand_aliasing={{0}: (8, {}), {1}: (9, {})} | custom-call | flops 16106127360 | bytes 9961472 | tf_op jit(solution)/shard_map/backward/pallas_call | solution.py:346
  (50 shorter events, 0.9 us)
Async XLA Ops:
  0.6 1.0 copy-start
  1.7 18.1 %collective-permute-start.3 = (bf16[256,128]{1,0:T(8,128)(2,1)S(1)}, bf16[256,128]{1,0:T(8,128)(2,1)S(1)}, u32[]{:S(2)}, u32[]{:S(2)}) collective-permute-start(bf16[256,128]{1,0:T(8,128)(2,1)S(1)} %piece.1.rest_0_), channel_id=1, source_target_pairs={{0,4},{12,8},{1,5},{13,9},{2,6},{14,10},{3,7},{15,11},{16,20},{28,... | collective-permute-start | bytes 196616 | tf_op jit(solution)/shard_map/ppermute | solution.py:396
  6.7 15.5 %collective-permute-start.4 = (bf16[256,128]{1,0:T(8,128)(2,1)S(1)}, bf16[256,128]{1,0:T(8,128)(2,1)S(1)}, u32[]{:S(2)}, u32[]{:S(2)}) collective-permute-start(bf16[256,128]{1,0:T(8,128)(2,1)S(1)} %piece.1.rest_0_), channel_id=1, source_target_pairs={{0,8},{12,4},{1,9},{13,5},{2,10},{14,6},{3,11},{15,7},{16,24},{28,... | collective-permute-start | bytes 196616 | tf_op jit(solution)/shard_map/ppermute | solution.py:396
  9.0 13.5 %collective-permute-start.5 = (bf16[256,128]{1,0:T(8,128)(2,1)S(1)}, bf16[256,128]{1,0:T(8,128)(2,1)S(1)}, u32[]{:S(2)}, u32[]{:S(2)}) collective-permute-start(bf16[256,128]{1,0:T(8,128)(2,1)S(1)} %piece.1.rest_0_), channel_id=1, source_target_pairs={{4,8},{8,4},{5,9},{9,5},{6,10},{10,6},{7,11},{11,7},{20,24},{24,20... | collective-permute-start | bytes 196616 | tf_op jit(solution)/shard_map/ppermute | solution.py:396
  9.6 1.6 %copy-start.1 = (bf16[2048,512]{1,0:T(8,128)(2,1)S(1)}, bf16[2048,512]{1,0:T(8,128)(2,1)}, u32[]{:S(2)}) copy-start(bf16[2048,512]{1,0:T(8,128)(2,1)} %loads_ref.5) | copy-start | bytes 6291460
  11.2 0.7 copy-start.5
  11.9 12.5 %copy-start.2 = (bf16[4,512,512]{2,1,0:T(8,128)(2,1)S(1)}, bf16[4,512,512]{2,1,0:T(8,128)(2,1)}, u32[]{:S(2)}) copy-start(bf16[4,512,512]{2,1,0:T(8,128)(2,1)} %couple_ref.1) | copy-start | bytes 6291460
  11.9 12.5 %copy-start.3 = (bf16[4,512,512]{2,1,0:T(8,128)(2,1)S(1)}, bf16[4,512,512]{2,1,0:T(8,128)(2,1)}, u32[]{:S(2)}) copy-start(bf16[4,512,512]{2,1,0:T(8,128)(2,1)} %inv_ref.7) | copy-start | bytes 6291460
  11.9 12.5 %copy-start.6 = (s32[4,512]{1,0:T(4,128)S(1)}, s32[4,512]{1,0:T(4,128)}, u32[]{:S(2)}) copy-start(s32[4,512]{1,0:T(4,128)} %rows_ref.1) | copy-start | bytes 24580
  17.7 5.1 %copy-start.13 = (bf16[512,256]{1,0:T(8,128)(2,1)}, bf16[512,256]{1,0:T(8,128)(2,1)S(1)}, u32[]{:S(2)}) copy-start(bf16[512,256]{1,0:T(8,128)(2,1)S(1)} %get-tuple-element.29.rest_0_) | copy-start | bytes 786436
  17.7 20.0 %collective-permute-start = (bf16[512,256]{1,0:T(8,128)(2,1)}, bf16[512,256]{1,0:T(8,128)(2,1)}, u32[]{:S(2)}, u32[]{:S(2)}) collective-permute-start(bf16[512,256]{1,0:T(8,128)(2,1)} %get-tuple-element.30), channel_id=1, source_target_pairs={{0,4},{4,0},{8,12},{12,8},{1,5},{5,1},{9,13},{13,9},{2,6},{6,2},{1... | collective-permute-start | bytes 786440 | tf_op jit(solution)/shard_map/ppermute | solution.py:406
  19.0 21.7 %collective-permute-start.1 = (bf16[512,256]{1,0:T(8,128)(2,1)}, bf16[512,256]{1,0:T(8,128)(2,1)}, u32[]{:S(2)}, u32[]{:S(2)}) collective-permute-start(bf16[512,256]{1,0:T(8,128)(2,1)} %get-tuple-element.31), channel_id=1, source_target_pairs={{0,8},{4,12},{8,0},{12,4},{1,9},{5,13},{9,1},{13,5},{2,10},{6,14},... | collective-permute-start | bytes 786440 | tf_op jit(solution)/shard_map/ppermute | solution.py:406
  19.8 22.4 %collective-permute-start.2 = (bf16[512,256]{1,0:T(8,128)(2,1)}, bf16[512,256]{1,0:T(8,128)(2,1)}, u32[]{:S(2)}, u32[]{:S(2)}) collective-permute-start(bf16[512,256]{1,0:T(8,128)(2,1)} %get-tuple-element.32), channel_id=1, source_target_pairs={{0,12},{4,8},{8,4},{12,0},{1,13},{5,9},{9,5},{13,1},{2,14},{6,10},... | collective-permute-start | bytes 786440 | tf_op jit(solution)/shard_map/ppermute | solution.py:406
  22.2 45.7 %collective-permute-start.15 = (bf16[512,256]{1,0:T(8,128)(2,1)}, bf16[512,256]{1,0:T(8,128)(2,1)}, u32[]{:S(2)}, u32[]{:S(2)}) collective-permute-start(bf16[512,256]{1,0:T(8,128)(2,1)} %get-tuple-element.42), channel_id=1, source_target_pairs={{0,4},{4,0},{8,12},{12,8},{1,5},{5,1},{9,13},{13,9},{2,6},{6,2},{1... | collective-permute-start | bytes 786440 | tf_op jit(solution)/shard_map/ppermute | solution.py:406
  22.9 13.1 %collective-permute-start.6 = (bf16[1024,128]{1,0:T(8,128)(2,1)S(1)}, bf16[1024,128]{1,0:T(8,128)(2,1)S(1)}, u32[]{:S(2)}, u32[]{:S(2)}) collective-permute-start(bf16[1024,128]{1,0:T(8,128)(2,1)S(1)} %gather_rows.1), channel_id=1, source_target_pairs={{0,16},{16,0},{1,17},{17,1},{2,18},{18,2},{3,19},{19,3},{4,20},{20... | collective-permute-start | bytes 786440 | tf_op jit(solution)/shard_map/ppermute | solution.py:400
  30.6 2.0 %copy-start.7 = (bf16[2048,1024]{1,0:T(8,128)(2,1)}, bf16[2048,1024]{1,0:T(8,128)(2,1)S(1)}, u32[]{:S(2)}) copy-start(bf16[2048,1024]{1,0:T(8,128)(2,1)S(1)} %get-tuple-element.34.spread_t_ref) | copy-start | bytes 12582916
  32.6 2.0 %copy-start.9 = (bf16[1024,2048]{1,0:T(8,128)(2,1)}, bf16[1024,2048]{1,0:T(8,128)(2,1)S(1)}, u32[]{:S(2)}) copy-start(bf16[1024,2048]{1,0:T(8,128)(2,1)S(1)} %get-tuple-element.28.spread_ref) | copy-start | bytes 12582916
  34.6 1.3 %copy-start.11 = (bf16[4,512,512]{2,1,0:T(8,128)(2,1)}, bf16[4,512,512]{2,1,0:T(8,128)(2,1)S(1)}, u32[]{:S(2)}) copy-start(bf16[4,512,512]{2,1,0:T(8,128)(2,1)S(1)} %get-tuple-element.35.inv_t_ref) | copy-start | bytes 6291460
  35.9 32.0 %collective-permute-start.16 = (bf16[512,256]{1,0:T(8,128)(2,1)S(1)}, bf16[512,256]{1,0:T(8,128)(2,1)S(1)}, u32[]{:S(2)}, u32[]{:S(2)}) collective-permute-start(bf16[512,256]{1,0:T(8,128)(2,1)S(1)} %get-tuple-element.43), channel_id=1, source_target_pairs={{0,8},{4,12},{8,0},{12,4},{1,9},{5,13},{9,1},{13,5},{2,10},{6,14},... | collective-permute-start | bytes 786440 | tf_op jit(solution)/shard_map/ppermute | solution.py:406
  37.7 30.3 %collective-permute-start.17 = (bf16[512,256]{1,0:T(8,128)(2,1)S(1)}, bf16[512,256]{1,0:T(8,128)(2,1)S(1)}, u32[]{:S(2)}, u32[]{:S(2)}) collective-permute-start(bf16[512,256]{1,0:T(8,128)(2,1)S(1)} %get-tuple-element.44), channel_id=1, source_target_pairs={{0,12},{4,8},{8,4},{12,0},{1,13},{5,9},{9,5},{13,1},{2,14},{6,10},... | collective-permute-start | bytes 786440 | tf_op jit(solution)/shard_map/ppermute | solution.py:406
  40.7 25.6 %collective-permute-start.7 = (bf16[2048,128]{1,0:T(8,128)(2,1)S(1)}, bf16[2048,128]{1,0:T(8,128)(2,1)S(1)}, u32[]{:S(2)}, u32[]{:S(2)}) collective-permute-start(bf16[2048,128]{1,0:T(8,128)(2,1)S(1)} %pad_maximum_fusion.2), channel_id=1, source_target_pairs={{0,2},{1,3},{2,0},{3,1},{4,6},{5,7},{6,4},{7,5},{8,10},{9,11},{10,... | collective-permute-start | bytes 1572872 | tf_op jit(solution)/shard_map/ppermute | solution.py:400
  42.2 2.2 %copy-start.10 = (bf16[1024,2048]{1,0:T(8,128)(2,1)S(1)}, bf16[1024,2048]{1,0:T(8,128)(2,1)}, u32[]{:S(2)}) copy-start(bf16[1024,2048]{1,0:T(8,128)(2,1)} %copy-done.9) | copy-start | bytes 12582916
  44.4 0.9 copy-start.14
  48.5 25.3 %collective-permute-start.9 = (bf16[1024,128]{1,0:T(8,128)(2,1)S(1)}, bf16[1024,128]{1,0:T(8,128)(2,1)S(1)}, u32[]{:S(2)}, u32[]{:S(2)}) collective-permute-start(bf16[1024,128]{1,0:T(8,128)(2,1)S(1)} %get-tuple-element.39), channel_id=1, source_target_pairs={{0,4},{12,8},{1,5},{13,9},{2,6},{14,10},{3,7},{15,11},{16,20},{28,... | collective-permute-start | bytes 786440 | tf_op jit(solution)/shard_map/ppermute | solution.py:417
  66.3 8.2 %collective-permute-start.11 = (bf16[1024,128]{1,0:T(8,128)(2,1)S(1)}, bf16[1024,128]{1,0:T(8,128)(2,1)S(1)}, u32[]{:S(2)}, u32[]{:S(2)}) collective-permute-start(bf16[1024,128]{1,0:T(8,128)(2,1)S(1)} %get-tuple-element.41), channel_id=1, source_target_pairs={{0,4},{12,8},{1,5},{13,9},{2,6},{14,10},{3,7},{15,11},{16,20},{28,... | collective-permute-start | bytes 786440 | tf_op jit(solution)/shard_map/ppermute | solution.py:417
  67.9 17.2 %collective-permute-start.8 = (bf16[4096,128]{1,0:T(8,128)(2,1)S(1)}, bf16[4096,128]{1,0:T(8,128)(2,1)S(1)}, u32[]{:S(2)}, u32[]{:S(2)}) collective-permute-start(bf16[4096,128]{1,0:T(8,128)(2,1)S(1)} %pad_maximum_fusion.1), channel_id=1, source_target_pairs={{0,1},{1,0},{2,3},{3,2},{4,5},{5,4},{6,7},{7,6},{8,9},{9,8},{10,11... | collective-permute-start | bytes 3145736 | tf_op jit(solution)/shard_map/ppermute | solution.py:400
  70.9 8.0 %collective-permute-start.18 = (bf16[1024,128]{1,0:T(8,128)(2,1)S(1)}, bf16[1024,128]{1,0:T(8,128)(2,1)S(1)}, u32[]{:S(2)}, u32[]{:S(2)}) collective-permute-start(bf16[1024,128]{1,0:T(8,128)(2,1)S(1)} %get-tuple-element.47), channel_id=1, source_target_pairs={{0,4},{12,8},{1,5},{13,9},{2,6},{14,10},{3,7},{15,11},{16,20},{28,... | collective-permute-start | bytes 786440 | tf_op jit(solution)/shard_map/ppermute | solution.py:417
  72.4 11.9 %collective-permute-start.20 = (bf16[1024,128]{1,0:T(8,128)(2,1)S(1)}, bf16[1024,128]{1,0:T(8,128)(2,1)S(1)}, u32[]{:S(2)}, u32[]{:S(2)}) collective-permute-start(bf16[1024,128]{1,0:T(8,128)(2,1)S(1)} %get-tuple-element.49), channel_id=1, source_target_pairs={{0,4},{12,8},{1,5},{13,9},{2,6},{14,10},{3,7},{15,11},{16,20},{28,... | collective-permute-start | bytes 786440 | tf_op jit(solution)/shard_map/ppermute | solution.py:417
  73.8 12.7 %collective-permute-start.10 = (bf16[1024,128]{1,0:T(8,128)(2,1)S(1)}, bf16[1024,128]{1,0:T(8,128)(2,1)S(1)}, u32[]{:S(2)}, u32[]{:S(2)}) collective-permute-start(bf16[1024,128]{1,0:T(8,128)(2,1)S(1)} %add_convert_fusion.3.one_ref), channel_id=1, source_target_pairs={{4,8},{8,4},{5,9},{9,5},{6,10},{10,6},{7,11},{11,7},{20,24},{24,20... | collective-permute-start | bytes 786440 | tf_op jit(solution)/shard_map/ppermute | solution.py:419
  74.6 19.0 %collective-permute-start.12 = (bf16[1024,128]{1,0:T(8,128)(2,1)S(1)}, bf16[1024,128]{1,0:T(8,128)(2,1)S(1)}, u32[]{:S(2)}, u32[]{:S(2)}) collective-permute-start(bf16[1024,128]{1,0:T(8,128)(2,1)S(1)} %add_convert_fusion.2.one_ref), channel_id=1, source_target_pairs={{4,8},{8,4},{5,9},{9,5},{6,10},{10,6},{7,11},{11,7},{20,24},{24,20... | collective-permute-start | bytes 786440 | tf_op jit(solution)/shard_map/ppermute | solution.py:419
  79.0 9.7 %collective-permute-start.19 = (bf16[1024,128]{1,0:T(8,128)(2,1)S(1)}, bf16[1024,128]{1,0:T(8,128)(2,1)S(1)}, u32[]{:S(2)}, u32[]{:S(2)}) collective-permute-start(bf16[1024,128]{1,0:T(8,128)(2,1)S(1)} %add_convert_fusion.1.one_ref), channel_id=1, source_target_pairs={{4,8},{8,4},{5,9},{9,5},{6,10},{10,6},{7,11},{11,7},{20,24},{24,20... | collective-permute-start | bytes 786440 | tf_op jit(solution)/shard_map/ppermute | solution.py:419
  84.4 6.6 %collective-permute-start.21 = (bf16[1024,128]{1,0:T(8,128)(2,1)S(1)}, bf16[1024,128]{1,0:T(8,128)(2,1)S(1)}, u32[]{:S(2)}, u32[]{:S(2)}) collective-permute-start(bf16[1024,128]{1,0:T(8,128)(2,1)S(1)} %add_convert_fusion.one_ref), channel_id=1, source_target_pairs={{4,8},{8,4},{5,9},{9,5},{6,10},{10,6},{7,11},{11,7},{20,24},{24,20... | collective-permute-start | bytes 786440 | tf_op jit(solution)/shard_map/ppermute | solution.py:419
  85.2 1.3 %copy-start.4 = (bf16[1024,512]{1,0:T(8,128)(2,1)S(1)}, bf16[1024,512]{1,0:T(8,128)(2,1)}, u32[]{:S(2)}) copy-start(bf16[1024,512]{1,0:T(8,128)(2,1)} %loads_ref.9) | copy-start | bytes 3145732
  87.5 26.8 %collective-permute-start.13 = (bf16[1024,128]{1,0:T(8,128)(2,1)S(1)}, bf16[1024,128]{1,0:T(8,128)(2,1)S(1)}, u32[]{:S(2)}, u32[]{:S(2)}) collective-permute-start(bf16[1024,128]{1,0:T(8,128)(2,1)S(1)} %root_solve.4.rest_0_), channel_id=1, source_target_pairs={{4,0},{8,12},{5,1},{9,13},{6,2},{10,14},{7,3},{11,15},{20,16},{24,... | collective-permute-start | bytes 786440 | tf_op jit(solution)/shard_map/ppermute | solution.py:425
  89.7 16.0 %collective-permute-start.22 = (bf16[1024,128]{1,0:T(8,128)(2,1)S(1)}, bf16[1024,128]{1,0:T(8,128)(2,1)S(1)}, u32[]{:S(2)}, u32[]{:S(2)}) collective-permute-start(bf16[1024,128]{1,0:T(8,128)(2,1)S(1)} %root_solve.6.rest_0_), channel_id=1, source_target_pairs={{4,0},{8,12},{5,1},{9,13},{6,2},{10,14},{7,3},{11,15},{20,16},{24,... | collective-permute-start | bytes 786440 | tf_op jit(solution)/shard_map/ppermute | solution.py:425
  92.0 19.3 %copy-start.8 = (bf16[2048,1024]{1,0:T(8,128)(2,1)S(1)}, bf16[2048,1024]{1,0:T(8,128)(2,1)}, u32[]{:S(2)}) copy-start(bf16[2048,1024]{1,0:T(8,128)(2,1)} %copy-done.7) | copy-start | bytes 12582916
  92.0 19.3 %copy-start.12 = (bf16[4,512,512]{2,1,0:T(8,128)(2,1)S(1)}, bf16[4,512,512]{2,1,0:T(8,128)(2,1)}, u32[]{:S(2)}) copy-start(bf16[4,512,512]{2,1,0:T(8,128)(2,1)} %copy-done.11) | copy-start | bytes 6291460
  92.0 19.3 %collective-permute-start.23 = (bf16[1024,128]{1,0:T(8,128)(2,1)S(1)}, bf16[1024,128]{1,0:T(8,128)(2,1)S(1)}, u32[]{:S(2)}, u32[]{:S(2)}) collective-permute-start(bf16[1024,128]{1,0:T(8,128)(2,1)S(1)} %root_solve.7.rest_1_), channel_id=1, source_target_pairs={{4,0},{8,12},{5,1},{9,13},{6,2},{10,14},{7,3},{11,15},{20,16},{24,... | collective-permute-start | bytes 786440 | tf_op jit(solution)/shard_map/ppermute | solution.py:425
  94.5 21.2 %collective-permute-start.14 = (bf16[1024,128]{1,0:T(8,128)(2,1)S(1)}, bf16[1024,128]{1,0:T(8,128)(2,1)S(1)}, u32[]{:S(2)}, u32[]{:S(2)}) collective-permute-start(bf16[1024,128]{1,0:T(8,128)(2,1)S(1)} %root_solve.5.rest_1_), channel_id=1, source_target_pairs={{4,0},{8,12},{5,1},{9,13},{6,2},{10,14},{7,3},{11,15},{20,16},{24,... | collective-permute-start | bytes 786440 | tf_op jit(solution)/shard_map/ppermute | solution.py:425
